TPU v7x, 128 devices: a whole 4x4x4 slice. The times are simulated.
128 devices in a mesh: dp: 8 (over z_hi, x), tensor: 16 (over z_lo, y, core).
Axes of the slice: x: 4, y: 4, z: 4 (z_hi: 2, z_lo: 2; z = z_hi * 2 + z_lo), core: 2. Of those that a mesh axis runs over, the one named last changes fastest.
Arguments:
- tokens: bfloat16 [16384, 2048], P(('dp', 'tensor')), may hold values from -6 to 6
- gain: float32 [2048], replicated, may hold values from 0.25 to 1.75
- gate_saved: bfloat16 [16384, 8192], P('dp', 'tensor'), may hold values from -12 to 12
- up_saved: bfloat16 [16384, 8192], P('dp', 'tensor'), may hold values from -6 to 6
- out_grad: bfloat16 [16384, 2048], P(('dp', 'tensor')), may hold values from -6 to 6
- gate_weight: bfloat16 [2048, 8192], P(None, 'tensor'), may hold values from -0.125 to 0.125
- up_weight: bfloat16 [2048, 8192], P(None, 'tensor'), may hold values from -0.125 to 0.125
- down_weight: bfloat16 [8192, 2048], P('tensor'), may hold values from -0.0625 to 0.0625
Outputs:
- token_grad: bfloat16 [16384, 2048], P(('dp', 'tensor'))
- gain_grad: float32 [2048], replicated
- gate_grad: bfloat16 [2048, 8192], P('dp', 'tensor')
- up_grad: bfloat16 [2048, 8192], P('dp', 'tensor')
- down_grad: bfloat16 [8192, 2048], P('tensor', 'dp')
All inputs are finite; a program needn't handle non-finite values.
Results may differ from a plain program's by a relative error of at most 0.022.
Values may be sent and summed in bfloat16 or wider, within the bound.
No kernel may reach another device: no remote copies, remote signals or barrier semaphores. Data moves between devices by JAX's collectives and lax.ppermute only.
A program may use at most 128 MiB of HBM per device.

v0:
```python
import jax
import jax.numpy as jnp
from jax import lax
from jax.sharding import PartitionSpec as P


def normalize(rows_in, gain):
    x = rows_in.astype(jnp.float32)
    inverse = lax.rsqrt(jnp.mean(x * x, axis=-1, keepdims=True) + 1e-05)
    return (x, inverse, (x * inverse * gain).astype(jnp.bfloat16))


def deltas(grad_rows, down_weight, gate_rows, up_rows):
    hidden_grad = lax.dot_general(
        grad_rows, down_weight, (((1,), (1,)), ((), ())), preferred_element_type=jnp.float32
    )
    gate_f = gate_rows.astype(jnp.float32)
    sigma = jax.nn.sigmoid(gate_f)
    gate_delta = (
        hidden_grad * up_rows.astype(jnp.float32) * sigma * (1.0 + gate_f * (1.0 - sigma))
    ).astype(jnp.bfloat16)
    up_delta = (hidden_grad * gate_f * sigma).astype(jnp.bfloat16)
    return (gate_delta, up_delta)


def left_product(left, right):
    return lax.dot_general(
        left, right, (((0,), (0,)), ((), ())), preferred_element_type=jnp.float32
    )


def local(tokens, gain, gate_saved, up_saved, out_grad, gate_weight, up_weight, down_weight):
    x, inverse, normed = normalize(tokens, gain)
    gate_f = gate_saved.astype(jnp.float32)
    activated = (gate_f * jax.nn.sigmoid(gate_f) * up_saved.astype(jnp.float32)).astype(
        jnp.bfloat16
    )
    grad_all = lax.all_gather(out_grad, "tensor", axis=0, tiled=True)
    gate_delta, up_delta = deltas(grad_all, down_weight, gate_saved, up_saved)
    down_part = left_product(activated, grad_all)
    piece_normed = lax.all_gather(normed, "tensor", axis=0, tiled=True)
    gate_rows = gate_delta
    up_rows = up_delta
    gate_part = left_product(piece_normed, gate_rows)
    up_part = left_product(piece_normed, up_rows)
    down_sum, gate_sum, up_sum = (
        lax.psum_scatter(
            down_part.astype(jnp.bfloat16), "dp", scatter_dimension=1, tiled=True
        ).astype(jnp.float32),
        lax.psum_scatter(
            gate_part.astype(jnp.bfloat16), "dp", scatter_dimension=0, tiled=True
        ).astype(jnp.float32),
        lax.psum_scatter(
            up_part.astype(jnp.bfloat16), "dp", scatter_dimension=0, tiled=True
        ).astype(jnp.float32),
    )
    gate_rows = gate_delta
    up_rows = up_delta
    total = lax.dot_general(
        gate_rows, gate_weight, (((1,), (1,)), ((), ())), preferred_element_type=jnp.float32
    )
    normed_grad = lax.psum_scatter(
        (
            total
            + lax.dot_general(
                up_rows, up_weight, (((1,), (1,)), ((), ())), preferred_element_type=jnp.float32
            )
        ).astype(jnp.bfloat16),
        "tensor",
        scatter_dimension=0,
        tiled=True,
    ).astype(jnp.float32)
    unit = x * inverse
    gain_grad = lax.psum(jnp.sum(normed_grad * unit, axis=0), ("dp", "tensor"))
    scaled = gain * normed_grad
    mean_term = jnp.mean(scaled * unit, axis=-1, keepdims=True)
    token_grad = (out_grad.astype(jnp.float32) + inverse * (scaled - unit * mean_term)).astype(
        jnp.bfloat16
    )
    return (
        token_grad,
        gain_grad,
        gate_sum.astype(jnp.bfloat16),
        up_sum.astype(jnp.bfloat16),
        down_sum.astype(jnp.bfloat16),
    )


def solution(mesh):
    placed = (
        P(("dp", "tensor"), None),
        P(),
        P("dp", "tensor"),
        P("dp", "tensor"),
        P(("dp", "tensor"), None),
        P(None, "tensor"),
        P(None, "tensor"),
        P("tensor", None),
    )
    return jax.shard_map(
        local,
        mesh=mesh,
        in_specs=placed,
        out_specs=(
            P(("dp", "tensor"), None),
            P(),
            P("dp", "tensor"),
            P("dp", "tensor"),
            P("tensor", "dp"),
        ),
        check_vma=False,
    )
```

profile of v0, /device:TPU:0, one launch (start us, length us, event | category | flops | bytes accessed | tf_op | source)
XLA Modules:
  0.0 475.4 jit_solution(14338089924162343253)
XLA Ops:
  7.2 0.0 all-gather.3.cloned.1.call-start
  7.2 0.7 all-gather.3.cloned.1.call-update
  7.9 0.0 reduce-scatter.5.cloned.1.call-start
  8.0 56.4 %all-gather.3.cloned.1.call-done = bf16[2048,2048]{1,0:T(8,128)(2,1)} async-done(((bf16[128,2048]{1,0:T(8,128)(2,1)}), bf16[2048,2048]{1,0:T(8,128)(2,1)}) %all-gather.3.cloned.1.call-update) | async-done | bytes 8388624 | tf_op jit(solution)/shard_map/all_gather | solution.py:38
  64.4 13.2 %fusion.2 = (bf16[2048,512]{1,0:T(8,128)(2,1)S(1)}, f32[2048,512]{1,0:T(8,128)}) fusion(bf16[2048,512]{1,0:T(8,128)(2,1)} %param.11, bf16[2048,512]{1,0:T(8,128)(2,1)} %param.10, bf16[2048,2048]{1,0:T(8,128)(2,1)} %all-gather.3.cloned.1.call-done, bf16[512,2048]{1,0:T(8,128)(2,1)} %param.15), kind=kOutput, calls=%fused_computation.9 | convolution fusion | flops 4307550208 | bytes 20971520 | tf_op jit(solution)/shard_map/dot_general | solution.py:14
  77.6 8.2 %fusion.26 = f32[2048,2048]{1,0:T(8,128)} fusion(bf16[2048,512]{1,0:T(8,128)(2,1)S(1)} %get-tuple-element.8, bf16[2048,512]{1,0:T(8,128)(2,1)S(1)} %copy-done), kind=kOutput, calls=%fused_computation.39 | convolution fusion | flops 4294967296 | bytes 20971520 | tf_op jit(solution)/shard_map/dot_general | solution.py:59
  85.8 16.3 %add_convert_fusion = bf16[2048,2048]{1,0:T(8,128)(2,1)} fusion(f32[2048,2048]{1,0:T(8,128)} %fusion.26, bf16[2048,512]{1,0:T(8,128)(2,1)} %param.14, f32[2048,512]{1,0:T(8,128)} %get-tuple-element.9, bf16[2048,512]{1,0:T(8,128)(2,1)} %param.10), kind=kOutput, calls=%fused_computation | convolution fusion | flops 4310695936 | bytes 33554432 | tf_op jit(solution)/shard_map/dot_general | solution.py:65
  102.1 0.0 reduce-scatter.5.cloned.1.call-update
  102.1 0.0 all-gather.5.cloned.1.call-start
  102.2 1.0 copy-done.2
  103.1 0.2 fusion.21
  103.3 74.6 %reduce-scatter.5.cloned.1.call-done = bf16[128,2048]{1,0:T(8,128)(2,1)} async-done(((bf16[2048,2048]{1,0:T(8,128)(2,1)}), bf16[128,2048]{1,0:T(8,128)(2,1)}) %reduce-scatter.5.cloned.1.call-update) | async-done | bytes 524304 | tf_op jit(solution)/shard_map/reduce_scatter | solution.py:62
  178.0 2.2 fusion.22
  180.2 0.0 reduce-scatter.11.cloned.1.call-start
  180.3 10.5 %convolution_convert_fusion = bf16[512,2048]{1,0:T(8,128)(2,1)} fusion(bf16[2048,2048]{1,0:T(8,128)(2,1)} %all-gather.3.cloned.1.call-done, bf16[2048,512]{1,0:T(8,128)(2,1)S(1)} %copy-done.5, bf16[2048,512]{1,0:T(8,128)(2,1)} %param.10), kind=kOutput, calls=%fused_computation.17 | convolution fusion | flops 4304404480 | bytes 14680064 | tf_op jit(solution)/shard_map/dot_general | solution.py:27
  190.8 0.3 reduce-scatter.7.cloned.1.call-start
  191.0 40.0 %all-gather.5.cloned.1.call-done = bf16[2048,2048]{1,0:T(8,128)(2,1)} async-done(((bf16[128,2048]{1,0:T(8,128)(2,1)}), bf16[2048,2048]{1,0:T(8,128)(2,1)}) %all-gather.5.cloned.1.call-update) | async-done | bytes 8388624 | tf_op jit(solution)/shard_map/all_gather | solution.py:41
  231.0 9.9 %convolution_convert_fusion.2 = bf16[2048,512]{1,0:T(8,128)(2,1)} fusion(bf16[2048,2048]{1,0:T(8,128)(2,1)} %all-gather.5.cloned.1.call-done, bf16[2048,512]{1,0:T(8,128)(2,1)} %copy-done.6), kind=kOutput, calls=%fused_computation.19 | convolution fusion | flops 4296015872 | bytes 12582912 | tf_op jit(solution)/shard_map/dot_general | solution.py:27
  240.9 0.0 reduce-scatter.9.cloned.1.call-start
  241.0 11.6 %convolution_convert_fusion.1 = bf16[2048,512]{1,0:T(8,128)(2,1)} fusion(bf16[2048,2048]{1,0:T(8,128)(2,1)} %all-gather.5.cloned.1.call-done, f32[2048,512]{1,0:T(8,128)} %get-tuple-element.9, bf16[2048,512]{1,0:T(8,128)(2,1)} %param.10), kind=kOutput, calls=%fused_computation.18 | convolution fusion | flops 4303355904 | bytes 16777216 | tf_op jit(solution)/shard_map/dot_general | solution.py:27
  252.6 67.7 %psum.7 = f32[2048]{0:T(1024)} all-reduce(f32[2048]{0:T(1024)S(1)} %get-tuple-element.5), channel_id=1, replica_groups=mesh['dp'=8,'tensor'=16] {'dp','tensor'}, use_global_device_ids=true, to_apply=%region_4.0 | all-reduce | flops 2048 | bytes 16384 | tf_op jit(solution)/shard_map/psum | solution.py:74
  320.3 2.3 fusion.18
  322.6 67.8 %reduce-scatter.7.cloned.1.call-done = bf16[256,512]{1,0:T(8,128)(2,1)} async-done(((bf16[2048,512]{1,0:T(8,128)(2,1)}), bf16[256,512]{1,0:T(8,128)(2,1)}) %reduce-scatter.7.cloned.1.call-update) | async-done | bytes 262160 | tf_op jit(solution)/shard_map/reduce_scatter | solution.py:50
  390.4 78.1 %reduce-scatter.9.cloned.1.call-done = bf16[256,512]{1,0:T(8,128)(2,1)} async-done(((bf16[2048,512]{1,0:T(8,128)(2,1)}), bf16[256,512]{1,0:T(8,128)(2,1)}) %reduce-scatter.9.cloned.1.call-update) | async-done | bytes 262160 | tf_op jit(solution)/shard_map/reduce_scatter | solution.py:53
  (20 shorter events, 0.1 us)
Async XLA Ops:
  7.2 70.4 %copy-start = (bf16[2048,512]{1,0:T(8,128)(2,1)S(1)}, bf16[2048,512]{1,0:T(8,128)(2,1)}, u32[]{:S(2)}) copy-start(bf16[2048,512]{1,0:T(8,128)(2,1)} %param.13) | copy-start | bytes 6291460
  7.2 57.2 %all-gather.3.cloned.1.call-start = ((), (), s32[]{:S(2)}) async-start(), calls=%async_computation.4 | async-start | bytes 8912896 | tf_op jit(solution)/shard_map/all_gather | solution.py:38
  7.9 170.1 %reduce-scatter.5.cloned.1.call-start = ((), (), s32[]{:S(2)}) async-start(), calls=%async_computation.5 | async-start | bytes 8912896 | tf_op jit(solution)/shard_map/reduce_scatter | solution.py:62
  77.6 8.2 %copy-start.6 = (bf16[2048,512]{1,0:T(8,128)(2,1)}, bf16[2048,512]{1,0:T(8,128)(2,1)S(1)}, u32[]{:S(2)}) copy-start(bf16[2048,512]{1,0:T(8,128)(2,1)S(1)} %get-tuple-element.8) | copy-start | bytes 6291460
  102.1 1.0 copy-start.2
  102.1 75.9 %copy-start.4 = (f32[2048]{0:T(1024)S(1)}, f32[2048]{0:T(1024)}, u32[]{:S(2)}) copy-start(f32[2048]{0:T(1024)} %param.9) | copy-start | bytes 24580
  102.1 78.2 %copy-start.5 = (bf16[2048,512]{1,0:T(8,128)(2,1)S(1)}, bf16[2048,512]{1,0:T(8,128)(2,1)}, u32[]{:S(2)}) copy-start(bf16[2048,512]{1,0:T(8,128)(2,1)} %param.11) | copy-start | bytes 6291460
  102.1 128.9 %all-gather.5.cloned.1.call-start = ((), (), s32[]{:S(2)}) async-start(), calls=%async_computation.6 | async-start | bytes 8912896 | tf_op jit(solution)/shard_map/all_gather | solution.py:41
  180.2 142.4 %reduce-scatter.11.cloned.1.call-start = ((), (), s32[]{:S(2)}) async-start(), calls=%async_computation.9 | async-start | bytes 2359296 | tf_op jit(solution)/shard_map/reduce_scatter | solution.py:47
  190.8 199.6 %reduce-scatter.7.cloned.1.call-start = ((), (), s32[]{:S(2)}) async-start(), calls=%async_computation.7 | async-start | bytes 2359296 | tf_op jit(solution)/shard_map/reduce_scatter | solution.py:50
  240.9 79.4 %copy-start.3 = (bf16[128,2048]{1,0:T(8,128)(2,1)S(1)}, bf16[128,2048]{1,0:T(8,128)(2,1)}, u32[]{:S(2)}) copy-start(bf16[128,2048]{1,0:T(8,128)(2,1)} %param.12) | copy-start | bytes 1572868
  240.9 227.6 %reduce-scatter.9.cloned.1.call-start = ((), (), s32[]{:S(2)}) async-start(), calls=%async_computation.8 | async-start | bytes 2359296 | tf_op jit(solution)/shard_map/reduce_scatter | solution.py:53
  241.0 227.5 %copy-start.1 = (bf16[2048,512]{1,0:T(8,128)(2,1)S(1)}, bf16[2048,512]{1,0:T(8,128)(2,1)}, u32[]{:S(2)}) copy-start(bf16[2048,512]{1,0:T(8,128)(2,1)} %param.13) | copy-start | bytes 6291460
Sparse Core Ops, SparseCore 0:
  9.7 54.6 all-gather.2
  102.2 75.6 reduce-scatter.4
  180.3 50.6 all-gather.4
  235.2 76.4 reduce-scatter.10
  316.4 73.9 reduce-scatter.6
  394.6 73.8 reduce-scatter.8
where the time goes:
time: 476 us; the launch traced here: 475 us
  waiting for transfers between devices  318 us (67%)
  matrix products  69.6 us (15%)
  blocking collectives  67.7 us (14%)
  between operations  14.2 us (3%)
    reduce_scatter x1, waiting for transfers between devices, local(): lax.psum_scatter(up_part.astype(jnp.bfloat16), 'dp', scatter_dimension=0,...  78.1 us
    reduce_scatter x1, waiting for transfers between devices, local(): lax.psum_scatter((total + lax.dot_general(up_rows, up_weight, (((1,), (1,...  74.6 us
    reduce_scatter x1, waiting for transfers between devices, local(): lax.psum_scatter(gate_part.astype(jnp.bfloat16), 'dp', scatter_dimension=...  67.8 us
    psum x1, blocking collectives, local(): gain_grad = lax.psum(jnp.sum(normed_grad * unit, axis=0), ('dp', 'tensor'))  67.7 us
    all_gather x1, waiting for transfers between devices, local(): grad_all = lax.all_gather(out_grad, 'tensor', axis=0, tiled=True)  56.4 us
    all_gather x1, waiting for transfers between devices, local(): piece_normed = lax.all_gather(normed, 'tensor', axis=0, tiled=True)  40 us
    dot_general x3, matrix products, left_product(): lax.dot_general(left, right, (((0,), (0,)), ((), ())), preferred_element_...  31.9 us
    dot_general x1, matrix products, local(): lax.dot_general(up_rows, up_weight, (((1,), (1,)), ((), ())), preferred_e...  16.3 us
  transfers between devices with their start and end apart: 6, of which 5 were waited for; matrix products, arithmetic and copies ran while one was open for 7% of the time, Pallas kernels for 0%

commit v1 on v0

v1 whole, which is shorter than its diff:
```python
import functools

import jax
import jax.numpy as jnp
import numpy as np
from jax import lax
from jax.experimental import pallas as pl
from jax.experimental.pallas import tpu as pltpu
from jax.sharding import Mesh, PartitionSpec as P

AXES = ("zh", "x", "zl", "y", "c")
SIZES = (2, 4, 2, 4, 2)
D = 2048
ROWS = 128
F = 512
BF = jnp.bfloat16
F32 = jnp.float32
MIB = 1024 * 1024


def send(value, **shift):
    ids = np.arange(128).reshape(SIZES)
    pairs = []
    for at in np.ndindex(*SIZES):
        to = tuple((a + shift.get(n, 0)) % s for a, n, s in zip(at, AXES, SIZES))
        pairs.append((int(ids[at]), int(ids[to])))
    return lax.ppermute(value, AXES, pairs)


def nt(a, b):
    return lax.dot_general(a, b, (((1,), (1,)), ((), ())), preferred_element_type=F32)


def nn(a, b):
    return lax.dot_general(a, b, (((1,), (0,)), ((), ())), preferred_element_type=F32)


def rows_of(ref, s_ref):
    return jnp.concatenate([ref[s_ref[p]] for p in range(8)], axis=0).astype(F32)


def down_kernel(s_ref, go, uo, gx, ux, *rest):
    dy, (out_own, out_oth, act_t) = rest[:8], rest[8:]

    @pl.when(pl.program_id(0) == 0)
    def _():
        for k, (g_ref, u_ref) in enumerate(((go.at[:, 0], uo.at[:, 0]), (gx.at[0], ux.at[0]))):
            for p in range(8):
                g = g_ref[s_ref[p]].astype(F32)
                u = u_ref[s_ref[p]].astype(F32)
                act = g * u / (1.0 + jnp.exp(-g))
                act_t[k * F : (k + 1) * F, p * ROWS : (p + 1) * ROWS] = act.T.astype(BF)

    cols = jnp.concatenate([d[...] for d in dy], axis=0)
    out_own[0] = nn(act_t[:F], cols).astype(BF)
    out_oth[0] = nn(act_t[F:], cols).astype(BF)


def down_call(scalars, gate4, up4, swapped, dy):
    grid_spec = pltpu.PrefetchScalarGridSpec(
        num_scalar_prefetch=1,
        grid=(8,),
        in_specs=[pl.BlockSpec((8, 1, ROWS, F), lambda i, s: (0, s[8], 0, 0))] * 2
        + [
            pl.BlockSpec((1, 8, ROWS, F), lambda i, s: (0, 0, 0, 0)),
            pl.BlockSpec((1, 8, ROWS, F), lambda i, s: (1, 0, 0, 0)),
        ]
        + [pl.BlockSpec((ROWS, 256), lambda i, s: (0, s[9 + i]))] * 8,
        out_specs=[pl.BlockSpec((1, F, 256), lambda i, s: (i, 0, 0))] * 2,
        scratch_shapes=[pltpu.VMEM((2 * F, 8 * ROWS), BF)],
    )
    return pl.pallas_call(
        down_kernel,
        grid_spec=grid_spec,
        out_shape=[jax.ShapeDtypeStruct((8, F, 256), BF)] * 2,
        compiler_params=pltpu.CompilerParams(vmem_limit_bytes=40 * MIB),
        cost_estimate=pl.CostEstimate(
            flops=2 * 1024 * 1024 * D, bytes_accessed=12 * MIB, transcendentals=1024 * 1024
        ),
        name="down",
    )(scalars, gate4, up4, swapped, swapped, *dy)


def delta_kernel(s_ref, go, uo, gx, ux, wdo, wgo, wuo, wdx, wgx, wux, *rest):
    dy = rest[:8]
    gd, ud, n_own, n_z, n_yp, n_ym, n_2, n_z2, rows, acc, sem = rest[8:]
    h = pl.program_id(0)

    @pl.when(h == 0)
    def _():
        copies = [
            pltpu.make_async_copy(d, rows.at[pl.ds(p * ROWS, ROWS)], sem.at[p])
            for p, d in enumerate(dy)
        ]
        for copy in copies:
            copy.start()
        for copy in copies:
            copy.wait()

    def part(g_ref, u_ref, wd, wg, wu):
        hidden = nt(rows[...], wd[...])
        g = rows_of(g_ref, s_ref)
        u = rows_of(u_ref, s_ref)
        sigma = 1.0 / (1.0 + jnp.exp(-g))
        hs = hidden * sigma
        gate_delta = (hs * u * (1.0 + g * (1.0 - sigma))).astype(BF)
        up_delta = (hs * g).astype(BF)
        gd[...] = gate_delta
        ud[...] = up_delta
        for n in range(4):
            at = slice(n * 512, (n + 1) * 512)
            term = nt(gate_delta, wg[at, :]) + nt(up_delta, wu[at, :])

            @pl.when(h == 0)
            def _():
                acc[:, at] = term

            @pl.when(h > 0)
            def _():
                acc[:, at] += term

    @pl.when(h < 2)
    def _():
        part(go.at[:, 0], uo.at[:, 0], wdo, wgo, wuo)

    @pl.when(h >= 2)
    def _():
        part(gx.at[0], ux.at[0], wdx, wgx, wux)

    @pl.when(h == 3)
    def _():
        for p, out in enumerate(
            (n_own, n_z, n_ym.at[0], n_yp.at[0], n_2, n_ym.at[1], n_yp.at[1], n_z2)
        ):
            out[...] = acc[p * ROWS : (p + 1) * ROWS].astype(BF)


def delta_call(scalars, gate4, up4, swapped, own, other, dy):
    def low(i):
        return jnp.minimum(i, 1)

    def high(i):
        return jnp.maximum(i - 2, 0)

    piece = jax.ShapeDtypeStruct((ROWS, D), BF)
    pair = jax.ShapeDtypeStruct((2, ROWS, D), BF)
    wide = jax.ShapeDtypeStruct((8 * ROWS, 2 * F), BF)
    whole = pl.BlockSpec((ROWS, D), lambda i, s: (0, 0))
    whole2 = pl.BlockSpec((2, ROWS, D), lambda i, s: (0, 0, 0))
    grid_spec = pltpu.PrefetchScalarGridSpec(
        num_scalar_prefetch=1,
        grid=(4,),
        in_specs=[pl.BlockSpec((8, 1, ROWS, 256), lambda i, s: (0, s[8], 0, low(i)))] * 2
        + [
            pl.BlockSpec((1, 8, ROWS, 256), lambda i, s: (0, 0, 0, high(i))),
            pl.BlockSpec((1, 8, ROWS, 256), lambda i, s: (1, 0, 0, high(i))),
            pl.BlockSpec((256, D), lambda i, s: (low(i), 0)),
            pl.BlockSpec((D, 256), lambda i, s: (0, low(i))),
            pl.BlockSpec((D, 256), lambda i, s: (0, low(i))),
            pl.BlockSpec((256, D), lambda i, s: (high(i), 0)),
            pl.BlockSpec((D, 256), lambda i, s: (0, high(i))),
            pl.BlockSpec((D, 256), lambda i, s: (0, high(i))),
        ]
        + [pl.BlockSpec(memory_space=pl.ANY)] * 8,
        out_specs=[pl.BlockSpec((8 * ROWS, 256), lambda i, s: (0, i))] * 2
        + [whole, whole, whole2, whole2, whole, whole],
        scratch_shapes=[
            pltpu.VMEM((8 * ROWS, D), BF),
            pltpu.VMEM((8 * ROWS, D), F32),
            pltpu.SemaphoreType.DMA((8,)),
        ],
    )
    return pl.pallas_call(
        delta_kernel,
        grid_spec=grid_spec,
        out_shape=[wide, wide, piece, piece, pair, pair, piece, piece],
        compiler_params=pltpu.CompilerParams(vmem_limit_bytes=56 * MIB),
        cost_estimate=pl.CostEstimate(
            flops=6 * 1024 * 1024 * D, bytes_accessed=32 * MIB, transcendentals=1024 * 1024
        ),
        name="deltas",
    )(scalars, gate4, up4, swapped, swapped, *own, *other, *dy)


def weight_kernel(s_ref, gd, ud, gain, wgo, wuo, wgx, wux, *rest):
    unit, (out_own, out_oth, out_gain) = rest[:8], rest[8:]
    lhs = jnp.concatenate([u[...] for u in unit], axis=1)
    scale = gain[...]
    total = jnp.zeros((256, 128), F32)
    for delta, at, w_own, w_oth in ((gd, 0, wgo, wgx), (ud, F, wuo, wux)):
        for half, w, out in ((0, w_own, out_own), (F, w_oth, out_oth)):
            grad = nn(lhs, delta[:, half : half + F])
            out[0, :, at : at + F] = (grad * scale).astype(BF)
            prod = grad * w[...].astype(F32)
            for k in range(4):
                total = total + prod[:, k * 128 : (k + 1) * 128]
    out_gain[0] = total


def weight_call(scalars, gd, ud, gain, own, other, unit):
    full = pl.BlockSpec((8 * ROWS, 2 * F), lambda i, s: (0, 0))
    rows = pl.BlockSpec((256, F), lambda i, s: (s[9 + i], 0))
    grid_spec = pltpu.PrefetchScalarGridSpec(
        num_scalar_prefetch=1,
        grid=(8,),
        in_specs=[full, full, pl.BlockSpec((256, 1), lambda i, s: (s[9 + i], 0))]
        + [rows] * 4
        + [pl.BlockSpec((256, ROWS), lambda i, s: (s[9 + i], 0))] * 8,
        out_specs=[
            pl.BlockSpec((1, 256, 2 * F), lambda i, s: (i, 0, 0)),
            pl.BlockSpec((1, 256, 2 * F), lambda i, s: (i, 0, 0)),
            pl.BlockSpec((1, 256, 128), lambda i, s: (s[9 + i], 0, 0)),
        ],
    )
    return pl.pallas_call(
        weight_kernel,
        grid_spec=grid_spec,
        out_shape=[jax.ShapeDtypeStruct((8, 256, 2 * F), BF)] * 2
        + [jax.ShapeDtypeStruct((8, 256, 128), F32)],
        compiler_params=pltpu.CompilerParams(vmem_limit_bytes=40 * MIB),
        cost_estimate=pl.CostEstimate(
            flops=4 * 1024 * 1024 * D, bytes_accessed=24 * MIB, transcendentals=0
        ),
        name="weights",
    )(scalars, gd, ud, gain, *own, *other, *unit)


def gather(own):
    from_z = send(own, zl=1)
    from_2 = send(own, y=2)
    from_m = send(own, y=1)
    from_p = send(own, y=-1)
    from_zm = send(from_z, y=1)
    from_zp = send(from_z, y=-1)
    from_z2 = send(from_2, zl=1)
    return (own, from_z, from_m, from_p, from_2, from_zm, from_zp, from_z2)


def total_of(*terms):
    out = terms[0].astype(F32)
    for term in terms[1:]:
        out = out + term.astype(F32)
    return out


def over_dp(own, other):
    back = send(other, c=1)
    parts = [
        total_of(own[2 * r : 2 * r + 2], back[2 * r : 2 * r + 2]) for r in range(4)
    ]
    got = [send(parts[r].astype(BF), x=r) for r in (1, 2, 3)]
    both = total_of(parts[0], *got)
    return both[0] + send(both[1].astype(BF), zh=1).astype(F32)


def local(tokens, gain, gate_saved, up_saved, out_grad, gate_weight, up_weight, down_weight):
    zh, x_at, zl, y, c = (lax.axis_index(a) for a in AXES)
    oz = 1 - zl
    places = [zl * 4 + y, oz * 4 + y]
    places += [zl * 4 + (y + k) % 4 for k in (3, 1, 2)]
    places += [oz * 4 + (y + k) % 4 for k in (3, 1, 2)]
    order = [((zh + q) % 2) * 4 + (x_at + r) % 4 for r in range(4) for q in range(2)]
    scalars = jnp.stack(places + [c] + order).astype(jnp.int32)

    dy = gather(out_grad)

    gate4 = gate_saved.reshape(8, 2, ROWS, F)
    up4 = up_saved.reshape(8, 2, ROWS, F)
    theirs = jnp.stack(
        [lax.dynamic_index_in_dim(a, 1 - c, 1, keepdims=False) for a in (gate4, up4)]
    )
    swapped = send(theirs, c=1)
    down_other = send(down_weight, c=1)
    gate_other = send(gate_weight, c=1)
    up_other = send(up_weight, c=1)

    x = tokens.astype(F32)
    inverse = lax.rsqrt(jnp.mean(x * x, axis=-1, keepdims=True) + 1e-05)
    unit = x * inverse
    units = gather(unit.astype(BF).T)

    down_own, down_oth = down_call(scalars, gate4, up4, swapped, dy)
    down_sum = over_dp(down_own, down_oth)

    gd, ud, n_own, n_z, n_yp, n_ym, n_2, n_z2 = delta_call(
        scalars,
        gate4,
        up4,
        swapped,
        (down_weight, gate_weight, up_weight),
        (down_other, gate_other, up_other),
        dy,
    )
    a = send(n_yp, y=1)
    b = send(n_ym, y=-1)
    d = send(n_z2, zl=1)

    w_own, w_oth, gain_part = weight_call(
        scalars,
        gd,
        ud,
        gain.reshape(D, 1),
        (gate_weight, up_weight),
        (gate_other, up_other),
        units,
    )
    gain_grad = lax.psum(jnp.sum(gain_part, axis=-1).reshape(D), AXES)
    both_sum = over_dp(w_own, w_oth)

    e = send(total_of(n_2, d).astype(BF), y=2)
    f = send(total_of(n_z, a[1], b[1]).astype(BF), zl=1)
    normed_grad = total_of(n_own, a[0], b[0], e, f)
    scaled = gain * normed_grad
    mean_term = jnp.mean(scaled * unit, axis=-1, keepdims=True)
    token_grad = (out_grad.astype(F32) + inverse * (scaled - unit * mean_term)).astype(BF)
    return (
        token_grad,
        gain_grad,
        both_sum[:, :F].astype(BF),
        both_sum[:, F:].astype(BF),
        down_sum.astype(BF),
    )


def solution(mesh):
    mesh = Mesh(mesh.devices.reshape(SIZES), AXES)
    dp, tensor = ("zh", "x"), ("zl", "y", "c")
    placed = (
        P(dp + tensor, None),
        P(),
        P(dp, tensor),
        P(dp, tensor),
        P(dp + tensor, None),
        P(None, tensor),
        P(None, tensor),
        P(tensor, None),
    )
    return jax.shard_map(
        local,
        mesh=mesh,
        in_specs=placed,
        out_specs=(
            P(dp + tensor, None),
            P(),
            P(dp, tensor),
            P(dp, tensor),
            P(tensor, dp),
        ),
        check_vma=False,
    )
```

time: 476 us -> 389 us (0.82)
  waiting for transfers between devices: 318 us -> 164 us
  matrix products: 69.6 us -> 0 us
  Pallas kernels: 0 us -> 63.6 us
  starting transfers between devices: 0.46 us -> 42.4 us
  local copies, waits for them, and re-layouts: 1 us -> 25 us
  between operations: 14.2 us -> 1.04 us
  other arithmetic: 4.68 us -> 17.5 us
  blocking collectives: 67.7 us -> 74 us
    reduce_scatter x4 -> x0, waiting for transfers between devices: 221 us -> none  [the longest x1 78.1 us: local(): lax.psum_scatter(up_part.astype(jnp.bfloat16), 'dp', scatter_dimension=0,...]
    ppermute x0 -> x33, waiting for transfers between devices: none -> 164 us  [send(): return lax.ppermute(value, AXES, pairs)]
    all_gather x2 -> x0, waiting for transfers between devices: 96.4 us -> none  [the longest x1 56.4 us: local(): grad_all = lax.all_gather(out_grad, 'tensor', axis=0, tiled=True)]
    dot_general x6 -> x0, matrix products: 69.6 us -> none  [the longest x3 31.9 us: left_product(): lax.dot_general(left, right, (((0,), (0,)), ((), ())), preferred_element_...]
    pallas_call x0 -> x3, Pallas kernels: none -> 63.6 us  [the longest x1 37.9 us: delta_call(): pl.pallas_call(delta_kernel, grid_spec=grid_spec, out_shape=[wide, wide,...]
    ppermute x0 -> x33, starting transfers between devices: none -> 42.4 us  [send(): return lax.ppermute(value, AXES, pairs)]
    unnamed x14 -> x64, local copies, waits for them, and re-layouts: 1 us -> 12.2 us
    pallas_call x0 -> x6, local copies, waits for them, and re-layouts: none -> 8.32 us  [delta_call(): pl.pallas_call(delta_kernel, grid_spec=grid_spec, out_shape=[wide, wide,...]
  transfers between devices with their start and end apart: 6 -> 33, of which waited for: 5 -> 21; matrix products, arithmetic and copies ran while one was open for 7% -> 6% of each run, Pallas kernels for 0% -> 3%
where the time goes in v1:
time: 389 us; the launch traced here: 387 us
  waiting for transfers between devices  164 us (42%)
  blocking collectives  74 us (19%)
  Pallas kernels  63.6 us (16%)
  starting transfers between devices  42.4 us (11%)
  local copies, waits for them, and re-layouts  25 us (6%)
  other arithmetic  17.5 us (4%)
    ppermute x33, waiting for transfers between devices, send(): return lax.ppermute(value, AXES, pairs)  164 us
    psum x1, blocking collectives, local(): gain_grad = lax.psum(jnp.sum(gain_part, axis=-1).reshape(D), AXES)  74 us
    ppermute x33, starting transfers between devices, send(): return lax.ppermute(value, AXES, pairs)  42.4 us
    pallas_call x1, Pallas kernels, delta_call(): pl.pallas_call(delta_kernel, grid_spec=grid_spec, out_shape=[wide, wide,...  37.9 us
    pallas_call x1, Pallas kernels, weight_call(): pl.pallas_call(weight_kernel, grid_spec=grid_spec, out_shape=[jax.ShapeDt...  14.6 us
    unnamed x64, local copies, waits for them, and re-layouts  12.2 us
    pallas_call x1, Pallas kernels, down_call(): pl.pallas_call(down_kernel, grid_spec=grid_spec, out_shape=[jax.ShapeDtyp...  11 us
    pallas_call x6, local copies, waits for them, and re-layouts, delta_call(): pl.pallas_call(delta_kernel, grid_spec=grid_spec, out_shape=[wide, wide,...  8.32 us
  transfers between devices with their start and end apart: 33, of which 21 were waited for; matrix products, arithmetic and copies ran while one was open for 6% of the time, Pallas kernels for 3%

profile of v1, /device:TPU:0, one launch (start us, length us, event | category | flops | bytes accessed | tf_op | source)
XLA Modules:
  0.0 387.0 jit_solution(10131601124751112025)
XLA Ops:
  2.7 3.2 collective-permute-start.7
  14.9 4.5 %collective-permute-done.7.rest_4_ = bf16[128,2048]{1,0:T(8,128)(2,1)S(1)} collective-permute-done((bf16[128,2048]{1,0:T(8,128)(2,1)}, bf16[128,2048]{1,0:T(8,128)(2,1)S(1)}, u32[]{:S(2)}, u32[]{:S(2)}) %collective-permute-start.7) | collective-permute-done | bytes 524320 | tf_op jit(solution)/shard_map/ppermute | solution.py:27
  19.3 9.8 %collective-permute-done.5.rest_2_ = bf16[128,2048]{1,0:T(8,128)(2,1)} collective-permute-done((bf16[128,2048]{1,0:T(8,128)(2,1)}, bf16[128,2048]{1,0:T(8,128)(2,1)}, u32[]{:S(2)}, u32[]{:S(2)}) %collective-permute-start.5) | collective-permute-done | bytes 524320 | tf_op jit(solution)/shard_map/ppermute | solution.py:27
  30.9 13.8 %collective-permute-done.8.rest_5_ = bf16[128,2048]{1,0:T(8,128)(2,1)S(1)} collective-permute-done((bf16[128,2048]{1,0:T(8,128)(2,1)S(1)}, bf16[128,2048]{1,0:T(8,128)(2,1)S(1)}, u32[]{:S(2)}, u32[]{:S(2)}) %collective-permute-start.8) | collective-permute-done | bytes 524320 | tf_op jit(solution)/shard_map/ppermute | solution.py:27
  46.0 11.9 %collective-permute-done.9.rest_6_ = bf16[128,2048]{1,0:T(8,128)(2,1)S(1)} collective-permute-done((bf16[128,2048]{1,0:T(8,128)(2,1)S(1)}, bf16[128,2048]{1,0:T(8,128)(2,1)S(1)}, u32[]{:S(2)}, u32[]{:S(2)}) %collective-permute-start.9) | collective-permute-done | bytes 524320 | tf_op jit(solution)/shard_map/ppermute | solution.py:27
  59.7 11.3 %collective-permute-done.10.rest_7_ = bf16[128,2048]{1,0:T(8,128)(2,1)} collective-permute-done((bf16[128,2048]{1,0:T(8,128)(2,1)S(1)}, bf16[128,2048]{1,0:T(8,128)(2,1)}, u32[]{:S(2)}, u32[]{:S(2)}) %collective-permute-start.10) | collective-permute-done | bytes 524320 | tf_op jit(solution)/shard_map/ppermute | solution.py:27
  71.1 37.9 %deltas.1 = (bf16[1024,1024]{1,0:T(8,128)(2,1)}, bf16[1024,1024]{1,0:T(8,128)(2,1)}, bf16[128,2048]{1,0:T(8,128)(2,1)}, bf16[128,2048]{1,0:T(8,128)(2,1)}, bf16[...) custom-call(s32[17]{0:T(128)} %stack.80.s_ref, ...), custom_call_target="tpu_custom_call" | custom-call | flops 12884901888 | bytes 33554432 | tf_op jit(solution)/shard_map/deltas/pallas_call | solution.py:173
  119.5 8.4 %collective-permute-done.13 = bf16[128,2048]{0,1:T(8,128)(2,1)} collective-permute-done((bf16[128,2048]{0,1:T(8,128)(2,1)}, bf16[128,2048]{0,1:T(8,128)(2,1)}, u32[]{:S(2)}, u32[]{:S(2)}) %collective-permute-start.13) | collective-permute-done | bytes 524320 | tf_op jit(solution)/shard_map/ppermute | solution.py:27
  131.2 7.5 %collective-permute-done.11 = bf16[2,128,2048]{1,2,0:T(8,128)(2,1)S(1)} collective-permute-done((bf16[2,128,2048]{1,2,0:T(8,128)(2,1)}, bf16[2,128,2048]{1,2,0:T(8,128)(2,1)S(1)}, u32[]{:S(2)}, u32[]{:S(2)}) %collective-permute-start.11) | collective-permute-done | bytes 1048608 | tf_op jit(solution)/shard_map/ppermute | solution.py:27
  147.1 5.5 %collective-permute-done.15 = bf16[128,2048]{0,1:T(8,128)(2,1)} collective-permute-done((bf16[128,2048]{0,1:T(8,128)(2,1)}, bf16[128,2048]{0,1:T(8,128)(2,1)}, u32[]{:S(2)}, u32[]{:S(2)}) %collective-permute-start.15) | collective-permute-done | bytes 524320 | tf_op jit(solution)/shard_map/ppermute | solution.py:27
  154.4 2.6 fusion.16
  157.5 3.4 collective-permute-start.19
  160.9 3.2 collective-permute-start.18
  164.1 5.5 %collective-permute-done.16.rest_1_ = bf16[2048,128]{1,0:T(8,128)(2,1)S(1)} collective-permute-done((bf16[2048,128]{1,0:T(8,128)(2,1)S(1)}, bf16[2048,128]{1,0:T(8,128)(2,1)S(1)}, u32[]{:S(2)}, u32[]{:S(2)}) %collective-permute-start.16) | collective-permute-done | bytes 524320 | tf_op jit(solution)/shard_map/ppermute | solution.py:27
  175.8 5.3 %collective-permute-done.17.rest_2_ = bf16[2048,128]{1,0:T(8,128)(2,1)} collective-permute-done((bf16[2048,128]{1,0:T(8,128)(2,1)S(1)}, bf16[2048,128]{1,0:T(8,128)(2,1)}, u32[]{:S(2)}, u32[]{:S(2)}) %collective-permute-start.17) | collective-permute-done | bytes 524320 | tf_op jit(solution)/shard_map/ppermute | solution.py:27
  181.9 5.1 %collective-permute-done.20.rest_5_ = bf16[2048,128]{1,0:T(8,128)(2,1)} collective-permute-done((bf16[2048,128]{1,0:T(8,128)(2,1)S(1)}, bf16[2048,128]{1,0:T(8,128)(2,1)}, u32[]{:S(2)}, u32[]{:S(2)}) %collective-permute-start.20) | collective-permute-done | bytes 524320 | tf_op jit(solution)/shard_map/ppermute | solution.py:27
  194.4 14.6 %weights.1 = (bf16[8,256,1024]{2,1,0:T(8,128)(2,1)}, bf16[8,256,1024]{2,1,0:T(8,128)(2,1)}, f32[8,256,128]{2,1,0:T(8,128)S(1)}) custom-call(s32[17]{0:T(128)S(1)} %copy-done.3, bf16[1024,1024]{1,0:T(8,128)(2,1)S(1)} %copy-done.18, bf16[1024,1024]{1,0:T(8,128)(2,1)S(1)} %copy-done.19, f32[2048,1]{1,0:T(8,128)S(1)} %copy.30.gain, ...), custom_call_target="tpu_custom_call" | custom-call | flops 8589934592 | bytes 25165824 | tf_op jit(solution)/shard_map/weights/pallas_call | solution.py:215
  209.2 11.0 %down.1 = (bf16[8,512,256]{2,1,0:T(8,128)(2,1)S(1)}, bf16[8,512,256]{2,1,0:T(8,128)(2,1)S(1)}) custom-call(s32[17]{0:T(128)S(1)} %copy-done.3, bf16[8,2,128,512]{3,2,1,0:T(8,128)(2,1)S(1)} %bitcast.74, bf16[8,2,128,512]{3,2,1,0:T(8,128)(2,1)S(1)} %bitcast.77, bf16[2,8,128,512]{3,2,1,0:T(8,128)(2,1)} %collective-permute-done.gx.ux, ...), custom_call_target="tpu_custom_call" | custom-call | flops 4294967296 | bytes 12582912 | tf_op jit(solution)/shard_map/down/pallas_call | solution.py:72
  220.8 3.8 collective-permute-done.28
  234.7 6.6 %collective-permute-done.29 = bf16[2,512,256]{2,1,0:T(8,128)(2,1)S(1)} collective-permute-done((bf16[2,512,256]{2,1,0:T(8,128)(2,1)S(1)}, bf16[2,512,256]{2,1,0:T(8,128)(2,1)S(1)}, u32[]{:S(2)}, u32[]{:S(2)}) %collective-permute-start.29) | collective-permute-done | bytes 524320 | tf_op jit(solution)/shard_map/ppermute | solution.py:27
  242.8 55.1 %collective-permute-done.30 = bf16[2,512,256]{2,1,0:T(8,128)(2,1)S(1)} collective-permute-done((bf16[2,512,256]{2,1,0:T(8,128)(2,1)S(1)}, bf16[2,512,256]{2,1,0:T(8,128)(2,1)S(1)}, u32[]{:S(2)}, u32[]{:S(2)}) %collective-permute-start.30) | collective-permute-done | bytes 524320 | tf_op jit(solution)/shard_map/ppermute | solution.py:27
  297.9 2.8 collective-permute-done.31
  303.0 3.6 collective-permute-start.27
  309.2 74.0 %psum.7 = f32[2048]{0:T(1024)} all-reduce(f32[2048]{0:T(1024)S(1)} %bitcast.80), channel_id=1, replica_groups=mesh['zh'=2,'x'=4,'zl'=2,'y'=4,'c'=2] {'zh','x','zl','y','c'}, use_global_device_ids=true, to_apply=%region_3.4 | all-reduce | flops 2048 | bytes 16384 | tf_op jit(solution)/shard_map/psum | solution.py:307
  (137 shorter events, 75.5 us)
Async XLA Ops:
  2.7 16.6 %collective-permute-start.7 = (bf16[128,2048]{1,0:T(8,128)(2,1)}, bf16[128,2048]{1,0:T(8,128)(2,1)S(1)}, u32[]{:S(2)}, u32[]{:S(2)}) collective-permute-start(bf16[128,2048]{1,0:T(8,128)(2,1)} %rest_0_.3), channel_id=1, source_target_pairs={{0,4},{1,5},{2,6},{3,7},{4,0},{5,1},{6,2},{7,3},{8,12},{9,13},{10,... | collective-permute-start | bytes 1572872 | tf_op jit(solution)/shard_map/ppermute | solution.py:27
  5.9 23.3 %collective-permute-start.5 = (bf16[128,2048]{1,0:T(8,128)(2,1)}, bf16[128,2048]{1,0:T(8,128)(2,1)}, u32[]{:S(2)}, u32[]{:S(2)}) collective-permute-start(bf16[128,2048]{1,0:T(8,128)(2,1)} %rest_0_.3), channel_id=1, source_target_pairs={{0,2},{1,3},{2,4},{3,5},{4,6},{5,7},{6,0},{7,1},{8,10},{9,11},{10,... | collective-permute-start | bytes 1572872 | tf_op jit(solution)/shard_map/ppermute | solution.py:27
  6.6 23.0 %collective-permute-start.6 = (bf16[128,2048]{1,0:T(8,128)(2,1)}, bf16[128,2048]{1,0:T(8,128)(2,1)}, u32[]{:S(2)}, u32[]{:S(2)}) collective-permute-start(bf16[128,2048]{1,0:T(8,128)(2,1)} %rest_0_.3), channel_id=1, source_target_pairs={{0,6},{1,7},{2,0},{3,1},{4,2},{5,3},{6,4},{7,5},{8,14},{9,15},{10,... | collective-permute-start | bytes 1572872 | tf_op jit(solution)/shard_map/ppermute | solution.py:27
  12.5 58.6 %collective-permute-start = (bf16[2,8,128,512]{3,2,1,0:T(8,128)(2,1)}, bf16[2,8,128,512]{3,2,1,0:T(8,128)(2,1)}, u32[]{:S(2)}, u32[]{:S(2)}) collective-permute-start(bf16[2,8,128,512]{3,2,1,0:T(8,128)(2,1)} %pad_maximum_fusion), channel_id=1, source_target_pairs={{0,1},{1,0},{2,3},{3,2},{4,5},{5,4},{6,7},{7,6},{8,9},{9,8},{10,11... | collective-permute-start | bytes 6291464 | tf_op jit(solution)/shard_map/ppermute | solution.py:27
  14.9 56.2 %collective-permute-start.2 = (bf16[2048,512]{1,0:T(8,128)(2,1)S(1)}, bf16[2048,512]{1,0:T(8,128)(2,1)}, u32[]{:S(2)}, u32[]{:S(2)}) collective-permute-start(bf16[2048,512]{1,0:T(8,128)(2,1)S(1)} %copy-done.4), channel_id=1, source_target_pairs={{0,1},{1,0},{2,3},{3,2},{4,5},{5,4},{6,7},{7,6},{8,9},{9,8},{10,11... | collective-permute-start | bytes 6291464 | tf_op jit(solution)/shard_map/ppermute | solution.py:27
  19.3 51.7 %collective-permute-start.3 = (bf16[2048,512]{1,0:T(8,128)(2,1)}, bf16[2048,512]{1,0:T(8,128)(2,1)}, u32[]{:S(2)}, u32[]{:S(2)}) collective-permute-start(bf16[2048,512]{1,0:T(8,128)(2,1)} %wuo.3), channel_id=1, source_target_pairs={{0,1},{1,0},{2,3},{3,2},{4,5},{5,4},{6,7},{7,6},{8,9},{9,8},{10,11... | collective-permute-start | bytes 6291464 | tf_op jit(solution)/shard_map/ppermute | solution.py:27
  29.2 41.9 %collective-permute-start.1 = (bf16[512,2048]{1,0:T(8,128)(2,1)}, bf16[512,2048]{1,0:T(8,128)(2,1)}, u32[]{:S(2)}, u32[]{:S(2)}) collective-permute-start(bf16[512,2048]{1,0:T(8,128)(2,1)} %wdo.1), channel_id=1, source_target_pairs={{0,1},{1,0},{2,3},{3,2},{4,5},{5,4},{6,7},{7,6},{8,9},{9,8},{10,11... | collective-permute-start | bytes 6291464 | tf_op jit(solution)/shard_map/ppermute | solution.py:27
  111.4 27.4 %collective-permute-start.11 = (bf16[2,128,2048]{1,2,0:T(8,128)(2,1)}, bf16[2,128,2048]{1,2,0:T(8,128)(2,1)S(1)}, u32[]{:S(2)}, u32[]{:S(2)}) collective-permute-start(bf16[2,128,2048]{1,2,0:T(8,128)(2,1)} %copy.25), channel_id=1, source_target_pairs={{0,2},{1,3},{2,4},{3,5},{4,6},{5,7},{6,0},{7,1},{8,10},{9,11},{10,... | collective-permute-start | bytes 3145736 | tf_op jit(solution)/shard_map/ppermute | solution.py:27
  114.0 26.3 %collective-permute-start.12 = (bf16[2,128,2048]{1,2,0:T(8,128)(2,1)}, bf16[2,128,2048]{1,2,0:T(8,128)(2,1)S(1)}, u32[]{:S(2)}, u32[]{:S(2)}) collective-permute-start(bf16[2,128,2048]{1,2,0:T(8,128)(2,1)} %copy.26), channel_id=1, source_target_pairs={{0,6},{1,7},{2,0},{3,1},{4,2},{5,3},{6,4},{7,5},{8,14},{9,15},{10,... | collective-permute-start | bytes 3145736 | tf_op jit(solution)/shard_map/ppermute | solution.py:27
  129.9 17.2 %collective-permute-start.14 = (bf16[128,2048]{0,1:T(8,128)(2,1)}, bf16[128,2048]{0,1:T(8,128)(2,1)S(1)}, u32[]{:S(2)}, u32[]{:S(2)}) collective-permute-start(bf16[128,2048]{0,1:T(8,128)(2,1)} %add_convert_fusion.6), channel_id=1, source_target_pairs={{0,4},{1,5},{2,6},{3,7},{4,0},{5,1},{6,2},{7,3},{8,12},{9,13},{10,... | collective-permute-start | bytes 1572872 | tf_op jit(solution)/shard_map/ppermute | solution.py:27
  157.5 16.4 %collective-permute-start.19 = (bf16[2048,128]{1,0:T(8,128)(2,1)S(1)}, bf16[2048,128]{1,0:T(8,128)(2,1)S(1)}, u32[]{:S(2)}, u32[]{:S(2)}) collective-permute-start(bf16[2048,128]{1,0:T(8,128)(2,1)S(1)} %get-tuple-element.47.rest_0_), channel_id=1, source_target_pairs={{0,4},{1,5},{2,6},{3,7},{4,0},{5,1},{6,2},{7,3},{8,12},{9,13},{10,... | collective-permute-start | bytes 1572872 | tf_op jit(solution)/shard_map/ppermute | solution.py:27
  160.9 20.3 %collective-permute-start.17 = (bf16[2048,128]{1,0:T(8,128)(2,1)S(1)}, bf16[2048,128]{1,0:T(8,128)(2,1)}, u32[]{:S(2)}, u32[]{:S(2)}) collective-permute-start(bf16[2048,128]{1,0:T(8,128)(2,1)S(1)} %get-tuple-element.47.rest_0_), channel_id=1, source_target_pairs={{0,2},{1,3},{2,4},{3,5},{4,6},{5,7},{6,0},{7,1},{8,10},{9,11},{10,... | collective-permute-start | bytes 1572872 | tf_op jit(solution)/shard_map/ppermute | solution.py:27
  160.9 21.1 %collective-permute-start.18 = (bf16[2048,128]{1,0:T(8,128)(2,1)S(1)}, bf16[2048,128]{1,0:T(8,128)(2,1)}, u32[]{:S(2)}, u32[]{:S(2)}) collective-permute-start(bf16[2048,128]{1,0:T(8,128)(2,1)S(1)} %get-tuple-element.47.rest_0_), channel_id=1, source_target_pairs={{0,6},{1,7},{2,0},{3,1},{4,2},{5,3},{6,4},{7,5},{8,14},{9,15},{10,... | collective-permute-start | bytes 1572872 | tf_op jit(solution)/shard_map/ppermute | solution.py:27
  169.6 17.4 %collective-permute-start.20 = (bf16[2048,128]{1,0:T(8,128)(2,1)S(1)}, bf16[2048,128]{1,0:T(8,128)(2,1)}, u32[]{:S(2)}, u32[]{:S(2)}) collective-permute-start(bf16[2048,128]{1,0:T(8,128)(2,1)S(1)} %collective-permute-done.16.rest_1_), channel_id=1, source_target_pairs={{0,2},{1,3},{2,4},{3,5},{4,6},{5,7},{6,0},{7,1},{8,10},{9,11},{10,... | collective-permute-start | bytes 1572872 | tf_op jit(solution)/shard_map/ppermute | solution.py:27
  171.3 16.2 %collective-permute-start.21 = (bf16[2048,128]{1,0:T(8,128)(2,1)S(1)}, bf16[2048,128]{1,0:T(8,128)(2,1)}, u32[]{:S(2)}, u32[]{:S(2)}) collective-permute-start(bf16[2048,128]{1,0:T(8,128)(2,1)S(1)} %collective-permute-done.16.rest_1_), channel_id=1, source_target_pairs={{0,6},{1,7},{2,0},{3,1},{4,2},{5,3},{6,4},{7,5},{8,14},{9,15},{10,... | collective-permute-start | bytes 1572872 | tf_op jit(solution)/shard_map/ppermute | solution.py:27
  209.1 17.8 %collective-permute-start.23 = (bf16[8,256,1024]{2,1,0:T(8,128)(2,1)}, bf16[8,256,1024]{2,1,0:T(8,128)(2,1)S(1)}, u32[]{:S(2)}, u32[]{:S(2)}) collective-permute-start(bf16[8,256,1024]{2,1,0:T(8,128)(2,1)} %get-tuple-element.28), channel_id=1, source_target_pairs={{0,1},{1,0},{2,3},{3,2},{4,5},{5,4},{6,7},{7,6},{8,9},{9,8},{10,11... | collective-permute-start | bytes 12582920 | tf_op jit(solution)/shard_map/ppermute | solution.py:27
  225.0 16.3 %collective-permute-start.29 = (bf16[2,512,256]{2,1,0:T(8,128)(2,1)S(1)}, bf16[2,512,256]{2,1,0:T(8,128)(2,1)S(1)}, u32[]{:S(2)}, u32[]{:S(2)}) collective-permute-start(bf16[2,512,256]{2,1,0:T(8,128)(2,1)S(1)} %get-tuple-element.44), channel_id=1, source_target_pairs={{0,16},{1,17},{2,18},{3,19},{4,20},{5,21},{6,22},{7,23},{8,24},{9,... | collective-permute-start | bytes 1572872 | tf_op jit(solution)/shard_map/ppermute | solution.py:27
  228.5 72.5 %collective-permute-start.24 = (bf16[2,256,1024]{2,1,0:T(8,128)(2,1)S(1)}, bf16[2,256,1024]{2,1,0:T(8,128)(2,1)S(1)}, u32[]{:S(2)}, u32[]{:S(2)}) collective-permute-start(bf16[2,256,1024]{2,1,0:T(8,128)(2,1)S(1)} %get-tuple-element.41), channel_id=1, source_target_pairs={{0,16},{1,17},{2,18},{3,19},{4,20},{5,21},{6,22},{7,23},{8,24},{9,... | collective-permute-start | bytes 3145736 | tf_op jit(solution)/shard_map/ppermute | solution.py:27
  230.0 71.0 %collective-permute-start.25 = (bf16[2,256,1024]{2,1,0:T(8,128)(2,1)S(1)}, bf16[2,256,1024]{2,1,0:T(8,128)(2,1)S(1)}, u32[]{:S(2)}, u32[]{:S(2)}) collective-permute-start(bf16[2,256,1024]{2,1,0:T(8,128)(2,1)S(1)} %get-tuple-element.43), channel_id=1, source_target_pairs={{0,32},{1,33},{2,34},{3,35},{4,36},{5,37},{6,38},{7,39},{8,40},{9,... | collective-permute-start | bytes 3145736 | tf_op jit(solution)/shard_map/ppermute | solution.py:27
  232.6 68.4 %collective-permute-start.26 = (bf16[2,256,1024]{2,1,0:T(8,128)(2,1)S(1)}, bf16[2,256,1024]{2,1,0:T(8,128)(2,1)S(1)}, u32[]{:S(2)}, u32[]{:S(2)}) collective-permute-start(bf16[2,256,1024]{2,1,0:T(8,128)(2,1)S(1)} %get-tuple-element.42), channel_id=1, source_target_pairs={{0,48},{1,49},{2,50},{3,51},{4,52},{5,53},{6,54},{7,55},{8,56},{9,... | collective-permute-start | bytes 3145736 | tf_op jit(solution)/shard_map/ppermute | solution.py:27
  234.1 63.8 %collective-permute-start.30 = (bf16[2,512,256]{2,1,0:T(8,128)(2,1)S(1)}, bf16[2,512,256]{2,1,0:T(8,128)(2,1)S(1)}, u32[]{:S(2)}, u32[]{:S(2)}) collective-permute-start(bf16[2,512,256]{2,1,0:T(8,128)(2,1)S(1)} %get-tuple-element.46), channel_id=1, source_target_pairs={{0,32},{1,33},{2,34},{3,35},{4,36},{5,37},{6,38},{7,39},{8,40},{9,... | collective-permute-start | bytes 1572872 | tf_op jit(solution)/shard_map/ppermute | solution.py:27
  241.3 59.4 %collective-permute-start.31 = (bf16[2,512,256]{2,1,0:T(8,128)(2,1)S(1)}, bf16[2,512,256]{2,1,0:T(8,128)(2,1)S(1)}, u32[]{:S(2)}, u32[]{:S(2)}) collective-permute-start(bf16[2,512,256]{2,1,0:T(8,128)(2,1)S(1)} %get-tuple-element.45), channel_id=1, source_target_pairs={{0,48},{1,49},{2,50},{3,51},{4,52},{5,53},{6,54},{7,55},{8,56},{9,... | collective-permute-start | bytes 1572872 | tf_op jit(solution)/shard_map/ppermute | solution.py:27
  303.0 82.0 %collective-permute-start.27 = (bf16[256,1024]{1,0:T(8,128)(2,1)}, bf16[256,1024]{1,0:T(8,128)(2,1)}, u32[]{:S(2)}, u32[]{:S(2)}) collective-permute-start(bf16[256,1024]{1,0:T(8,128)(2,1)} %fusion.15), channel_id=1, source_target_pairs={{0,64},{1,65},{2,66},{3,67},{4,68},{5,69},{6,70},{7,71},{8,72},{9,... | collective-permute-start | bytes 1572872 | tf_op jit(solution)/shard_map/ppermute | solution.py:27
  306.7 76.5 %collective-permute-start.32 = (bf16[512,256]{1,0:T(8,128)(2,1)S(1)}, bf16[512,256]{1,0:T(8,128)(2,1)}, u32[]{:S(2)}, u32[]{:S(2)}) collective-permute-start(bf16[512,256]{1,0:T(8,128)(2,1)S(1)} %fusion.19), channel_id=1, source_target_pairs={{0,64},{1,65},{2,66},{3,67},{4,68},{5,69},{6,70},{7,71},{8,72},{9,... | collective-permute-start | bytes 786440 | tf_op jit(solution)/shard_map/ppermute | solution.py:27
  (39 other events, 474.8 us)

commit v2 on v0

v2 whole, which is shorter than its diff:
```python
import functools

import jax
import jax.numpy as jnp
import numpy as np
from jax import lax
from jax.experimental import pallas as pl
from jax.experimental.pallas import tpu as pltpu
from jax.sharding import Mesh, PartitionSpec as P

AXES = ("zh", "x", "zl", "y", "c")
SIZES = (2, 4, 2, 4, 2)
D = 2048
ROWS = 128
F = 512
BF = jnp.bfloat16
F32 = jnp.float32
MIB = 1024 * 1024
ANY = pl.BlockSpec(memory_space=pl.ANY)


def send(value, **shift):
    ids = np.arange(128).reshape(SIZES)
    pairs = []
    for at in np.ndindex(*SIZES):
        to = tuple((a + shift.get(n, 0)) % s for a, n, s in zip(at, AXES, SIZES))
        pairs.append((int(ids[at]), int(ids[to])))
    return lax.ppermute(value, AXES, pairs)


def nt(a, b):
    return lax.dot_general(a, b, (((1,), (1,)), ((), ())), preferred_element_type=F32)


def nn(a, b):
    return lax.dot_general(a, b, (((1,), (0,)), ((), ())), preferred_element_type=F32)


def struct(*shape, dtype=BF):
    return jax.ShapeDtypeStruct(shape, dtype)


def params():
    return pltpu.CompilerParams(vmem_limit_bytes=60 * MIB)


def cost(mults=0):
    return pl.CostEstimate(flops=2 * mults + 1024, bytes_accessed=1024, transcendentals=0)


def after(value, *others):
    return lax.optimization_barrier((value, *others))[0]


def first_kernel(s_ref, tokens, gate, up, wg, wu, wd, unit_t, pack):
    @pl.when(pl.program_id(0) == 0)
    def _():
        x = tokens[...].astype(F32)
        unit = x * lax.rsqrt(jnp.mean(x * x, axis=-1, keepdims=True) + 1e-05)
        unit_t[...] = unit.T.astype(BF)

    for j in range(2):
        pack[j, :128] = gate[j, 0]
        pack[j, 128:256] = up[j, 0]
        pack[j, 256:512] = wg[j * 256 : j * 256 + 256]
        pack[j, 512:768] = wu[j * 256 : j * 256 + 256]
        for k in range(4):
            at = 768 + k * 64
            pack[j, at : at + 64] = wd[j * 64 : j * 64 + 64, k * F : k * F + F]


def first_call(scalars, tokens, gate4, up4, wg, wu, wd):
    half = pl.BlockSpec((2, 1, ROWS, F), lambda i, s: (i, 1 - s[8], 0, 0))
    rows = pl.BlockSpec((512, F), lambda i, s: (i, 0))
    return pl.pallas_call(
        first_kernel,
        grid_spec=pltpu.PrefetchScalarGridSpec(
            num_scalar_prefetch=1,
            grid=(4,),
            in_specs=[
                pl.BlockSpec((ROWS, D), lambda i, s: (0, 0)),
                half,
                half,
                rows,
                rows,
                pl.BlockSpec((128, D), lambda i, s: (i, 0)),
            ],
            out_specs=[
                pl.BlockSpec((D, ROWS), lambda i, s: (0, 0)),
                pl.BlockSpec((2, 1024, F), lambda i, s: (i, 0, 0)),
            ],
        ),
        out_shape=[struct(D, ROWS), struct(8, 1024, F)],
        compiler_params=params(),
        cost_estimate=cost(),
        name="first",
    )(scalars, tokens, gate4, up4, wg, wu, wd)


def factor_kernel(s_ref, go, uo, gx, ux, for_gate, for_up, act_t):
    for g, u, at in ((go[0, 0], uo[0, 0], 0), (gx[0], ux[0], F)):
        g = g.astype(F32)
        u = u.astype(F32)
        sigma = 1.0 / (1.0 + jnp.exp(-g))
        silu = g * sigma
        for_up[:, at : at + F] = silu.astype(BF)
        for_gate[:, at : at + F] = (u * sigma * (1.0 + g * (1.0 - sigma))).astype(BF)
        act_t[at : at + F, :] = (silu * u).T.astype(BF)


def factor_call(scalars, gate4, up4, swapped):
    mine = pl.BlockSpec((1, 1, ROWS, F), lambda i, s: (s[i], s[8], 0, 0))
    rows = pl.BlockSpec((ROWS, 2 * F), lambda i, s: (i, 0))
    return pl.pallas_call(
        factor_kernel,
        grid_spec=pltpu.PrefetchScalarGridSpec(
            num_scalar_prefetch=1,
            grid=(8,),
            in_specs=[
                mine,
                mine,
                pl.BlockSpec((1, ROWS, F), lambda i, s: (s[i], 0, 0)),
                pl.BlockSpec((1, ROWS, F), lambda i, s: (s[i], 1, 0)),
            ],
            out_specs=[rows, rows, pl.BlockSpec((2 * F, ROWS), lambda i, s: (0, i))],
        ),
        out_shape=[struct(8 * ROWS, 2 * F)] * 3,
        compiler_params=params(),
        cost_estimate=cost(),
        name="factors",
    )(scalars, gate4, up4, swapped, swapped)


def delta_body(dy, for_gate, for_up, weights, gd, ud, outs, held, sem):
    wd, wg, wu, pack = weights
    wd_own, wd_oth, wg_own, wg_oth, wu_own, wu_oth = held
    moves = ((wd, wd_own), (pack.at[:, 768:1024], wd_oth), (wg, wg_own))
    moves += ((pack.at[:, 256:512], wg_oth), (wu, wu_own), (pack.at[:, 512:768], wu_oth))
    copies = [pltpu.make_async_copy(a, b, sem.at[k]) for k, (a, b) in enumerate(moves)]
    for copy in copies:
        copy.start()
    rows = jnp.concatenate([d[...] for d in dy], axis=0)

    def store(hidden, at):
        gd[:, at] = (hidden * for_gate[:, at].astype(F32)).astype(BF)
        ud[:, at] = (hidden * for_up[:, at].astype(F32)).astype(BF)

    copies[0].wait()
    store(nt(rows, wd_own[...]), slice(0, F))
    copies[1].wait()
    hidden = 0
    for k in range(4):
        block = wd_oth[:, k * 64 : k * 64 + 64, :].reshape(F, F)
        hidden = hidden + nt(rows[:, k * F : k * F + F], block)
    store(hidden, slice(F, 2 * F))
    for copy in copies[2:]:
        copy.wait()
    for n in range(4):
        at, two = slice(n * 512, n * 512 + 512), slice(2 * n, 2 * n + 2)
        out = nt(gd[:, :F], wg_own[at, :])
        out = out + nt(gd[:, F:], wg_oth[two].reshape(F, F))
        out = out + nt(ud[:, :F], wu_own[at, :])
        out = (out + nt(ud[:, F:], wu_oth[two].reshape(F, F))).astype(BF)
        for k, ref in enumerate(outs):
            ref[:, at] = out[k * ROWS : k * ROWS + ROWS]


def delta_kernel_a(*refs):
    dy, (fg, fu), weights, (gd, ud, own, z, ym, yp) = refs[:4], refs[4:6], refs[6:10], refs[-13:-7]
    delta_body(dy, fg, fu, weights, gd, ud, (own, z, ym.at[0], yp.at[0]), refs[-7:-1], refs[-1])


def delta_kernel_b(*refs):
    dy, (fg, fu), weights = refs[:4], refs[4:6], refs[6:10]
    gd, ud, two, ym, yp, z2 = refs[-13:-7]
    delta_body(dy, fg, fu, weights, gd, ud, (two, ym.at[0], yp.at[0], z2), refs[-7:-1], refs[-1])


def delta_call(second, dy, factors, weights, pairs=(), behind=()):
    at = 1 if second else 0
    whole = pl.BlockSpec((ROWS, D), lambda i: (0, 0))
    side = pl.BlockSpec((1, ROWS, D), lambda i: (at, 0, 0))
    wide = pl.BlockSpec((4 * ROWS, 2 * F), lambda i: (at, 0))
    here = pl.BlockSpec((4 * ROWS, 2 * F), lambda i: (0, 0))
    outs = [struct(4 * ROWS, 2 * F)] * 2
    pair = struct(2, ROWS, D)
    if second:
        outs += [struct(ROWS, D), pair, pair, struct(ROWS, D)]
        out_specs = [here, here, whole, side, side, whole]
        aliases = {10: 3, 11: 4}
    else:
        outs += [struct(ROWS, D), struct(ROWS, D), pair, pair]
        out_specs = [here, here, whole, whole, side, side]
        aliases = {}
    extra = (*pairs, *behind)
    return pl.pallas_call(
        delta_kernel_b if second else delta_kernel_a,
        grid=(1,),
        in_specs=[whole] * 4 + [wide] * 2 + [ANY] * 4 + [ANY] * len(extra),
        out_specs=out_specs,
        out_shape=outs,
        scratch_shapes=[pltpu.VMEM((F, D), BF), pltpu.VMEM((8, 256, F), BF)]
        + [pltpu.VMEM((D, F), BF), pltpu.VMEM((8, 256, F), BF)] * 2
        + [pltpu.SemaphoreType.DMA((6,))],
        input_output_aliases=aliases,
        compiler_params=params(),
        cost_estimate=cost(6 * 512 * 1024 * D if second else 0),
        name="deltas_b" if second else "deltas_a",
    )(*dy, *factors, *weights, *extra)


def down_kernel(s_ref, act_t, *refs):
    dy, (out_own, out_oth) = refs[:16], refs[-2:]
    for q in range(2):
        cols = jnp.concatenate([d[...] for d in dy[8 * q : 8 * q + 8]], axis=0)
        out = nn(act_t[...], cols).astype(BF)
        out_own[q] = out[:F]
        out_oth[q] = out[F:]


def down_call(scalars, act_t, dy, behind):
    cols = [pl.BlockSpec((ROWS, 256), lambda i, s, q=q: (0, s[9 + 2 * i + q])) for q in range(2)]
    return pl.pallas_call(
        down_kernel,
        grid_spec=pltpu.PrefetchScalarGridSpec(
            num_scalar_prefetch=1,
            grid=(4,),
            in_specs=[pl.BlockSpec((2 * F, 8 * ROWS), lambda i, s: (0, 0))]
            + [cols[0]] * 8
            + [cols[1]] * 8
            + [ANY] * len(behind),
            out_specs=[pl.BlockSpec((2, F, 256), lambda i, s: (i, 0, 0))] * 2,
        ),
        out_shape=[struct(8, F, 256)] * 2,
        compiler_params=params(),
        cost_estimate=cost(),
        name="down",
    )(scalars, act_t, *dy, *dy, *behind)


def weight_kernel(s_ref, gda, gdb, uda, udb, *refs):
    out_own, out_oth, out_gain = refs[-3:]
    for q in range(2):
        unit, gain, wgo, wuo, wgx, wux = refs[6 * q : 6 * q + 6]
        low = jnp.concatenate([unit[s_ref[p]] for p in range(4)], axis=1)
        high = jnp.concatenate([unit[s_ref[p]] for p in range(4, 8)], axis=1)
        scale = gain[...]
        total = jnp.zeros((256, 128), F32)
        for da, db, at, w_own, w_oth in (
            (gda, gdb, 0, wgo[...], wgx[0]),
            (uda, udb, F, wuo[...], wux[0]),
        ):
            for half, w, out in ((0, w_own, out_own), (F, w_oth, out_oth)):
                grad = nn(low, da[:, half : half + F]) + nn(high, db[:, half : half + F])
                out[q, :, at : at + F] = (grad * scale).astype(BF)
                prod = grad * w.astype(F32)
                for k in range(4):
                    total = total + prod[:, k * 128 : (k + 1) * 128]
        out_gain[q] = total


def weight_call(scalars, deltas, unit, gain, own, other, behind):
    full = pl.BlockSpec((4 * ROWS, 2 * F), lambda i, s: (0, 0))
    specs, args = [full] * 4, list(deltas)
    for q in range(2):
        at = lambda i, s, q=q: (s[9 + 2 * i + q], 0)
        specs.append(pl.BlockSpec((8, 256, ROWS), lambda i, s, q=q: (0, s[9 + 2 * i + q], 0)))
        specs += [pl.BlockSpec((256, 1), at)] + [pl.BlockSpec((256, F), at)] * 2
        for k in (1, 2):
            specs.append(pl.BlockSpec((1, 256, F), lambda i, s, q=q, k=k: (s[9 + 2 * i + q], k, 0)))
        args += [unit, gain, *own, *other]
    specs += [ANY] * len(behind)
    args += behind
    return pl.pallas_call(
        weight_kernel,
        grid_spec=pltpu.PrefetchScalarGridSpec(
            num_scalar_prefetch=1,
            grid=(4,),
            in_specs=specs,
            out_specs=[pl.BlockSpec((2, 256, 2 * F), lambda i, s: (i, 0, 0))] * 2
            + [pl.BlockSpec((2, 256, 128), lambda i, s: (i, 0, 0))],
        ),
        out_shape=[struct(8, 256, 2 * F)] * 2 + [struct(8, 256, 128, dtype=F32)],
        compiler_params=params(),
        cost_estimate=cost(),
        name="weights",
    )(scalars, *args)


def last_kernel(tokens, dy, gain, own, a, b, e, f, out):
    x = tokens[...].astype(F32)
    inverse = lax.rsqrt(jnp.mean(x * x, axis=-1, keepdims=True) + 1e-05)
    unit = x * inverse
    normed_grad = total_of(own[...], a[0], b[0], e[...], f[...])
    scaled = gain[...] * normed_grad
    mean_term = jnp.mean(scaled * unit, axis=-1, keepdims=True)
    out[...] = (dy[...].astype(F32) + inverse * (scaled - unit * mean_term)).astype(BF)


def last_call(tokens, dy, gain, own, a, b, e, f):
    rows = pl.BlockSpec((32, D), lambda i: (i, 0))
    first = pl.BlockSpec((1, 32, D), lambda i: (0, i, 0))
    return pl.pallas_call(
        last_kernel,
        grid=(4,),
        in_specs=[rows, rows, pl.BlockSpec((1, D), lambda i: (0, 0)), rows, first, first, rows, rows],
        out_specs=rows,
        out_shape=struct(ROWS, D),
        compiler_params=params(),
        cost_estimate=cost(),
        name="last",
    )(tokens, dy, gain, own, a, b, e, f)


def total_of(*terms):
    out = terms[0].astype(F32)
    for term in terms[1:]:
        out = out + term.astype(F32)
    return out


def pair_sums(own, back):
    return [total_of(own[2 * r : 2 * r + 2], back[2 * r : 2 * r + 2]) for r in range(4)]


def along_x(parts):
    return [send(parts[r].astype(BF), x=r) for r in (1, 2, 3)]


def local(tokens, gain, gate_saved, up_saved, out_grad, gate_weight, up_weight, down_weight):
    zh, x_at, zl, y, c = (lax.axis_index(a) for a in AXES)
    oz = 1 - zl
    near = [zl * 4 + (y + k) % 4 for k in (0, 3, 1, 2)]
    far = [oz * 4 + (y + k) % 4 for k in (0, 3, 1, 2)]
    places = [near[0], far[0], near[1], near[2], near[3], far[1], far[2], far[3]]
    order = [((zh + q) % 2) * 4 + (x_at + r) % 4 for r in range(4) for q in range(2)]
    scalars = jnp.stack(places + [c] + order).astype(jnp.int32)

    d_z = send(out_grad, zl=1)
    d_2 = send(out_grad, y=2)
    d_m = send(out_grad, y=1)
    d_p = send(out_grad, y=-1)
    gate4 = gate_saved.reshape(8, 2, ROWS, F)
    up4 = up_saved.reshape(8, 2, ROWS, F)
    unit_t, pack = first_call(scalars, tokens, gate4, up4, gate_weight, up_weight, down_weight)
    pack = send(pack, c=1)
    weights = (down_weight, gate_weight, up_weight, pack)

    d_zm = send(d_z, y=1)
    d_zp = send(d_z, y=-1)
    d_z2 = send(d_2, zl=1)
    unit = lax.all_gather(after(unit_t, d_m, d_p, d_zm, d_zp, d_z2), ("zl", "y"), axis=0, tiled=False)
    *factors, act_t = factor_call(scalars, gate4, up4, pack)
    dy_a = (out_grad, d_z, d_m, d_p)
    dy_b = (d_2, d_zm, d_zp, d_z2)
    gd_a, ud_a, n_own, n_z, ym, yp = delta_call(False, dy_a, factors, weights)
    down_own, down_oth = down_call(scalars, act_t, dy_a + dy_b, (gd_a,))
    gd_b, ud_b, n_2, n_ym, n_yp, n_z2 = delta_call(
        True, dy_b, factors, weights, (ym, yp), (down_oth,)
    )
    down_back = send(down_oth, c=1)
    parts = pair_sums(down_own, after(down_back, gd_b))
    down_got = along_x(parts)
    a = send(n_yp, y=1)
    b = send(n_ym, y=-1)

    w_own, w_oth, gain_part = weight_call(
        scalars,
        (gd_a, gd_b, ud_a, ud_b),
        unit,
        gain.reshape(D, 1),
        (gate_weight, up_weight),
        (pack, pack),
        [down_back],
    )
    gain_rows = jnp.sum(gain_part, axis=-1).reshape(4, 2, 256)
    gain_rows = jnp.roll(gain_rows, (x_at, zh), (0, 1)).transpose(1, 0, 2).reshape(16, 128)
    w_back = send(after(w_oth, a, b, *down_got), c=1)
    gain_rows = total_of(gain_rows, *(send(gain_rows, x=r) for r in (1, 2, 3)))
    w_parts = pair_sums(w_own, after(w_back, gain_rows))
    w_got = along_x(w_parts)
    down_both = total_of(parts[0], *down_got)
    down_last = send(down_both[1].astype(BF), zh=1)
    d = send(n_z2, zl=1)
    e = send(total_of(n_2, d).astype(BF), y=2)
    f = send(total_of(n_z, a[1], b[1]).astype(BF), zl=1)
    for shift in ({"zh": 1}, {"c": 1}, {"zl": 1}, {"y": 1}, {"y": 2}):
        gain_rows = gain_rows + send(gain_rows, **shift)
    token_grad = last_call(tokens, out_grad, gain.reshape(1, D), n_own, a, b, e, f)

    w_both = total_of(w_parts[0], *(after(g, gain_rows, token_grad) for g in w_got))
    both_sum = w_both[0] + send(w_both[1].astype(BF), zh=1).astype(F32)
    return (
        token_grad,
        gain_rows.reshape(D),
        both_sum[:, :F].astype(BF),
        both_sum[:, F:].astype(BF),
        (down_both[0] + down_last.astype(F32)).astype(BF),
    )


def solution(mesh):
    mesh = Mesh(mesh.devices.reshape(SIZES), AXES)
    dp, tensor = ("zh", "x"), ("zl", "y", "c")
    placed = (
        P(dp + tensor, None),
        P(),
        P(dp, tensor),
        P(dp, tensor),
        P(dp + tensor, None),
        P(None, tensor),
        P(None, tensor),
        P(tensor, None),
    )
    return jax.shard_map(
        local,
        mesh=mesh,
        in_specs=placed,
        out_specs=(
            P(dp + tensor, None),
            P(),
            P(dp, tensor),
            P(dp, tensor),
            P(tensor, dp),
        ),
        check_vma=False,
    )
```

time: 476 us -> 251 us (0.53)
  waiting for transfers between devices: 318 us -> 97.8 us
  Pallas kernels: 0 us -> 73.2 us
  matrix products: 69.6 us -> 0 us
  blocking collectives: 67.7 us -> 0 us
  starting transfers between devices: 0.46 us -> 40.2 us
  other arithmetic: 4.68 us -> 19.8 us
    reduce_scatter x4 -> x0, waiting for transfers between devices: 221 us -> none  [the longest x1 78.1 us: local(): lax.psum_scatter(up_part.astype(jnp.bfloat16), 'dp', scatter_dimension=0,...]
    ppermute x0 -> x31, waiting for transfers between devices: none -> 97.8 us  [send(): return lax.ppermute(value, AXES, pairs)]
    all_gather x2 -> x1, waiting for transfers between devices: 96.4 us -> 0.01 us  [local(): lax.all_gather(after(unit_t, d_m, d_p, d_zm, d_zp, d_z2), ('zl', 'y'), ax...]
    pallas_call x0 -> x7, Pallas kernels: none -> 73.2 us  [the longest x2 25.4 us: delta_call(): pl.pallas_call(delta_kernel_b if second else delta_kernel_a, grid=(1,), i...]
    dot_general x6 -> x0, matrix products: 69.6 us -> none  [the longest x3 31.9 us: left_product(): lax.dot_general(left, right, (((0,), (0,)), ((), ())), preferred_element_...]
    psum x1 -> x0, blocking collectives: 67.7 us -> none  [local(): gain_grad = lax.psum(jnp.sum(normed_grad * unit, axis=0), ('dp', 'tensor'))]
    ppermute x0 -> x31, starting transfers between devices: none -> 40.2 us  [send(): return lax.ppermute(value, AXES, pairs)]
    convert_element_type x1 -> x5, other arithmetic: 2.26 us -> 12.6 us  [the longest x2 9.36 us: along_x(): return [send(parts[r].astype(BF), x=r) for r in (1, 2, 3)]]
  transfers between devices with their start and end apart: 6 -> 32, of which waited for: 5 -> 16; matrix products, arithmetic and copies ran while one was open for 7% -> 7% of each run, Pallas kernels for 0% -> 26%
where the time goes in v2:
time: 251 us; the launch traced here: 250 us
  waiting for transfers between devices  97.8 us (39%)
  Pallas kernels  73.2 us (29%)
  starting transfers between devices  40.2 us (16%)
  other arithmetic  19.8 us (8%)
  between operations  14.4 us (6%)
  local copies, waits for them, and re-layouts  4.66 us (2%)
    ppermute x31, waiting for transfers between devices, send(): return lax.ppermute(value, AXES, pairs)  97.8 us
    ppermute x31, starting transfers between devices, send(): return lax.ppermute(value, AXES, pairs)  40.2 us
    pallas_call x2, Pallas kernels, delta_call(): pl.pallas_call(delta_kernel_b if second else delta_kernel_a, grid=(1,), i...  25.4 us
    pallas_call x1, Pallas kernels, weight_call(): pl.pallas_call(weight_kernel, grid_spec=pltpu.PrefetchScalarGridSpec(num_...  16.1 us
    pallas_call x1, Pallas kernels, down_call(): pl.pallas_call(down_kernel, grid_spec=pltpu.PrefetchScalarGridSpec(num_sc...  9.72 us
    convert_element_type x2, other arithmetic, along_x(): return [send(parts[r].astype(BF), x=r) for r in (1, 2, 3)]  9.36 us
    pallas_call x1, Pallas kernels, factor_call(): pl.pallas_call(factor_kernel, grid_spec=pltpu.PrefetchScalarGridSpec(num_...  9.28 us
    pallas_call x1, Pallas kernels, first_call(): pl.pallas_call(first_kernel, grid_spec=pltpu.PrefetchScalarGridSpec(num_s...  8.35 us
  transfers between devices with their start and end apart: 32, of which 16 were waited for; matrix products, arithmetic and copies ran while one was open for 7% of the time, Pallas kernels for 26%

profile of v2, /device:TPU:0, one launch (start us, length us, event | category | flops | bytes accessed | tf_op | source)
XLA Modules:
  0.0 250.1 jit_solution(14583129405579915419)
XLA Ops:
  8.0 8.4 %first.1 = (bf16[2048,128]{1,0:T(8,128)(2,1)}, bf16[8,1024,512]{2,1,0:T(8,128)(2,1)}) custom-call(s32[17]{0:T(128)} %stack.71.s_ref, bf16[128,2048]{1,0:T(8,128)(2,1)} %tokens.3, bf16[8,2,128,512]{3,2,1,0:T(8,128)(2,1)} %bitcast.53, bf16[8,2,128,512]{3,2,1,0:T(8,128)(2,1)} %bitcast.55, bf16[2048,512]{1,0:T(8,128)(2,1)} %refs_8_.7, ...), custom_call_target="tpu_custom_call" | custom-call | flops 1024 | bytes 1024 | tf_op jit(solution)/shard_map/first/pallas_call | solution.py:75
  20.0 2.9 %collective-permute-start.4 = (bf16[128,2048]{1,0:T(8,128)(2,1)S(1)}, bf16[128,2048]{1,0:T(8,128)(2,1)S(1)}, u32[]{:S(2)}, u32[]{:S(2)}) collective-permute-start(bf16[128,2048]{1,0:T(8,128)(2,1)S(1)} %copy-done), channel_id=1, source_target_pairs={{0,4},{1,5},{2,6},{3,7},{4,0},{5,1},{6,2},{7,3},{8,12},{9,13},{10,... | collective-permute-start | bytes 1572872 | tf_op jit(solution)/shard_map/ppermute | solution.py:28
  24.2 6.7 %collective-permute-done.refs_1_.refs_9_ = bf16[128,2048]{1,0:T(8,128)(2,1)S(1)} collective-permute-done((bf16[128,2048]{1,0:T(8,128)(2,1)S(1)}, bf16[128,2048]{1,0:T(8,128)(2,1)S(1)}, u32[]{:S(2)}, u32[]{:S(2)}) %collective-permute-start) | collective-permute-done | bytes 524320 | tf_op jit(solution)/shard_map/ppermute | solution.py:28
  36.2 10.7 %collective-permute-done.4.refs_4_.refs_12_.refs_0_ = bf16[128,2048]{1,0:T(8,128)(2,1)S(1)} collective-permute-done((bf16[128,2048]{1,0:T(8,128)(2,1)S(1)}, bf16[128,2048]{1,0:T(8,128)(2,1)S(1)}, u32[]{:S(2)}, u32[]{:S(2)}) %collective-permute-start.4) | collective-permute-done | bytes 524320 | tf_op jit(solution)/shard_map/ppermute | solution.py:28
  47.0 9.8 %collective-permute-done.5.refs_5_.refs_13_.refs_1_ = bf16[128,2048]{1,0:T(8,128)(2,1)S(1)} collective-permute-done((bf16[128,2048]{1,0:T(8,128)(2,1)S(1)}, bf16[128,2048]{1,0:T(8,128)(2,1)S(1)}, u32[]{:S(2)}, u32[]{:S(2)}) %collective-permute-start.5) | collective-permute-done | bytes 524320 | tf_op jit(solution)/shard_map/ppermute | solution.py:28
  60.1 9.3 %factors.1 = (bf16[1024,1024]{1,0:T(8,128)(2,1)}, bf16[1024,1024]{1,0:T(8,128)(2,1)}, bf16[1024,1024]{1,0:T(8,128)(2,1)}) custom-call(s32[17]{0:T(128)} %stack.71.s_ref, bf16[8,2,128,512]{3,2,1,0:T(8,128)(2,1)} %bitcast.54, bf16[8,2,128,512]{3,2,1,0:T(8,128)(2,1)} %bitcast.56, ...), custom_call_target="tpu_custom_call" | custom-call | flops 1024 | bytes 1024 | tf_op jit(solution)/shard_map/factors/pallas_call | solution.py:114
  69.5 12.6 %deltas_a.1 = (bf16[512,1024]{1,0:T(8,128)(2,1)}, bf16[512,1024]{1,0:T(8,128)(2,1)}, bf16[128,2048]{1,0:T(8,128)(2,1)}, bf16[128,2048]{1,0:T(8,128)(2,1)}, bf16[...) custom-call(bf16[128,2048]{1,0:T(8,128)(2,1)} %dy.1, bf16[128,2048]{1,0:T(8,128)(2,1)} %copy-done.2, ...), custom_call_target="tpu_custom_call" | custom-call | flops 1024 | bytes 1024 | tf_op jit(solution)/shard_map/deltas_a/pallas_call | solution.py:196
  82.1 9.7 %down.1 = (bf16[8,512,256]{2,1,0:T(8,128)(2,1)}, bf16[8,512,256]{2,1,0:T(8,128)(2,1)}) custom-call(s32[17]{0:T(128)} %stack.71.s_ref, bf16[1024,1024]{1,0:T(8,128)(2,1)} %get-tuple-element.40.act_t, bf16[128,2048]{1,0:T(8,128)(2,1)} %dy.1, bf16[128,2048]{1,0:T(8,128)(2,1)} %copy-done.2, bf16[128,2048]{1,0:T(8,128)(2,1)} %copy-done.3, ...), custom_call_target="tpu_custom_call" | custom-call | flops 1024 | bytes 1024 | tf_op jit(solution)/shard_map/down/pallas_call | solution.py:223
  92.1 12.8 %deltas_b.1 = (bf16[512,1024]{1,0:T(8,128)(2,1)}, bf16[512,1024]{1,0:T(8,128)(2,1)}, bf16[128,2048]{1,0:T(8,128)(2,1)}, bf16[2,128,2048]{2,1,0:T(8,128)(2,1)}, b...) custom-call(bf16[128,2048]{1,0:T(8,128)(2,1)} %copy-done.6, ...), custom_call_target="tpu_custom_call", output_to_operand_aliasing={{3}: (10, {}), {4}: (11, {})} | custom-call | flops 12884902912 | bytes 1024 | tf_op jit(solution)/shard_map/deltas_b/pallas_call | solution.py:196
  105.2 3.0 %collective-permute-start.9 = (bf16[2,128,2048]{2,1,0:T(8,128)(2,1)}, bf16[2,128,2048]{2,1,0:T(8,128)(2,1)}, u32[]{:S(2)}, u32[]{:S(2)}) collective-permute-start(bf16[2,128,2048]{2,1,0:T(8,128)(2,1)} %get-tuple-element.44), channel_id=1, source_target_pairs={{0,6},{1,7},{2,0},{3,1},{4,2},{5,3},{6,4},{7,5},{8,14},{9,15},{10,... | collective-permute-start | bytes 3145736 | tf_op jit(solution)/shard_map/ppermute | solution.py:28
  108.2 3.5 %add_convert_fusion.3 = (bf16[2,512,256]{2,1,0:T(8,128)(2,1)}, bf16[2,512,256]{2,1,0:T(8,128)(2,1)}, bf16[2,512,256]{2,1,0:T(8,128)(2,1)}) fusion(bf16[8,512,256]{2,1,0:T(8,128)(2,1)S(1)} %collective-permute-done.13.refs_12_, bf16[8,512,256]{2,1,0:T(8,128)(2,1)} %get-tuple-element.56), kind=kLoop, calls=%fused_computation.12 | loop fusion | flops 3145728 | bytes 4718592 | tf_op jit(solution)/shard_map/convert_element_type | solution.py:327
  113.2 2.7 %collective-permute-start.23 = (bf16[2,512,256]{2,1,0:T(8,128)(2,1)}, bf16[2,512,256]{2,1,0:T(8,128)(2,1)S(1)}, u32[]{:S(2)}, u32[]{:S(2)}) collective-permute-start(bf16[2,512,256]{2,1,0:T(8,128)(2,1)} %get-tuple-element.67), channel_id=1, source_target_pairs={{0,32},{1,33},{2,34},{3,35},{4,36},{5,37},{6,38},{7,39},{8,40},{9,... | collective-permute-start | bytes 1572872 | tf_op jit(solution)/shard_map/ppermute | solution.py:28
  118.7 16.1 %weights.1 = (bf16[8,256,1024]{2,1,0:T(8,128)(2,1)}, bf16[8,256,1024]{2,1,0:T(8,128)(2,1)}, f32[8,256,128]{2,1,0:T(8,128)}) custom-call(s32[17]{0:T(128)} %stack.71.s_ref, bf16[512,1024]{1,0:T(8,128)(2,1)} %get-tuple-element.41.refs_16_.gda, bf16[512,1024]{1,0:T(8,128)(2,1)} %get-tuple-element.48.gdb, bf16[512,1024]{1,0:T(8,128)(2,1)} %get-tuple-element.49.uda, ...), custom_call_target="tpu_custom_call" | custom-call | flops 1024 | bytes 1024 | tf_op jit(solution)/shard_map/weights/pallas_call | solution.py:274
  134.9 4.2 %collective-permute-done.23 = bf16[2,512,256]{2,1,0:T(8,128)(2,1)S(1)} collective-permute-done((bf16[2,512,256]{2,1,0:T(8,128)(2,1)}, bf16[2,512,256]{2,1,0:T(8,128)(2,1)S(1)}, u32[]{:S(2)}, u32[]{:S(2)}) %collective-permute-start.23) | collective-permute-done | bytes 524320 | tf_op jit(solution)/shard_map/ppermute | solution.py:28
  145.6 3.3 %collective-permute-done.15 = f32[16,128]{1,0:T(8,128)S(1)} collective-permute-done((f32[16,128]{1,0:T(8,128)S(1)}, f32[16,128]{1,0:T(8,128)S(1)}, u32[]{:S(2)}, u32[]{:S(2)}) %collective-permute-start.15) | collective-permute-done | bytes 8224 | tf_op jit(solution)/shard_map/ppermute | solution.py:28
  149.8 3.4 %collective-permute-start.17 = (f32[16,128]{1,0:T(8,128)S(1)}, f32[16,128]{1,0:T(8,128)S(1)}, u32[]{:S(2)}, u32[]{:S(2)}) collective-permute-start(f32[16,128]{1,0:T(8,128)S(1)} %add_add_fusion), channel_id=1, source_target_pairs={{0,64},{1,65},{2,66},{3,67},{4,68},{5,69},{6,70},{7,71},{8,72},{9,... | collective-permute-start | bytes 24584 | tf_op jit(solution)/shard_map/ppermute | solution.py:28
  153.2 2.8 %collective-permute-done.17 = f32[16,128]{1,0:T(8,128)S(1)} collective-permute-done((f32[16,128]{1,0:T(8,128)S(1)}, f32[16,128]{1,0:T(8,128)S(1)}, u32[]{:S(2)}, u32[]{:S(2)}) %collective-permute-start.17) | collective-permute-done | bytes 8224 | tf_op jit(solution)/shard_map/ppermute | solution.py:28
  160.8 5.9 %add_convert_fusion.2 = (bf16[2,256,1024]{2,1,0:T(8,128)(2,1)S(1)}, bf16[2,256,1024]{2,1,0:T(8,128)(2,1)}, bf16[2,256,1024]{2,1,0:T(8,128)(2,1)}) fusion(bf16[8,256,1024]{2,1,0:T(8,128)(2,1)} %collective-permute-done.25, bf16[8,256,1024]{2,1,0:T(8,128)(2,1)} %get-tuple-element.54), kind=kLoop, calls=%fused_computation.3 | loop fusion | flops 6291456 | bytes 9437184 | tf_op jit(solution)/shard_map/convert_element_type | solution.py:327
  175.6 8.6 %collective-permute-done.12.f = bf16[128,2048]{1,0:T(8,128)(2,1)S(1)} collective-permute-done((bf16[128,2048]{1,0:T(8,128)(2,1)S(1)}, bf16[128,2048]{1,0:T(8,128)(2,1)S(1)}, u32[]{:S(2)}, u32[]{:S(2)}) %collective-permute-start.12) | collective-permute-done | bytes 524320 | tf_op jit(solution)/shard_map/ppermute | solution.py:28
  185.0 4.4 %last.1 = bf16[128,2048]{1,0:T(8,128)(2,1)} custom-call(bf16[128,2048]{1,0:T(8,128)(2,1)} %tokens.3, bf16[128,2048]{1,0:T(8,128)(2,1)} %dy.1, f32[1,2048]{1,0:T(1,128)} %bitcast.57, bf16[128,2048]{1,0:T(8,128)(2,1)} %get-tuple-element.37.own, bf16[2,128,2048]{2,1,0:T(8,128)(2,1)} %copy-done.5, bf16[2,128,2048]{2,1,0:T(8,128)(2,1)} %collective-permute-done.9.b, ...), custom_call_target="tpu_custom_call" | custom-call | flops 1024 | bytes 1024 | tf_op jit(solution)/shard_map/last/pallas_call | solution.py:303
  191.5 21.8 %collective-permute-done.28 = bf16[2,256,1024]{2,1,0:T(8,128)(2,1)S(1)} collective-permute-done((bf16[2,256,1024]{2,1,0:T(8,128)(2,1)}, bf16[2,256,1024]{2,1,0:T(8,128)(2,1)S(1)}, u32[]{:S(2)}, u32[]{:S(2)}) %collective-permute-start.28) | collective-permute-done | bytes 1048608 | tf_op jit(solution)/shard_map/ppermute | solution.py:28
  213.4 3.7 %collective-permute-done.26 = bf16[2,256,1024]{2,1,0:T(8,128)(2,1)} collective-permute-done((bf16[2,256,1024]{2,1,0:T(8,128)(2,1)S(1)}, bf16[2,256,1024]{2,1,0:T(8,128)(2,1)}, u32[]{:S(2)}, u32[]{:S(2)}) %collective-permute-start.26) | collective-permute-done | bytes 1048608 | tf_op jit(solution)/shard_map/ppermute | solution.py:28
  217.0 3.3 %convert_add_fusion = f32[2,256,1024]{2,1,0:T(8,128)S(1)} fusion(bf16[2,256,1024]{2,1,0:T(8,128)(2,1)S(1)} %collective-permute-done.28, bf16[2,256,1024]{2,1,0:T(8,128)(2,1)} %collective-permute-done.27, bf16[2,256,1024]{2,1,0:T(8,128)(2,1)} %collective-permute-done.26, bf16[8,256,1024]{2,1,0:T(8,128)(2,1)} %collective-permute-done.25, ...), kind=kLoop, calls=%fused_computation | loop fusion | flops 4718592 | bytes 7340032 | tf_op jit(solution)/shard_map/add | solution.py:318
  224.1 17.3 %collective-permute-done.30 = bf16[512,256]{1,0:T(8,128)(2,1)S(1)} collective-permute-done((bf16[512,256]{1,0:T(8,128)(2,1)S(1)}, bf16[512,256]{1,0:T(8,128)(2,1)S(1)}, u32[]{:S(2)}, u32[]{:S(2)}) %collective-permute-start.30) | collective-permute-done | bytes 262176 | tf_op jit(solution)/shard_map/ppermute | solution.py:28
  (115 shorter events, 48.8 us)
Async XLA Ops:
  7.2 111.6 %all-gather.3.cloned.1.call-start = ((), (), s32[]{:S(2)}) async-start(), calls=%async_computation | async-start | bytes 4718592 | tf_op jit(solution)/shard_map/all_gather | solution.py:352
  16.3 43.8 %collective-permute-start.3 = (bf16[8,1024,512]{2,1,0:T(8,128)(2,1)}, bf16[8,1024,512]{2,1,0:T(8,128)(2,1)}, u32[]{:S(2)}, u32[]{:S(2)}) collective-permute-start(bf16[8,1024,512]{2,1,0:T(8,128)(2,1)} %get-tuple-element.34), channel_id=1, source_target_pairs={{0,1},{1,0},{2,3},{3,2},{4,5},{5,4},{6,7},{7,6},{8,9},{9,8},{10,11... | collective-permute-start | bytes 25165832 | tf_op jit(solution)/shard_map/ppermute | solution.py:28
  16.3 14.6 %collective-permute-start = (bf16[128,2048]{1,0:T(8,128)(2,1)S(1)}, bf16[128,2048]{1,0:T(8,128)(2,1)S(1)}, u32[]{:S(2)}, u32[]{:S(2)}) collective-permute-start(bf16[128,2048]{1,0:T(8,128)(2,1)S(1)} %copy-done), channel_id=1, source_target_pairs={{0,8},{1,9},{2,10},{3,11},{4,12},{5,13},{6,14},{7,15},{8,0},{9,1},... | collective-permute-start | bytes 1572872 | tf_op jit(solution)/shard_map/ppermute | solution.py:28
  18.4 15.3 %collective-permute-start.1 = (bf16[128,2048]{1,0:T(8,128)(2,1)S(1)}, bf16[128,2048]{1,0:T(8,128)(2,1)S(1)}, u32[]{:S(2)}, u32[]{:S(2)}) collective-permute-start(bf16[128,2048]{1,0:T(8,128)(2,1)S(1)} %copy-done), channel_id=1, source_target_pairs={{0,2},{1,3},{2,4},{3,5},{4,6},{5,7},{6,0},{7,1},{8,10},{9,11},{10,... | collective-permute-start | bytes 1572872 | tf_op jit(solution)/shard_map/ppermute | solution.py:28
  20.0 26.9 %collective-permute-start.4 = (bf16[128,2048]{1,0:T(8,128)(2,1)S(1)}, bf16[128,2048]{1,0:T(8,128)(2,1)S(1)}, u32[]{:S(2)}, u32[]{:S(2)}) collective-permute-start(bf16[128,2048]{1,0:T(8,128)(2,1)S(1)} %copy-done), channel_id=1, source_target_pairs={{0,4},{1,5},{2,6},{3,7},{4,0},{5,1},{6,2},{7,3},{8,12},{9,13},{10,... | collective-permute-start | bytes 1572872 | tf_op jit(solution)/shard_map/ppermute | solution.py:28
  22.9 24.1 %collective-permute-start.2 = (bf16[128,2048]{1,0:T(8,128)(2,1)S(1)}, bf16[128,2048]{1,0:T(8,128)(2,1)S(1)}, u32[]{:S(2)}, u32[]{:S(2)}) collective-permute-start(bf16[128,2048]{1,0:T(8,128)(2,1)S(1)} %copy-done), channel_id=1, source_target_pairs={{0,6},{1,7},{2,0},{3,1},{4,2},{5,3},{6,4},{7,5},{8,14},{9,15},{10,... | collective-permute-start | bytes 1572872 | tf_op jit(solution)/shard_map/ppermute | solution.py:28
  30.9 25.9 %collective-permute-start.5 = (bf16[128,2048]{1,0:T(8,128)(2,1)S(1)}, bf16[128,2048]{1,0:T(8,128)(2,1)S(1)}, u32[]{:S(2)}, u32[]{:S(2)}) collective-permute-start(bf16[128,2048]{1,0:T(8,128)(2,1)S(1)} %collective-permute-done.refs_1_.refs_9_), channel_id=1, source_target_pairs={{0,2},{1,3},{2,4},{3,5},{4,6},{5,7},{6,0},{7,1},{8,10},{9,11},{10,... | collective-permute-start | bytes 1572872 | tf_op jit(solution)/shard_map/ppermute | solution.py:28
  33.7 23.1 %collective-permute-start.6 = (bf16[128,2048]{1,0:T(8,128)(2,1)S(1)}, bf16[128,2048]{1,0:T(8,128)(2,1)S(1)}, u32[]{:S(2)}, u32[]{:S(2)}) collective-permute-start(bf16[128,2048]{1,0:T(8,128)(2,1)S(1)} %collective-permute-done.refs_1_.refs_9_), channel_id=1, source_target_pairs={{0,6},{1,7},{2,0},{3,1},{4,2},{5,3},{6,4},{7,5},{8,14},{9,15},{10,... | collective-permute-start | bytes 1572872 | tf_op jit(solution)/shard_map/ppermute | solution.py:28
  91.8 16.4 %collective-permute-start.13 = (bf16[8,512,256]{2,1,0:T(8,128)(2,1)}, bf16[8,512,256]{2,1,0:T(8,128)(2,1)S(1)}, u32[]{:S(2)}, u32[]{:S(2)}) collective-permute-start(bf16[8,512,256]{2,1,0:T(8,128)(2,1)} %get-tuple-element.42.refs_12_), channel_id=1, source_target_pairs={{0,1},{1,0},{2,3},{3,2},{4,5},{5,4},{6,7},{7,6},{8,9},{9,8},{10,11... | collective-permute-start | bytes 6291464 | tf_op jit(solution)/shard_map/ppermute | solution.py:28
  104.9 29.9 %collective-permute-start.8 = (bf16[2,128,2048]{2,1,0:T(8,128)(2,1)}, bf16[2,128,2048]{2,1,0:T(8,128)(2,1)S(1)}, u32[]{:S(2)}, u32[]{:S(2)}) collective-permute-start(bf16[2,128,2048]{2,1,0:T(8,128)(2,1)} %get-tuple-element.43), channel_id=1, source_target_pairs={{0,2},{1,3},{2,4},{3,5},{4,6},{5,7},{6,0},{7,1},{8,10},{9,11},{10,... | collective-permute-start | bytes 3145736 | tf_op jit(solution)/shard_map/ppermute | solution.py:28
  105.2 29.7 %collective-permute-start.9 = (bf16[2,128,2048]{2,1,0:T(8,128)(2,1)}, bf16[2,128,2048]{2,1,0:T(8,128)(2,1)}, u32[]{:S(2)}, u32[]{:S(2)}) collective-permute-start(bf16[2,128,2048]{2,1,0:T(8,128)(2,1)} %get-tuple-element.44), channel_id=1, source_target_pairs={{0,6},{1,7},{2,0},{3,1},{4,2},{5,3},{6,4},{7,5},{8,14},{9,15},{10,... | collective-permute-start | bytes 3145736 | tf_op jit(solution)/shard_map/ppermute | solution.py:28
  111.7 23.2 %collective-permute-start.22 = (bf16[2,512,256]{2,1,0:T(8,128)(2,1)}, bf16[2,512,256]{2,1,0:T(8,128)(2,1)S(1)}, u32[]{:S(2)}, u32[]{:S(2)}) collective-permute-start(bf16[2,512,256]{2,1,0:T(8,128)(2,1)} %get-tuple-element.68), channel_id=1, source_target_pairs={{0,16},{1,17},{2,18},{3,19},{4,20},{5,21},{6,22},{7,23},{8,24},{9,... | collective-permute-start | bytes 1572872 | tf_op jit(solution)/shard_map/ppermute | solution.py:28
  113.2 25.9 %collective-permute-start.23 = (bf16[2,512,256]{2,1,0:T(8,128)(2,1)}, bf16[2,512,256]{2,1,0:T(8,128)(2,1)S(1)}, u32[]{:S(2)}, u32[]{:S(2)}) collective-permute-start(bf16[2,512,256]{2,1,0:T(8,128)(2,1)} %get-tuple-element.67), channel_id=1, source_target_pairs={{0,32},{1,33},{2,34},{3,35},{4,36},{5,37},{6,38},{7,39},{8,40},{9,... | collective-permute-start | bytes 1572872 | tf_op jit(solution)/shard_map/ppermute | solution.py:28
  115.9 23.2 %collective-permute-start.24 = (bf16[2,512,256]{2,1,0:T(8,128)(2,1)}, bf16[2,512,256]{2,1,0:T(8,128)(2,1)S(1)}, u32[]{:S(2)}, u32[]{:S(2)}) collective-permute-start(bf16[2,512,256]{2,1,0:T(8,128)(2,1)} %get-tuple-element.66), channel_id=1, source_target_pairs={{0,48},{1,49},{2,50},{3,51},{4,52},{5,53},{6,54},{7,55},{8,56},{9,... | collective-permute-start | bytes 1572872 | tf_op jit(solution)/shard_map/ppermute | solution.py:28
  139.1 21.6 %collective-permute-start.25 = (bf16[8,256,1024]{2,1,0:T(8,128)(2,1)}, bf16[8,256,1024]{2,1,0:T(8,128)(2,1)}, u32[]{:S(2)}, u32[]{:S(2)}) collective-permute-start(bf16[8,256,1024]{2,1,0:T(8,128)(2,1)} %get-tuple-element.58), channel_id=1, source_target_pairs={{0,1},{1,0},{2,3},{3,2},{4,5},{5,4},{6,7},{7,6},{8,9},{9,8},{10,11... | collective-permute-start | bytes 12582920 | tf_op jit(solution)/shard_map/ppermute | solution.py:28
  139.2 18.9 %collective-permute-start.10 = (bf16[128,2048]{1,0:T(8,128)(2,1)}, bf16[128,2048]{1,0:T(8,128)(2,1)}, u32[]{:S(2)}, u32[]{:S(2)}) collective-permute-start(bf16[128,2048]{1,0:T(8,128)(2,1)} %get-tuple-element.46), channel_id=1, source_target_pairs={{0,8},{1,9},{2,10},{3,11},{4,12},{5,13},{6,14},{7,15},{8,0},{9,1},... | collective-permute-start | bytes 1572872 | tf_op jit(solution)/shard_map/ppermute | solution.py:28
  159.3 15.9 %collective-permute-start.11 = (bf16[128,2048]{1,0:T(8,128)(2,1)S(1)}, bf16[128,2048]{1,0:T(8,128)(2,1)S(1)}, u32[]{:S(2)}, u32[]{:S(2)}) collective-permute-start(bf16[128,2048]{1,0:T(8,128)(2,1)S(1)} %add_convert_fusion.6), channel_id=1, source_target_pairs={{0,4},{1,5},{2,6},{3,7},{4,0},{5,1},{6,2},{7,3},{8,12},{9,13},{10,... | collective-permute-start | bytes 1572872 | tf_op jit(solution)/shard_map/ppermute | solution.py:28
  160.8 13.4 %collective-permute-start.20 = (f32[16,128]{1,0:T(8,128)S(1)}, f32[16,128]{1,0:T(8,128)S(1)}, u32[]{:S(2)}, u32[]{:S(2)}) collective-permute-start(f32[16,128]{1,0:T(8,128)S(1)} %add.262), channel_id=1, source_target_pairs={{0,2},{1,3},{2,4},{3,5},{4,6},{5,7},{6,0},{7,1},{8,10},{9,11},{10,... | collective-permute-start | bytes 24584 | tf_op jit(solution)/shard_map/ppermute | solution.py:28
  166.7 46.7 %collective-permute-start.28 = (bf16[2,256,1024]{2,1,0:T(8,128)(2,1)}, bf16[2,256,1024]{2,1,0:T(8,128)(2,1)S(1)}, u32[]{:S(2)}, u32[]{:S(2)}) collective-permute-start(bf16[2,256,1024]{2,1,0:T(8,128)(2,1)} %get-tuple-element.64), channel_id=1, source_target_pairs={{0,48},{1,49},{2,50},{3,51},{4,52},{5,53},{6,54},{7,55},{8,56},{9,... | collective-permute-start | bytes 3145736 | tf_op jit(solution)/shard_map/ppermute | solution.py:28
  168.9 44.5 %collective-permute-start.27 = (bf16[2,256,1024]{2,1,0:T(8,128)(2,1)}, bf16[2,256,1024]{2,1,0:T(8,128)(2,1)}, u32[]{:S(2)}, u32[]{:S(2)}) collective-permute-start(bf16[2,256,1024]{2,1,0:T(8,128)(2,1)} %get-tuple-element.65), channel_id=1, source_target_pairs={{0,32},{1,33},{2,34},{3,35},{4,36},{5,37},{6,38},{7,39},{8,40},{9,... | collective-permute-start | bytes 3145736 | tf_op jit(solution)/shard_map/ppermute | solution.py:28
  170.0 47.0 %collective-permute-start.26 = (bf16[2,256,1024]{2,1,0:T(8,128)(2,1)S(1)}, bf16[2,256,1024]{2,1,0:T(8,128)(2,1)}, u32[]{:S(2)}, u32[]{:S(2)}) collective-permute-start(bf16[2,256,1024]{2,1,0:T(8,128)(2,1)S(1)} %get-tuple-element.63), channel_id=1, source_target_pairs={{0,16},{1,17},{2,18},{3,19},{4,20},{5,21},{6,22},{7,23},{8,24},{9,... | collective-permute-start | bytes 3145736 | tf_op jit(solution)/shard_map/ppermute | solution.py:28
  175.2 14.2 %collective-permute-start.21 = (f32[16,128]{1,0:T(8,128)S(1)}, f32[16,128]{1,0:T(8,128)S(1)}, u32[]{:S(2)}, u32[]{:S(2)}) collective-permute-start(f32[16,128]{1,0:T(8,128)S(1)} %add.263), channel_id=1, source_target_pairs={{0,4},{1,5},{2,6},{3,7},{4,0},{5,1},{6,2},{7,3},{8,12},{9,13},{10,... | collective-permute-start | bytes 24584 | tf_op jit(solution)/shard_map/ppermute | solution.py:28
  220.4 21.8 %collective-permute-start.29 = (bf16[256,1024]{1,0:T(8,128)(2,1)S(1)}, bf16[256,1024]{1,0:T(8,128)(2,1)S(1)}, u32[]{:S(2)}, u32[]{:S(2)}) collective-permute-start(bf16[256,1024]{1,0:T(8,128)(2,1)S(1)} %fusion.3), channel_id=1, source_target_pairs={{0,64},{1,65},{2,66},{3,67},{4,68},{5,69},{6,70},{7,71},{8,72},{9,... | collective-permute-start | bytes 1572872 | tf_op jit(solution)/shard_map/ppermute | solution.py:28
  221.7 19.7 %collective-permute-start.30 = (bf16[512,256]{1,0:T(8,128)(2,1)S(1)}, bf16[512,256]{1,0:T(8,128)(2,1)S(1)}, u32[]{:S(2)}, u32[]{:S(2)}) collective-permute-start(bf16[512,256]{1,0:T(8,128)(2,1)S(1)} %fusion.6), channel_id=1, source_target_pairs={{0,64},{1,65},{2,66},{3,67},{4,68},{5,69},{6,70},{7,71},{8,72},{9,... | collective-permute-start | bytes 786440 | tf_op jit(solution)/shard_map/ppermute | solution.py:28
  (29 other events, 394.5 us)
Sparse Core Ops, SparseCore 0:
  60.3 55.8 all-gather.2

commit v3 on v2

v3 whole, which is shorter than its diff:
```python
import functools

import jax
import jax.numpy as jnp
import numpy as np
from jax import lax
from jax.experimental import pallas as pl
from jax.experimental.pallas import tpu as pltpu
from jax.sharding import Mesh, PartitionSpec as P

AXES = ("zh", "x", "zl", "y", "c")
SIZES = (2, 4, 2, 4, 2)
D = 2048
ROWS = 128
F = 512
BF = jnp.bfloat16
F32 = jnp.float32
MIB = 1024 * 1024
ANY = pl.BlockSpec(memory_space=pl.ANY)


def send(value, **shift):
    ids = np.arange(128).reshape(SIZES)
    pairs = []
    for at in np.ndindex(*SIZES):
        to = tuple((a + shift.get(n, 0)) % s for a, n, s in zip(at, AXES, SIZES))
        pairs.append((int(ids[at]), int(ids[to])))
    return lax.ppermute(value, AXES, pairs)


def nt(a, b):
    return lax.dot_general(a, b, (((1,), (1,)), ((), ())), preferred_element_type=F32)


def nn(a, b):
    return lax.dot_general(a, b, (((1,), (0,)), ((), ())), preferred_element_type=F32)


def struct(*shape, dtype=BF):
    return jax.ShapeDtypeStruct(shape, dtype)


def params():
    return pltpu.CompilerParams(vmem_limit_bytes=60 * MIB)


def cost(mults=0):
    return pl.CostEstimate(flops=2 * mults + 1024, bytes_accessed=1024, transcendentals=0)


def after(value, *others):
    return lax.optimization_barrier((value, *others))[0]


def first_kernel(s_ref, tokens, gain, gate, up, wg, wu, wd, normed_t, pack):
    @pl.when(pl.program_id(0) == 0)
    def _():
        x = tokens[...].astype(F32)
        unit = x * lax.rsqrt(jnp.mean(x * x, axis=-1, keepdims=True) + 1e-05)
        normed_t[...] = (unit * gain[...]).astype(BF).T

    for j in range(2):
        pack[j, :128] = gate[j, 0]
        pack[j, 128:256] = up[j, 0]
        pack[j, 256:512] = wg[j * 256 : j * 256 + 256]
        pack[j, 512:768] = wu[j * 256 : j * 256 + 256]
        for k in range(4):
            at = 768 + k * 64
            pack[j, at : at + 64] = wd[j * 64 : j * 64 + 64, k * F : k * F + F]


def first_call(scalars, tokens, gain, gate4, up4, wg, wu, wd):
    half = pl.BlockSpec((2, 1, ROWS, F), lambda i, s: (i, 1 - s[8], 0, 0))
    rows = pl.BlockSpec((512, F), lambda i, s: (i, 0))
    return pl.pallas_call(
        first_kernel,
        grid_spec=pltpu.PrefetchScalarGridSpec(
            num_scalar_prefetch=1,
            grid=(4,),
            in_specs=[
                pl.BlockSpec((ROWS, D), lambda i, s: (0, 0)),
                pl.BlockSpec((1, D), lambda i, s: (0, 0)),
                half,
                half,
                rows,
                rows,
                pl.BlockSpec((128, D), lambda i, s: (i, 0)),
            ],
            out_specs=[
                pl.BlockSpec((D, ROWS), lambda i, s: (0, 0)),
                pl.BlockSpec((2, 1024, F), lambda i, s: (i, 0, 0)),
            ],
        ),
        out_shape=[struct(D, ROWS), struct(8, 1024, F)],
        compiler_params=params(),
        cost_estimate=cost(),
        name="first",
    )(scalars, tokens, gain, gate4, up4, wg, wu, wd)


def factor_kernel(s_ref, gate, up, for_gate, for_up, act_t):
    g = gate[...].astype(F32)
    u = up[...].astype(F32)
    sigma = 0.5 + 0.5 * jnp.tanh(0.5 * g)
    silu = g * sigma
    for_up[...] = silu.astype(BF)
    for_gate[...] = (u * sigma * (1.0 + g * (1.0 - sigma))).astype(BF)
    act_t[...] = (silu * u).astype(BF).T


def factor_call(scalars, gate, up, other):
    if other:
        specs = [pl.BlockSpec((None, ROWS, F), lambda i, s, k=k: (s[i], k, 0)) for k in range(2)]
    else:
        specs = [pl.BlockSpec((None, None, ROWS, F), lambda i, s: (s[i], s[8], 0, 0))] * 2
    rows = pl.BlockSpec((ROWS, F), lambda i, s: (i, 0))
    return pl.pallas_call(
        factor_kernel,
        grid_spec=pltpu.PrefetchScalarGridSpec(
            num_scalar_prefetch=1,
            grid=(8,),
            in_specs=specs,
            out_specs=[rows, rows, pl.BlockSpec((F, ROWS), lambda i, s: (0, i))],
        ),
        out_shape=[struct(8 * ROWS, F)] * 2 + [struct(F, 8 * ROWS)],
        compiler_params=params(),
        cost_estimate=cost(),
        name="factors_other" if other else "factors_own",
    )(scalars, gate, up)


def delta_body(dy, factors, weights, gd, ud, outs, held, sem):
    wd, wg, wu, pack = weights
    wd_own, wd_oth, wg_own, wg_oth, wu_own, wu_oth = held
    moves = ((wd, wd_own), (pack.at[:, 768:1024], wd_oth), (wg, wg_own))
    moves += ((pack.at[:, 256:512], wg_oth), (wu, wu_own), (pack.at[:, 512:768], wu_oth))
    copies = [pltpu.make_async_copy(a, b, sem.at[k]) for k, (a, b) in enumerate(moves)]
    for copy in copies:
        copy.start()
    rows = jnp.concatenate(dy, axis=0)

    def store(hidden, at):
        for_gate, for_up = factors[2:] if at.start else factors[:2]
        gd[:, at] = (hidden * for_gate[...].astype(F32)).astype(BF)
        ud[:, at] = (hidden * for_up[...].astype(F32)).astype(BF)

    copies[0].wait()
    store(nt(rows, wd_own[...]), slice(0, F))
    copies[1].wait()
    hidden = 0
    for k in range(4):
        block = wd_oth[:, k * 64 : k * 64 + 64, :].reshape(F, F)
        hidden = hidden + nt(rows[:, k * F : k * F + F], block)
    store(hidden, slice(F, 2 * F))
    for copy in copies[2:]:
        copy.wait()
    for n in range(4):
        at, two = slice(n * 512, n * 512 + 512), slice(2 * n, 2 * n + 2)
        out = nt(gd[:, :F], wg_own[at, :])
        out = out + nt(gd[:, F:], wg_oth[two].reshape(F, F))
        out = out + nt(ud[:, :F], wu_own[at, :])
        out = (out + nt(ud[:, F:], wu_oth[two].reshape(F, F))).astype(BF)
        for k, ref in enumerate(outs):
            ref[:, at] = out[k * ROWS : k * ROWS + ROWS]


def delta_kernel_a(*refs):
    dy = [r[...] for r in refs[:4]]
    gd, ud, *outs = refs[-13:-7]
    delta_body(dy, refs[4:8], refs[8:12], gd, ud, outs, refs[-7:-1], refs[-1])


def delta_kernel_b(*refs):
    dy = [r[k] for r in refs[:2] for k in range(2)]
    gd, ud, ym, yp = refs[-11:-7]
    outs = (ym.at[0], ym.at[1], yp.at[0], yp.at[1])
    delta_body(dy, refs[2:6], refs[6:10], gd, ud, outs, refs[-7:-1], refs[-1])


def delta_call(second, dy, factors, weights, behind=()):
    at = 1 if second else 0
    wide = pl.BlockSpec((4 * ROWS, F), lambda i: (at, 0))
    here = pl.BlockSpec((4 * ROWS, 2 * F), lambda i: (0, 0))
    if second:
        count, piece = 2, struct(2, ROWS, D)
        spec = pl.BlockSpec((2, ROWS, D), lambda i: (0, 0, 0))
    else:
        count, piece = 4, struct(ROWS, D)
        spec = pl.BlockSpec((ROWS, D), lambda i: (0, 0))
    return pl.pallas_call(
        delta_kernel_b if second else delta_kernel_a,
        grid=(1,),
        in_specs=[spec] * count + [wide] * 4 + [ANY] * 4 + [ANY] * len(behind),
        out_specs=[here, here] + [spec] * count,
        out_shape=[struct(4 * ROWS, 2 * F)] * 2 + [piece] * count,
        scratch_shapes=[pltpu.VMEM((F, D), BF), pltpu.VMEM((8, 256, F), BF)]
        + [pltpu.VMEM((D, F), BF), pltpu.VMEM((8, 256, F), BF)] * 2
        + [pltpu.SemaphoreType.DMA((6,))],
        compiler_params=params(),
        cost_estimate=cost(),
        name="deltas_b" if second else "deltas_a",
    )(*dy, *factors, *weights, *behind)


def down_kernel(s_ref, act_own, act_oth, *refs):
    out_own, out_oth = refs[-2:]
    for q in range(2):
        dy = refs[6 * q : 6 * q + 6]
        cols = [d[...] for d in dy[:4]] + [d[k] for d in dy[4:] for k in range(2)]
        cols = jnp.concatenate(cols, axis=0)
        out_own[q] = nn(act_own[...], cols).astype(BF)
        out_oth[q] = nn(act_oth[...], cols).astype(BF)


def down_call(scalars, acts, dy, behind):
    specs = [pl.BlockSpec((F, 8 * ROWS), lambda i, s: (0, 0))] * 2
    for q in range(2):
        specs += [pl.BlockSpec((ROWS, 256), lambda i, s, q=q: (0, s[9 + 2 * i + q]))] * 4
        specs += [pl.BlockSpec((2, ROWS, 256), lambda i, s, q=q: (0, 0, s[9 + 2 * i + q]))] * 2
    return pl.pallas_call(
        down_kernel,
        grid_spec=pltpu.PrefetchScalarGridSpec(
            num_scalar_prefetch=1,
            grid=(4,),
            in_specs=specs + [ANY] * len(behind),
            out_specs=[pl.BlockSpec((2, F, 256), lambda i, s: (i, 0, 0))] * 2,
        ),
        out_shape=[struct(8, F, 256)] * 2,
        compiler_params=params(),
        cost_estimate=cost(),
        name="down",
    )(scalars, *acts, *dy, *dy, *behind)


def weight_kernel(s_ref, gda, gdb, uda, udb, *refs):
    out_own, out_oth, out_gain = refs[-3:]
    for q in range(2):
        unit, (wgo, wuo, wgx, wux) = refs[10 * q : 10 * q + 6], refs[10 * q + 6 : 10 * q + 10]
        low = jnp.concatenate([u[...] for u in unit[:4]], axis=1)
        high = jnp.concatenate([u[k] for u in unit[4:] for k in range(2)], axis=1)
        total = jnp.zeros((256, 128), F32)
        for da, db, at, w_own, w_oth in (
            (gda, gdb, 0, wgo[...], wgx[0]),
            (uda, udb, F, wuo[...], wux[0]),
        ):
            for half, w, out in ((0, w_own, out_own), (F, w_oth, out_oth)):
                grad = nn(low, da[:, half : half + F]) + nn(high, db[:, half : half + F])
                out[q, :, at : at + F] = grad.astype(BF)
                prod = grad * w.astype(F32)
                for k in range(4):
                    total = total + prod[:, k * 128 : (k + 1) * 128]
        out_gain[q] = total


def weight_call(places, scalars, deltas, unit, own, pack, behind):
    count = len(places)
    step = places[1] - places[0] if count > 1 else 0

    def row(i, s, q):
        return s[9 + 2 * (places[0] + step * i) + q]

    full = pl.BlockSpec((4 * ROWS, 2 * F), lambda i, s: (0, 0))
    specs, args = [full] * 4, list(deltas)
    for q in range(2):
        at = lambda i, s, q=q: (row(i, s, q), 0)
        specs += [pl.BlockSpec((256, ROWS), at)] * 4
        specs += [pl.BlockSpec((2, 256, ROWS), lambda i, s, q=q: (0, row(i, s, q), 0))] * 2
        specs += [pl.BlockSpec((256, F), at)] * 2
        for k in (1, 2):
            specs.append(pl.BlockSpec((1, 256, F), lambda i, s, q=q, k=k: (row(i, s, q), k, 0)))
        args += [*unit, *own, pack, pack]
    specs += [ANY] * len(behind)
    args += behind
    return pl.pallas_call(
        weight_kernel,
        grid_spec=pltpu.PrefetchScalarGridSpec(
            num_scalar_prefetch=1,
            grid=(count,),
            in_specs=specs,
            out_specs=[pl.BlockSpec((2, 256, 2 * F), lambda i, s: (i, 0, 0))] * 2
            + [pl.BlockSpec((2, 256, 128), lambda i, s: (i, 0, 0))],
        ),
        out_shape=[struct(2 * count, 256, 2 * F)] * 2 + [struct(2 * count, 256, 128, dtype=F32)],
        compiler_params=params(),
        cost_estimate=cost(),
        name="weights_" + "_".join(str(r) for r in places),
    )(scalars, *args)


def last_kernel(tokens, dy, gain, own, a, b, e, f, *refs):
    x = tokens[...].astype(F32)
    inverse = lax.rsqrt(jnp.mean(x * x, axis=-1, keepdims=True) + 1e-05)
    unit = x * inverse
    normed_grad = total_of(own[...], a[0], b[0], e[...], f[...])
    scaled = gain[...] * normed_grad
    mean_term = jnp.mean(scaled * unit, axis=-1, keepdims=True)
    refs[-1][...] = (dy[...].astype(F32) + inverse * (scaled - unit * mean_term)).astype(BF)


def last_call(tokens, dy, gain, own, a, b, e, f, behind):
    rows = pl.BlockSpec((32, D), lambda i: (i, 0))
    first = pl.BlockSpec((1, 32, D), lambda i: (0, i, 0))
    return pl.pallas_call(
        last_kernel,
        grid=(4,),
        in_specs=[rows, rows, pl.BlockSpec((1, D), lambda i: (0, 0)), rows, first, first, rows, rows]
        + [ANY] * len(behind),
        out_specs=rows,
        out_shape=struct(ROWS, D),
        compiler_params=params(),
        cost_estimate=cost(),
        name="last",
    )(tokens, dy, gain, own, a, b, e, f, *behind)


def total_of(*terms):
    out = terms[0].astype(F32)
    for term in terms[1:]:
        out = out + term.astype(F32)
    return out


def sum_call(body, own, back, behind, out_specs, out_shape, name):
    block = pl.BlockSpec((2, *own.shape[1:]), lambda i: (i, 0, 0))
    return pl.pallas_call(
        body,
        grid=(own.shape[0] // 2,),
        in_specs=[block, block] + [ANY] * len(behind),
        out_specs=out_specs,
        out_shape=out_shape,
        compiler_params=params(),
        cost_estimate=cost(),
        name=name,
    )(own, back, *behind)


def pair_sums(own, back, behind=()):
    count, rows, cols = own.shape

    def body(own, back, *refs):
        total = total_of(own[...], back[...]).astype(BF)
        for r, out in enumerate(refs[len(behind) :]):

            @pl.when(pl.program_id(0) == r)
            def _():
                out[...] = total

    specs = [pl.BlockSpec((2, rows, cols), lambda i: (0, 0, 0))] * (count // 2)
    shapes = [struct(2, rows, cols)] * (count // 2)
    return sum_call(body, own, back, behind, specs, shapes, "pair_sums")


def split_sums(own, back, behind=()):
    count, rows, cols = own.shape
    half = rows // 2

    def body(own, back, *refs):
        refs = refs[len(behind) :]
        total = total_of(own[...], back[...]).astype(BF)
        for r, out in enumerate(refs[:-2]):

            @pl.when(pl.program_id(0) == r)
            def _():
                out[...] = total[:, :half]

        for q, out in enumerate(refs[-2:]):
            out[0] = total[q, half:]

    specs = [pl.BlockSpec((2, half, cols), lambda i: (0, 0, 0))] * (count // 2)
    specs += [pl.BlockSpec((1, half, cols), lambda i: (i, 0, 0))] * 2
    shapes = [struct(2, half, cols)] * (count // 2) + [struct(count // 2, half, cols)] * 2
    return sum_call(body, own, back, behind, specs, shapes, "split_sums")


def local(tokens, gain, gate_saved, up_saved, out_grad, gate_weight, up_weight, down_weight):
    zh, x_at, zl, y, c = (lax.axis_index(a) for a in AXES)
    near = [zl * 4 + (y + k) % 4 for k in (0, 2, 3, 1)]
    far = [(1 - zl) * 4 + (y + k) % 4 for k in (0, 2, 3, 1)]
    places = [p for pair in zip(near, far) for p in pair]
    order = [((zh + q) % 2) * 4 + (x_at + r) % 4 for r in range(4) for q in range(2)]
    scalars = jnp.stack(places + [c] + order).astype(jnp.int32)

    d_z = send(out_grad, zl=1)
    d_2 = send(out_grad, y=2)
    gate4 = gate_saved.reshape(8, 2, ROWS, F)
    up4 = up_saved.reshape(8, 2, ROWS, F)
    normed_t, pack = first_call(
        scalars, tokens, gain.reshape(1, D), gate4, up4, gate_weight, up_weight, down_weight
    )
    pack = send(after(pack, d_z, d_2), c=1)
    weights = (down_weight, gate_weight, up_weight, pack)

    d_pair = jnp.stack([out_grad, after(d_z, d_2)])
    d_m = send(d_pair, y=1)
    d_p = send(d_pair, y=-1)
    d_z2 = send(d_2, zl=1)
    *factors, act_own = factor_call(scalars, after(gate4, d_pair), up4, False)
    normed_b = after(normed_t, pack, act_own)
    u_z = send(normed_b, zl=1)
    u_2 = send(normed_b, y=2)
    *others, act_oth = factor_call(scalars, pack, pack, True)
    factors += others
    dy_a, dy_b = (out_grad, d_z, d_2, d_z2), (d_m, d_p)
    gd_a, ud_a, n_own, n_z, n_2, n_z2 = delta_call(False, dy_a, factors, weights)
    u_pair = jnp.stack([normed_t, after(u_z, u_2, gd_a)])
    u_m = send(u_pair, y=1)
    u_p = send(u_pair, y=-1)
    u_z2 = send(after(u_2, gd_a), zl=1)
    down_own, down_oth = down_call(
        scalars, (act_own, act_oth), dy_a + dy_b, (gd_a, u_pair, u_2)
    )
    down_back = send(down_oth, c=1)
    gd_b, ud_b, n_ym, n_yp = delta_call(True, dy_b, factors, weights, (down_oth,))
    parts = pair_sums(down_own, down_back, (gd_b, u_z2))
    down_got = [send(parts[r], x=r) for r in (1, 2, 3)]
    a = send(n_yp, y=1)
    b = send(n_ym, y=-1)
    d = send(n_z2, zl=1)

    w_args = (
        scalars,
        (gd_a, gd_b, ud_a, ud_b),
        (normed_t, u_z, u_2, u_z2, u_m, u_p),
        (gate_weight, up_weight),
        pack,
    )
    own_0, oth_0, gain_0 = weight_call((0,), *w_args, [parts[0], d])
    own_r, oth_r, gain_r = weight_call((1, 2, 3), *w_args, [own_0])
    back_r = send(after(oth_r, a, b, *down_got), c=1)
    f = send(total_of(after(n_z, oth_r), a[1], b[1]).astype(BF), zl=1)
    *up_r, low_same, low_other = split_sums(own_r, back_r)
    up_got = [send(up_r[r - 1], x=r) for r in (1, 2, 3)]
    low_got = send(low_other, zh=1)
    back_0 = send(after(oth_0, low_other), c=1)
    part_0 = total_of(own_0, back_0)
    down_both = total_of(parts[0], *(after(g, low_other) for g in down_got))
    down_last = send(down_both[1].astype(BF), zh=1)
    e = send(total_of(n_2, after(d, low_other)).astype(BF), y=2)
    token_grad = last_call(tokens, out_grad, gain.reshape(1, D), n_own, a, b, e, f, ())

    gain_rows = jnp.concatenate([jnp.sum(g, axis=-1) for g in (gain_0, gain_r)])
    gain_rows = jnp.roll(gain_rows.reshape(4, 2, 256), (x_at, zh), (0, 1))
    gain_rows = gain_rows.transpose(1, 0, 2).reshape(D)
    gain_rows = gain_rows.reshape(16, 128)
    low_sum = total_of(low_same, low_got)
    low_x = [send(low_sum[r - 1].astype(BF), x=r) for r in (1, 2, 3)]
    up_got = [after(g, token_grad) for g in up_got]
    up_sum = total_of(part_0[:, :128], *up_got)
    rest = send(jnp.concatenate([up_sum[1], part_0[1, 128:]]).astype(BF), zh=1).astype(F32)
    gain_rows = after(gain_rows, *up_got)
    for shift in ({"c": 1}, {"y": 1}, {"y": 2}, {"zl": 1}, {"zh": 1}):
        gain_rows = gain_rows + send(gain_rows, **shift)
    gain_rows = after(gain_rows, *low_x)
    gain_rows = total_of(gain_rows, *(send(gain_rows, x=k) for k in (1, 2, 3)))
    gain_rows = gain_rows.reshape(D) / gain
    low_all = total_of(part_0[0, 128:] + rest[128:], *low_x)
    both_sum = jnp.concatenate([up_sum[0] + rest[:128], low_all])
    return (
        token_grad,
        gain_rows,
        both_sum[:, :F].astype(BF),
        both_sum[:, F:].astype(BF),
        (down_both[0] + down_last.astype(F32)).astype(BF),
    )


def solution(mesh):
    mesh = Mesh(mesh.devices.reshape(SIZES), AXES)
    dp, tensor = ("zh", "x"), ("zl", "y", "c")
    placed = (
        P(dp + tensor, None),
        P(),
        P(dp, tensor),
        P(dp, tensor),
        P(dp + tensor, None),
        P(None, tensor),
        P(None, tensor),
        P(tensor, None),
    )
    return jax.shard_map(
        local,
        mesh=mesh,
        in_specs=placed,
        out_specs=(
            P(dp + tensor, None),
            P(),
            P(dp, tensor),
            P(dp, tensor),
            P(tensor, dp),
        ),
        check_vma=False,
    )
```

time: 251 us -> 210 us (0.84)
  waiting for transfers between devices: 97.8 us -> 42.6 us
  Pallas kernels: 73.2 us -> 93.1 us
  starting transfers between devices: 40.2 us -> 53.8 us
  between operations: 14.4 us -> 1 us
  other arithmetic: 19.8 us -> 11.5 us
    ppermute x31 -> x39, waiting for transfers between devices: 97.8 us -> 42.6 us  [send(): return lax.ppermute(value, AXES, pairs)]
    ppermute x31 -> x39, starting transfers between devices: 40.2 us -> 53.8 us  [send(): return lax.ppermute(value, AXES, pairs)]
    pallas_call x0 -> x2, Pallas kernels: none -> 10.7 us  [sum_call(): pl.pallas_call(body, grid=(own.shape[0] // 2,), in_specs=[block, block] +...]
    convert_element_type x4 -> x3, other arithmetic: 11.8 us -> 4.52 us  [the longest x1 2.38 us: local(): f = send(total_of(after(n_z, oth_r), a[1], b[1]).astype(BF), zl=1)]
    pallas_call x1 -> x2, Pallas kernels: 9.28 us -> 14.2 us  [factor_call(): pl.pallas_call(factor_kernel, grid_spec=pltpu.PrefetchScalarGridSpec(num_...]
    pallas_call x1 -> x2, Pallas kernels: 16.1 us -> 20.5 us  [weight_call(): pl.pallas_call(weight_kernel, grid_spec=pltpu.PrefetchScalarGridSpec(num_...]
    unnamed x42 -> x44, local copies, waits for them, and re-layouts: 1.67 us -> 5.51 us
    add x3, other arithmetic: 4.81 us -> 2.17 us  [total_of(): out = out + term.astype(F32)]
  transfers between devices with their start and end apart: 32 -> 39, of which waited for: 16 -> 21; matrix products, arithmetic and copies ran while one was open for 7% -> 6% of each run, Pallas kernels for 26% -> 40%
where the time goes in v3:
time: 210 us; the launch traced here: 209 us
  Pallas kernels  93.1 us (44%)
  starting transfers between devices  53.8 us (26%)
  waiting for transfers between devices  42.6 us (20%)
  other arithmetic  11.5 us (5%)
  local copies, waits for them, and re-layouts  7.13 us (3%)
    ppermute x39, starting transfers between devices, send(): return lax.ppermute(value, AXES, pairs)  53.8 us
    ppermute x39, waiting for transfers between devices, send(): return lax.ppermute(value, AXES, pairs)  42.6 us
    pallas_call x2, Pallas kernels, delta_call(): pl.pallas_call(delta_kernel_b if second else delta_kernel_a, grid=(1,), i...  25.3 us
    pallas_call x2, Pallas kernels, weight_call(): pl.pallas_call(weight_kernel, grid_spec=pltpu.PrefetchScalarGridSpec(num_...  20.5 us
    pallas_call x2, Pallas kernels, factor_call(): pl.pallas_call(factor_kernel, grid_spec=pltpu.PrefetchScalarGridSpec(num_...  14.2 us
    pallas_call x2, Pallas kernels, sum_call(): pl.pallas_call(body, grid=(own.shape[0] // 2,), in_specs=[block, block] +...  10.7 us
    pallas_call x1, Pallas kernels, down_call(): pl.pallas_call(down_kernel, grid_spec=pltpu.PrefetchScalarGridSpec(num_sc...  9.54 us
    pallas_call x1, Pallas kernels, first_call(): pl.pallas_call(first_kernel, grid_spec=pltpu.PrefetchScalarGridSpec(num_s...  8.44 us
  transfers between devices with their start and end apart: 39, of which 21 were waited for; matrix products, arithmetic and copies ran while one was open for 6% of the time, Pallas kernels for 40%

profile of v3, /device:TPU:0, one launch (start us, length us, event | category | flops | bytes accessed | tf_op | source)
XLA Modules:
  0.0 209.2 jit_solution(17755936420907187473)
XLA Ops:
  0.6 3.4 %collective-permute-start.1 = (bf16[128,2048]{1,0:T(8,128)(2,1)}, bf16[128,2048]{1,0:T(8,128)(2,1)}, u32[]{:S(2)}, u32[]{:S(2)}) collective-permute-start(bf16[128,2048]{1,0:T(8,128)(2,1)} %dy.1), channel_id=1, source_target_pairs={{0,4},{1,5},{2,6},{3,7},{4,0},{5,1},{6,2},{7,3},{8,12},{9,13},{10,... | collective-permute-start | bytes 1572872 | tf_op jit(solution)/shard_map/ppermute | solution.py:28
  6.5 8.4 %first.1 = (bf16[2048,128]{1,0:T(8,128)(2,1)}, bf16[8,1024,512]{2,1,0:T(8,128)(2,1)}) custom-call(s32[17]{0:T(128)} %stack.89.s_ref, bf16[128,2048]{1,0:T(8,128)(2,1)} %tokens.3, f32[1,2048]{1,0:T(1,128)} %bitcast.72, bf16[8,2,128,512]{3,2,1,0:T(8,128)(2,1)} %bitcast.67, bf16[8,2,128,512]{3,2,1,0:T(8,128)(2,1)} %bitcast.69, bf16[2048,512]{1,0:T(8,128)(2,1)} %refs_16_.3, ...), custom_call_target="tpu_custom_call" | custom-call | flops 1024 | bytes 1024 | tf_op jit(solution)/shard_map/first/pallas_call | solution.py:75
  21.7 7.1 %factors_own.1 = (bf16[1024,512]{1,0:T(8,128)(2,1)}, bf16[1024,512]{1,0:T(8,128)(2,1)}, bf16[512,1024]{1,0:T(8,128)(2,1)}) custom-call(s32[17]{0:T(128)} %stack.89.s_ref, bf16[8,2,128,512]{3,2,1,0:T(8,128)(2,1)} %bitcast.68, bf16[8,2,128,512]{3,2,1,0:T(8,128)(2,1)} %bitcast.70), custom_call_target="tpu_custom_call" | custom-call | flops 1024 | bytes 1024 | tf_op jit(solution)/shard_map/factors_own/pallas_call | solution.py:117
  34.9 7.1 %factors_other.1 = (bf16[1024,512]{1,0:T(8,128)(2,1)}, bf16[1024,512]{1,0:T(8,128)(2,1)}, bf16[512,1024]{1,0:T(8,128)(2,1)}) custom-call(s32[17]{0:T(128)} %stack.89.s_ref, bf16[8,1024,512]{2,1,0:T(8,128)(2,1)} %collective-permute-done.3.gate.up.refs_11_.refs_9_.refs_8_.refs_18_.refs_19_, ...), custom_call_target="tpu_custom_call" | custom-call | flops 1024 | bytes 1024 | tf_op jit(solution)/shard_map/factors_other/pallas_call | solution.py:117
  44.0 12.6 %deltas_a.1 = (bf16[512,1024]{1,0:T(8,128)(2,1)}, bf16[512,1024]{1,0:T(8,128)(2,1)}, bf16[128,2048]{1,0:T(8,128)(2,1)}, bf16[128,2048]{1,0:T(8,128)(2,1)}, bf16[...) custom-call(bf16[128,2048]{1,0:T(8,128)(2,1)} %dy.1, bf16[128,2048]{1,0:T(8,128)(2,1)} %copy-done.9, ...), custom_call_target="tpu_custom_call" | custom-call | flops 1024 | bytes 1024 | tf_op jit(solution)/shard_map/deltas_a/pallas_call | solution.py:190
  59.9 9.5 %down.1 = (bf16[8,512,256]{2,1,0:T(8,128)(2,1)}, bf16[8,512,256]{2,1,0:T(8,128)(2,1)}) custom-call(s32[17]{0:T(128)} %stack.89.s_ref, bf16[512,1024]{1,0:T(8,128)(2,1)} %get-tuple-element.67.act_own, bf16[512,1024]{1,0:T(8,128)(2,1)} %get-tuple-element.68.act_oth, bf16[128,2048]{1,0:T(8,128)(2,1)} %dy.1, bf16[128,2048]{1,0:T(8,128)(2,1)} %copy-done.9, ...), custom_call_target="tpu_custom_call" | custom-call | flops 1024 | bytes 1024 | tf_op jit(solution)/shard_map/down/pallas_call | solution.py:220
  73.7 12.7 %deltas_b.1 = (bf16[512,1024]{1,0:T(8,128)(2,1)}, bf16[512,1024]{1,0:T(8,128)(2,1)}, bf16[2,128,2048]{2,1,0:T(8,128)(2,1)}, bf16[2,128,2048]{2,1,0:T(8,128)(2,1)}) custom-call(bf16[2,128,2048]{2,1,0:T(8,128)(2,1)} %copy-done.8, bf16[2,128,2048]{2,1,0:T(8,128)(2,1)} %copy-done.7, bf16[1024,512]{1,0:T(8,128)(2,1)} %get-tuple-element.60.refs_4_.refs_2_, ...), custom_call_target="tpu_custom_call" | custom-call | flops 1024 | bytes 1024 | tf_op jit(solution)/shard_map/deltas_b/pallas_call | solution.py:190
  86.5 3.2 %collective-permute-start.9 = (bf16[2,128,2048]{2,1,0:T(8,128)(2,1)}, bf16[2,128,2048]{2,1,0:T(8,128)(2,1)}, u32[]{:S(2)}, u32[]{:S(2)}) collective-permute-start(bf16[2,128,2048]{2,1,0:T(8,128)(2,1)} %get-tuple-element.75), channel_id=1, source_target_pairs={{0,6},{1,7},{2,0},{3,1},{4,2},{5,3},{6,4},{7,5},{8,14},{9,15},{10,... | collective-permute-start | bytes 3145736 | tf_op jit(solution)/shard_map/ppermute | solution.py:28
  89.7 4.8 %pair_sums.1 = (bf16[2,512,256]{2,1,0:T(8,128)(2,1)}, bf16[2,512,256]{2,1,0:T(8,128)(2,1)}, bf16[2,512,256]{2,1,0:T(8,128)(2,1)}, bf16[2,512,256]{2,1,0:T(8,128)(2,1)}) custom-call(bf16[8,512,256]{2,1,0:T(8,128)(2,1)} %get-tuple-element.82.own, bf16[8,512,256]{2,1,0:T(8,128)(2,1)} %collective-permute-done.14.back, ...), custom_call_target="tpu_custom_call" | custom-call | flops 1024 | bytes 1024 | tf_op jit(solution)/shard_map/pair_sums/pallas_call | solution.py:325
  97.8 3.0 %collective-permute-start.16 = (bf16[2,512,256]{2,1,0:T(8,128)(2,1)}, bf16[2,512,256]{2,1,0:T(8,128)(2,1)}, u32[]{:S(2)}, u32[]{:S(2)}) collective-permute-start(bf16[2,512,256]{2,1,0:T(8,128)(2,1)} %get-tuple-element.88), channel_id=1, source_target_pairs={{0,32},{1,33},{2,34},{3,35},{4,36},{5,37},{6,38},{7,39},{8,40},{9,... | collective-permute-start | bytes 1572872 | tf_op jit(solution)/shard_map/ppermute | solution.py:28
  101.0 2.8 %collective-permute-start.17 = (bf16[2,512,256]{2,1,0:T(8,128)(2,1)}, bf16[2,512,256]{2,1,0:T(8,128)(2,1)}, u32[]{:S(2)}, u32[]{:S(2)}) collective-permute-start(bf16[2,512,256]{2,1,0:T(8,128)(2,1)} %get-tuple-element.89), channel_id=1, source_target_pairs={{0,48},{1,49},{2,50},{3,51},{4,52},{5,53},{6,54},{7,55},{8,56},{9,... | collective-permute-start | bytes 1572872 | tf_op jit(solution)/shard_map/ppermute | solution.py:28
  103.8 7.2 %weights_0.1 = (bf16[2,256,1024]{2,1,0:T(8,128)(2,1)}, bf16[2,256,1024]{2,1,0:T(8,128)(2,1)}, f32[2,256,128]{2,1,0:T(8,128)}) custom-call(s32[17]{0:T(128)} %stack.89.s_ref, bf16[512,1024]{1,0:T(8,128)(2,1)} %get-tuple-element.69.refs_12_.gda, bf16[512,1024]{1,0:T(8,128)(2,1)} %get-tuple-element.78.refs_0_.gdb, bf16[512,1024]{1,0:T(8,128)(2,1)} %get-tuple-element.79.uda, ...), custom_call_target="tpu_custom_call" | custom-call | flops 1024 | bytes 1024 | tf_op jit(solution)/shard_map/weights_0/pallas_call | solution.py:274
  111.0 13.3 %weights_1_2_3.1 = (bf16[6,256,1024]{2,1,0:T(8,128)(2,1)}, bf16[6,256,1024]{2,1,0:T(8,128)(2,1)}, f32[6,256,128]{2,1,0:T(8,128)}) custom-call(s32[17]{0:T(128)} %stack.89.s_ref, bf16[512,1024]{1,0:T(8,128)(2,1)} %get-tuple-element.69.refs_12_.gda, bf16[512,1024]{1,0:T(8,128)(2,1)} %get-tuple-element.78.refs_0_.gdb, bf16[512,1024]{1,0:T(8,128)(2,1)} %get-tuple-element.79.uda, ...), custom_call_target="tpu_custom_call" | custom-call | flops 1024 | bytes 1024 | tf_op jit(solution)/shard_map/weights_1_2_3/pallas_call | solution.py:274
  127.8 3.4 %collective-permute-done.18.back = bf16[6,256,1024]{2,1,0:T(8,128)(2,1)S(1)} collective-permute-done((bf16[6,256,1024]{2,1,0:T(8,128)(2,1)}, bf16[6,256,1024]{2,1,0:T(8,128)(2,1)S(1)}, u32[]{:S(2)}, u32[]{:S(2)}) %collective-permute-start.18) | collective-permute-done | bytes 3145760 | tf_op jit(solution)/shard_map/ppermute | solution.py:28
  132.9 5.9 %split_sums.1 = (bf16[2,128,1024]{2,1,0:T(8,128)(2,1)}, bf16[2,128,1024]{2,1,0:T(8,128)(2,1)}, bf16[2,128,1024]{2,1,0:T(8,128)(2,1)}, bf16[3,128,1024]{2,1,0:T(8,128)(2,1)}, bf16[3,128,1024]{2,1,0:T(8,128)(2,1)}) custom-call(bf16[6,256,1024]{2,1,0:T(8,128)(2,1)} %get-tuple-element.85.own, bf16[6,256,1024]{2,1,0:T(8,128)(2,1)} %copy-done.11), custom_call_target="tpu_custom_call" | custom-call | flops 1024 | bytes 1024 | tf_op jit(solution)/shard_map/split_sums/pallas_call | solution.py:325
  142.1 2.7 %collective-permute-start.22 = (bf16[2,128,1024]{2,1,0:T(8,128)(2,1)}, bf16[2,128,1024]{2,1,0:T(8,128)(2,1)S(1)}, u32[]{:S(2)}, u32[]{:S(2)}) collective-permute-start(bf16[2,128,1024]{2,1,0:T(8,128)(2,1)} %get-tuple-element.99), channel_id=1, source_target_pairs={{0,32},{1,33},{2,34},{3,35},{4,36},{5,37},{6,38},{7,39},{8,40},{9,... | collective-permute-start | bytes 1572872 | tf_op jit(solution)/shard_map/ppermute | solution.py:28
  145.8 3.7 %collective-permute-start.29 = (bf16[3,128,1024]{2,1,0:T(8,128)(2,1)}, bf16[3,128,1024]{2,1,0:T(8,128)(2,1)S(1)}, u32[]{:S(2)}, u32[]{:S(2)}) collective-permute-start(bf16[3,128,1024]{2,1,0:T(8,128)(2,1)} %get-tuple-element.91), channel_id=1, source_target_pairs={{0,64},{1,65},{2,66},{3,67},{4,68},{5,69},{6,70},{7,71},{8,72},{9,... | collective-permute-start | bytes 2359304 | tf_op jit(solution)/shard_map/ppermute | solution.py:28
  149.6 6.9 %collective-permute-done.19.e = bf16[128,2048]{1,0:T(8,128)(2,1)S(1)} collective-permute-done((bf16[128,2048]{1,0:T(8,128)(2,1)}, bf16[128,2048]{1,0:T(8,128)(2,1)S(1)}, u32[]{:S(2)}, u32[]{:S(2)}) %collective-permute-start.19) | collective-permute-done | bytes 524320 | tf_op jit(solution)/shard_map/ppermute | solution.py:28
  157.3 4.4 %last.1 = bf16[128,2048]{1,0:T(8,128)(2,1)} custom-call(bf16[128,2048]{1,0:T(8,128)(2,1)} %tokens.3, bf16[128,2048]{1,0:T(8,128)(2,1)} %dy.1, f32[1,2048]{1,0:T(1,128)} %bitcast.73, bf16[128,2048]{1,0:T(8,128)(2,1)} %get-tuple-element.66.own, bf16[2,128,2048]{2,1,0:T(8,128)(2,1)} %copy-done.12, bf16[2,128,2048]{2,1,0:T(8,128)(2,1)} %collective-permute-done.9.b, ...), custom_call_target="tpu_custom_call" | custom-call | flops 1024 | bytes 1024 | tf_op jit(solution)/shard_map/last/pallas_call | solution.py:303
  161.7 6.2 %collective-permute-done.22 = bf16[2,128,1024]{2,1,0:T(8,128)(2,1)S(1)} collective-permute-done((bf16[2,128,1024]{2,1,0:T(8,128)(2,1)}, bf16[2,128,1024]{2,1,0:T(8,128)(2,1)S(1)}, u32[]{:S(2)}, u32[]{:S(2)}) %collective-permute-start.22) | collective-permute-done | bytes 524320 | tf_op jit(solution)/shard_map/ppermute | solution.py:28
  171.3 2.8 %collective-permute-done.25 = f32[16,128]{1,0:T(8,128)S(1)} collective-permute-done((f32[16,128]{1,0:T(8,128)S(1)}, f32[16,128]{1,0:T(8,128)S(1)}, u32[]{:S(2)}, u32[]{:S(2)}) %collective-permute-start.25) | collective-permute-done | bytes 8224 | tf_op jit(solution)/shard_map/ppermute | solution.py:28
  179.9 3.7 %collective-permute-start.38 = (bf16[512,256]{1,0:T(8,128)(2,1)S(1)}, bf16[512,256]{1,0:T(8,128)(2,1)S(1)}, u32[]{:S(2)}, u32[]{:S(2)}) collective-permute-start(bf16[512,256]{1,0:T(8,128)(2,1)S(1)} %fusion.10), channel_id=1, source_target_pairs={{0,64},{1,65},{2,66},{3,67},{4,68},{5,69},{6,70},{7,71},{8,72},{9,... | collective-permute-start | bytes 786440 | tf_op jit(solution)/shard_map/ppermute | solution.py:28
  183.6 3.1 %collective-permute-start.28 = (f32[16,128]{1,0:T(8,128)S(1)}, f32[16,128]{1,0:T(8,128)S(1)}, u32[]{:S(2)}, u32[]{:S(2)}) collective-permute-start(f32[16,128]{1,0:T(8,128)S(1)} %add.254), channel_id=1, source_target_pairs={{0,64},{1,65},{2,66},{3,67},{4,68},{5,69},{6,70},{7,71},{8,72},{9,... | collective-permute-start | bytes 24584 | tf_op jit(solution)/shard_map/ppermute | solution.py:28
  192.6 4.8 %collective-permute-done.32 = bf16[128,1024]{1,0:T(8,128)(2,1)S(1)} collective-permute-done((bf16[128,1024]{1,0:T(8,128)(2,1)S(1)}, bf16[128,1024]{1,0:T(8,128)(2,1)S(1)}, u32[]{:S(2)}, u32[]{:S(2)}) %collective-permute-start.32) | collective-permute-done | bytes 262176 | tf_op jit(solution)/shard_map/ppermute | solution.py:28
  (142 shorter events, 65.3 us)
Async XLA Ops:
  0.6 15.6 %collective-permute-start.1 = (bf16[128,2048]{1,0:T(8,128)(2,1)}, bf16[128,2048]{1,0:T(8,128)(2,1)}, u32[]{:S(2)}, u32[]{:S(2)}) collective-permute-start(bf16[128,2048]{1,0:T(8,128)(2,1)} %dy.1), channel_id=1, source_target_pairs={{0,4},{1,5},{2,6},{3,7},{4,0},{5,1},{6,2},{7,3},{8,12},{9,13},{10,... | collective-permute-start | bytes 1572872 | tf_op jit(solution)/shard_map/ppermute | solution.py:28
  19.7 39.0 %collective-permute-start.5 = (bf16[2,128,2048]{2,1,0:T(8,128)(2,1)}, bf16[2,128,2048]{2,1,0:T(8,128)(2,1)S(1)}, u32[]{:S(2)}, u32[]{:S(2)}) collective-permute-start(bf16[2,128,2048]{2,1,0:T(8,128)(2,1)} %pad_maximum_fusion), channel_id=1, source_target_pairs={{0,6},{1,7},{2,0},{3,1},{4,2},{5,3},{6,4},{7,5},{8,14},{9,15},{10,... | collective-permute-start | bytes 3145736 | tf_op jit(solution)/shard_map/ppermute | solution.py:28
  21.2 37.5 %collective-permute-start.4 = (bf16[2,128,2048]{2,1,0:T(8,128)(2,1)}, bf16[2,128,2048]{2,1,0:T(8,128)(2,1)S(1)}, u32[]{:S(2)}, u32[]{:S(2)}) collective-permute-start(bf16[2,128,2048]{2,1,0:T(8,128)(2,1)} %pad_maximum_fusion), channel_id=1, source_target_pairs={{0,2},{1,3},{2,4},{3,5},{4,6},{5,7},{6,0},{7,1},{8,10},{9,11},{10,... | collective-permute-start | bytes 3145736 | tf_op jit(solution)/shard_map/ppermute | solution.py:28
  31.3 26.1 %collective-permute-start.7 = (bf16[2048,128]{1,0:T(8,128)(2,1)S(1)}, bf16[2048,128]{1,0:T(8,128)(2,1)S(1)}, u32[]{:S(2)}, u32[]{:S(2)}) collective-permute-start(bf16[2048,128]{1,0:T(8,128)(2,1)S(1)} %copy-done.3), channel_id=1, source_target_pairs={{0,4},{1,5},{2,6},{3,7},{4,0},{5,1},{6,2},{7,3},{8,12},{9,13},{10,... | collective-permute-start | bytes 1572872 | tf_op jit(solution)/shard_map/ppermute | solution.py:28
  33.0 24.5 %collective-permute-start.6 = (bf16[2048,128]{1,0:T(8,128)(2,1)S(1)}, bf16[2048,128]{1,0:T(8,128)(2,1)S(1)}, u32[]{:S(2)}, u32[]{:S(2)}) collective-permute-start(bf16[2048,128]{1,0:T(8,128)(2,1)S(1)} %copy-done.3), channel_id=1, source_target_pairs={{0,8},{1,9},{2,10},{3,11},{4,12},{5,13},{6,14},{7,15},{8,0},{9,1},... | collective-permute-start | bytes 1572872 | tf_op jit(solution)/shard_map/ppermute | solution.py:28
  69.5 17.0 %collective-permute-start.14 = (bf16[8,512,256]{2,1,0:T(8,128)(2,1)}, bf16[8,512,256]{2,1,0:T(8,128)(2,1)}, u32[]{:S(2)}, u32[]{:S(2)}) collective-permute-start(bf16[8,512,256]{2,1,0:T(8,128)(2,1)} %get-tuple-element.73.refs_10_), channel_id=1, source_target_pairs={{0,1},{1,0},{2,3},{3,2},{4,5},{5,4},{6,7},{7,6},{8,9},{9,8},{10,11... | collective-permute-start | bytes 6291464 | tf_op jit(solution)/shard_map/ppermute | solution.py:28
  69.6 16.8 %collective-permute-start.11 = (bf16[2048,128]{1,0:T(8,128)(2,1)}, bf16[2048,128]{1,0:T(8,128)(2,1)S(1)}, u32[]{:S(2)}, u32[]{:S(2)}) collective-permute-start(bf16[2048,128]{1,0:T(8,128)(2,1)} %copy-done.2), channel_id=1, source_target_pairs={{0,8},{1,9},{2,10},{3,11},{4,12},{5,13},{6,14},{7,15},{8,0},{9,1},... | collective-permute-start | bytes 1572872 | tf_op jit(solution)/shard_map/ppermute | solution.py:28
  71.6 26.2 %collective-permute-start.13 = (bf16[2,2048,128]{2,1,0:T(8,128)(2,1)}, bf16[2,2048,128]{2,1,0:T(8,128)(2,1)S(1)}, u32[]{:S(2)}, u32[]{:S(2)}) collective-permute-start(bf16[2,2048,128]{2,1,0:T(8,128)(2,1)} %pad_maximum_fusion.1.refs_13_), channel_id=1, source_target_pairs={{0,6},{1,7},{2,0},{3,1},{4,2},{5,3},{6,4},{7,5},{8,14},{9,15},{10,... | collective-permute-start | bytes 3145736 | tf_op jit(solution)/shard_map/ppermute | solution.py:28
  73.6 27.5 %collective-permute-start.12 = (bf16[2,2048,128]{2,1,0:T(8,128)(2,1)}, bf16[2,2048,128]{2,1,0:T(8,128)(2,1)S(1)}, u32[]{:S(2)}, u32[]{:S(2)}) collective-permute-start(bf16[2,2048,128]{2,1,0:T(8,128)(2,1)} %pad_maximum_fusion.1.refs_13_), channel_id=1, source_target_pairs={{0,2},{1,3},{2,4},{3,5},{4,6},{5,7},{6,0},{7,1},{8,10},{9,11},{10,... | collective-permute-start | bytes 3145736 | tf_op jit(solution)/shard_map/ppermute | solution.py:28
  73.6 22.0 %collective-permute-start.10 = (bf16[128,2048]{1,0:T(8,128)(2,1)}, bf16[128,2048]{1,0:T(8,128)(2,1)}, u32[]{:S(2)}, u32[]{:S(2)}) collective-permute-start(bf16[128,2048]{1,0:T(8,128)(2,1)} %get-tuple-element.77), channel_id=1, source_target_pairs={{0,8},{1,9},{2,10},{3,11},{4,12},{5,13},{6,14},{7,15},{8,0},{9,1},... | collective-permute-start | bytes 1572872 | tf_op jit(solution)/shard_map/ppermute | solution.py:28
  86.4 37.9 %collective-permute-start.8 = (bf16[2,128,2048]{2,1,0:T(8,128)(2,1)}, bf16[2,128,2048]{2,1,0:T(8,128)(2,1)S(1)}, u32[]{:S(2)}, u32[]{:S(2)}) collective-permute-start(bf16[2,128,2048]{2,1,0:T(8,128)(2,1)} %get-tuple-element.74), channel_id=1, source_target_pairs={{0,2},{1,3},{2,4},{3,5},{4,6},{5,7},{6,0},{7,1},{8,10},{9,11},{10,... | collective-permute-start | bytes 3145736 | tf_op jit(solution)/shard_map/ppermute | solution.py:28
  86.5 37.8 %collective-permute-start.9 = (bf16[2,128,2048]{2,1,0:T(8,128)(2,1)}, bf16[2,128,2048]{2,1,0:T(8,128)(2,1)}, u32[]{:S(2)}, u32[]{:S(2)}) collective-permute-start(bf16[2,128,2048]{2,1,0:T(8,128)(2,1)} %get-tuple-element.75), channel_id=1, source_target_pairs={{0,6},{1,7},{2,0},{3,1},{4,2},{5,3},{6,4},{7,5},{8,14},{9,15},{10,... | collective-permute-start | bytes 3145736 | tf_op jit(solution)/shard_map/ppermute | solution.py:28
  95.6 28.7 %collective-permute-start.15 = (bf16[2,512,256]{2,1,0:T(8,128)(2,1)}, bf16[2,512,256]{2,1,0:T(8,128)(2,1)S(1)}, u32[]{:S(2)}, u32[]{:S(2)}) collective-permute-start(bf16[2,512,256]{2,1,0:T(8,128)(2,1)} %get-tuple-element.87), channel_id=1, source_target_pairs={{0,16},{1,17},{2,18},{3,19},{4,20},{5,21},{6,22},{7,23},{8,24},{9,... | collective-permute-start | bytes 1572872 | tf_op jit(solution)/shard_map/ppermute | solution.py:28
  97.8 26.6 %collective-permute-start.16 = (bf16[2,512,256]{2,1,0:T(8,128)(2,1)}, bf16[2,512,256]{2,1,0:T(8,128)(2,1)}, u32[]{:S(2)}, u32[]{:S(2)}) collective-permute-start(bf16[2,512,256]{2,1,0:T(8,128)(2,1)} %get-tuple-element.88), channel_id=1, source_target_pairs={{0,32},{1,33},{2,34},{3,35},{4,36},{5,37},{6,38},{7,39},{8,40},{9,... | collective-permute-start | bytes 1572872 | tf_op jit(solution)/shard_map/ppermute | solution.py:28
  101.0 23.4 %collective-permute-start.17 = (bf16[2,512,256]{2,1,0:T(8,128)(2,1)}, bf16[2,512,256]{2,1,0:T(8,128)(2,1)}, u32[]{:S(2)}, u32[]{:S(2)}) collective-permute-start(bf16[2,512,256]{2,1,0:T(8,128)(2,1)} %get-tuple-element.89), channel_id=1, source_target_pairs={{0,48},{1,49},{2,50},{3,51},{4,52},{5,53},{6,54},{7,55},{8,56},{9,... | collective-permute-start | bytes 1572872 | tf_op jit(solution)/shard_map/ppermute | solution.py:28
  127.7 18.1 %collective-permute-start.20 = (bf16[128,2048]{1,0:T(8,128)(2,1)}, bf16[128,2048]{1,0:T(8,128)(2,1)}, u32[]{:S(2)}, u32[]{:S(2)}) collective-permute-start(bf16[128,2048]{1,0:T(8,128)(2,1)} %fusion.2), channel_id=1, source_target_pairs={{0,8},{1,9},{2,10},{3,11},{4,12},{5,13},{6,14},{7,15},{8,0},{9,1},... | collective-permute-start | bytes 1572872 | tf_op jit(solution)/shard_map/ppermute | solution.py:28
  140.8 15.7 %collective-permute-start.19 = (bf16[128,2048]{1,0:T(8,128)(2,1)}, bf16[128,2048]{1,0:T(8,128)(2,1)S(1)}, u32[]{:S(2)}, u32[]{:S(2)}) collective-permute-start(bf16[128,2048]{1,0:T(8,128)(2,1)} %add_convert_fusion.1), channel_id=1, source_target_pairs={{0,4},{1,5},{2,6},{3,7},{4,0},{5,1},{6,2},{7,3},{8,12},{9,13},{10,... | collective-permute-start | bytes 1572872 | tf_op jit(solution)/shard_map/ppermute | solution.py:28
  140.8 20.8 %collective-permute-start.21 = (bf16[2,128,1024]{2,1,0:T(8,128)(2,1)}, bf16[2,128,1024]{2,1,0:T(8,128)(2,1)S(1)}, u32[]{:S(2)}, u32[]{:S(2)}) collective-permute-start(bf16[2,128,1024]{2,1,0:T(8,128)(2,1)} %get-tuple-element.97), channel_id=1, source_target_pairs={{0,16},{1,17},{2,18},{3,19},{4,20},{5,21},{6,22},{7,23},{8,24},{9,... | collective-permute-start | bytes 1572872 | tf_op jit(solution)/shard_map/ppermute | solution.py:28
  142.1 25.8 %collective-permute-start.22 = (bf16[2,128,1024]{2,1,0:T(8,128)(2,1)}, bf16[2,128,1024]{2,1,0:T(8,128)(2,1)S(1)}, u32[]{:S(2)}, u32[]{:S(2)}) collective-permute-start(bf16[2,128,1024]{2,1,0:T(8,128)(2,1)} %get-tuple-element.99), channel_id=1, source_target_pairs={{0,32},{1,33},{2,34},{3,35},{4,36},{5,37},{6,38},{7,39},{8,40},{9,... | collective-permute-start | bytes 1572872 | tf_op jit(solution)/shard_map/ppermute | solution.py:28
  144.8 23.3 %collective-permute-start.23 = (bf16[2,128,1024]{2,1,0:T(8,128)(2,1)}, bf16[2,128,1024]{2,1,0:T(8,128)(2,1)S(1)}, u32[]{:S(2)}, u32[]{:S(2)}) collective-permute-start(bf16[2,128,1024]{2,1,0:T(8,128)(2,1)} %get-tuple-element.101), channel_id=1, source_target_pairs={{0,48},{1,49},{2,50},{3,51},{4,52},{5,53},{6,54},{7,55},{8,56},{9,... | collective-permute-start | bytes 1572872 | tf_op jit(solution)/shard_map/ppermute | solution.py:28
  145.8 40.8 %collective-permute-start.29 = (bf16[3,128,1024]{2,1,0:T(8,128)(2,1)}, bf16[3,128,1024]{2,1,0:T(8,128)(2,1)S(1)}, u32[]{:S(2)}, u32[]{:S(2)}) collective-permute-start(bf16[3,128,1024]{2,1,0:T(8,128)(2,1)} %get-tuple-element.91), channel_id=1, source_target_pairs={{0,64},{1,65},{2,66},{3,67},{4,68},{5,69},{6,70},{7,71},{8,72},{9,... | collective-permute-start | bytes 2359304 | tf_op jit(solution)/shard_map/ppermute | solution.py:28
  171.3 18.9 %collective-permute-start.36 = (bf16[2,256,1024]{2,1,0:T(8,128)(2,1)}, bf16[2,256,1024]{2,1,0:T(8,128)(2,1)S(1)}, u32[]{:S(2)}, u32[]{:S(2)}) collective-permute-start(bf16[2,256,1024]{2,1,0:T(8,128)(2,1)} %get-tuple-element.107), channel_id=1, source_target_pairs={{0,1},{1,0},{2,3},{3,2},{4,5},{5,4},{6,7},{7,6},{8,9},{9,8},{10,11... | collective-permute-start | bytes 3145736 | tf_op jit(solution)/shard_map/ppermute | solution.py:28
  179.9 23.1 %collective-permute-start.38 = (bf16[512,256]{1,0:T(8,128)(2,1)S(1)}, bf16[512,256]{1,0:T(8,128)(2,1)S(1)}, u32[]{:S(2)}, u32[]{:S(2)}) collective-permute-start(bf16[512,256]{1,0:T(8,128)(2,1)S(1)} %fusion.10), channel_id=1, source_target_pairs={{0,64},{1,65},{2,66},{3,67},{4,68},{5,69},{6,70},{7,71},{8,72},{9,... | collective-permute-start | bytes 786440 | tf_op jit(solution)/shard_map/ppermute | solution.py:28
  191.6 16.3 %collective-permute-start.37 = (bf16[256,1024]{1,0:T(8,128)(2,1)S(1)}, bf16[256,1024]{1,0:T(8,128)(2,1)S(1)}, u32[]{:S(2)}, u32[]{:S(2)}) collective-permute-start(bf16[256,1024]{1,0:T(8,128)(2,1)S(1)} %pad_maximum_fusion.2), channel_id=1, source_target_pairs={{0,64},{1,65},{2,66},{3,67},{4,68},{5,69},{6,70},{7,71},{8,72},{9,... | collective-permute-start | bytes 1572872 | tf_op jit(solution)/shard_map/ppermute | solution.py:28
  (37 other events, 292.5 us)

commit v4 on v3

--- a/solution.py
+++ b/solution.py
@@ -41,7 +41,7 @@
 
 
 def params():
-    return pltpu.CompilerParams(vmem_limit_bytes=60 * MIB)
+    return pltpu.CompilerParams(vmem_limit_bytes=38 * MIB)
 
 
 def cost(mults=0):
@@ -370,6 +370,16 @@
     specs += [pl.BlockSpec((1, half, cols), lambda i: (i, 0, 0))] * 2
     shapes = [struct(2, half, cols)] * (count // 2) + [struct(count // 2, half, cols)] * 2
     return sum_call(body, own, back, behind, specs, shapes, "split_sums")
+
+
+def two_parts(rows):
+    high = rows.astype(BF)
+    low = (rows - high.astype(F32)).astype(BF)
+    return jnp.concatenate([high, low, jnp.zeros((12, rows.shape[1]), BF)])
+
+
+def from_parts(rows):
+    return rows[:2].astype(F32) + rows[2:4].astype(F32)
 
 
 def local(tokens, gain, gate_saved, up_saved, out_grad, gate_weight, up_weight, down_weight):
@@ -430,7 +440,13 @@
     f = send(total_of(after(n_z, oth_r), a[1], b[1]).astype(BF), zl=1)
     *up_r, low_same, low_other = split_sums(own_r, back_r)
     up_got = [send(up_r[r - 1], x=r) for r in (1, 2, 3)]
-    low_got = send(low_other, zh=1)
+    gain_rows = jnp.concatenate([jnp.sum(g, axis=-1) for g in (gain_0, gain_r)])
+    gain_rows = jnp.roll(gain_rows.reshape(4, 2, 256), (x_at, zh), (0, 1))
+    gain_rows = gain_rows.transpose(1, 0, 2).reshape(D)
+    gain_rows = gain_rows.reshape(2, 1024)
+    low_got = send(jnp.concatenate([low_other.reshape(384, 1024), two_parts(gain_rows)]), zh=1)
+    gain_rows = gain_rows + from_parts(low_got[384:])
+    low_got = low_got[:384].reshape(3, 128, 1024)
     back_0 = send(after(oth_0, low_other), c=1)
     part_0 = total_of(own_0, back_0)
     down_both = total_of(parts[0], *(after(g, low_other) for g in down_got))
@@ -438,23 +454,23 @@
     e = send(total_of(n_2, after(d, low_other)).astype(BF), y=2)
     token_grad = last_call(tokens, out_grad, gain.reshape(1, D), n_own, a, b, e, f, ())
 
-    gain_rows = jnp.concatenate([jnp.sum(g, axis=-1) for g in (gain_0, gain_r)])
-    gain_rows = jnp.roll(gain_rows.reshape(4, 2, 256), (x_at, zh), (0, 1))
-    gain_rows = gain_rows.transpose(1, 0, 2).reshape(D)
-    gain_rows = gain_rows.reshape(16, 128)
+    up_got = [after(g, token_grad) for g in up_got]
+    gain_rows = after(gain_rows, *up_got)
+    gain_rows = gain_rows + send(gain_rows, c=1)
     low_sum = total_of(low_same, low_got)
-    low_x = [send(low_sum[r - 1].astype(BF), x=r) for r in (1, 2, 3)]
-    up_got = [after(g, token_grad) for g in up_got]
+    low_x = [
+        send(jnp.concatenate([low_sum[r - 1].astype(BF), two_parts(gain_rows)]), x=r)
+        for r in (1, 2, 3)
+    ]
+    gain_rows = gain_rows + total_of(*(from_parts(g[128:]) for g in low_x))
     up_sum = total_of(part_0[:, :128], *up_got)
-    rest = send(jnp.concatenate([up_sum[1], part_0[1, 128:]]).astype(BF), zh=1).astype(F32)
-    gain_rows = after(gain_rows, *up_got)
-    for shift in ({"c": 1}, {"y": 1}, {"y": 2}, {"zl": 1}, {"zh": 1}):
-        gain_rows = gain_rows + send(gain_rows, **shift)
-    gain_rows = after(gain_rows, *low_x)
-    gain_rows = total_of(gain_rows, *(send(gain_rows, x=k) for k in (1, 2, 3)))
+    rest = send(jnp.concatenate([up_sum[1], part_0[1, 128:]]).astype(BF), zh=1)
+    gain_rows = total_of(gain_rows, *(send(gain_rows, y=k) for k in (1, 2, 3)))
+    gain_rows = after(gain_rows, rest)
+    gain_rows = gain_rows + send(gain_rows, zl=1)
     gain_rows = gain_rows.reshape(D) / gain
-    low_all = total_of(part_0[0, 128:] + rest[128:], *low_x)
-    both_sum = jnp.concatenate([up_sum[0] + rest[:128], low_all])
+    low_all = total_of(part_0[0, 128:], rest[128:], *(g[:128] for g in low_x))
+    both_sum = jnp.concatenate([total_of(up_sum[0], rest[:128]), low_all])
     return (
         token_grad,
         gain_rows,

time: 210 us -> 200 us (0.952)
  Pallas kernels: 93.1 us -> 62.8 us
  local copies, waits for them, and re-layouts: 7.13 us -> 24.5 us
  waiting for transfers between devices: 42.6 us -> 57.3 us
  starting transfers between devices: 53.8 us -> 44.7 us
  other arithmetic: 11.5 us -> 8.22 us
    unnamed x44 -> x112, local copies, waits for them, and re-layouts: 5.51 us -> 23.3 us
    ppermute x39 -> x36, waiting for transfers between devices: 42.6 us -> 57.3 us  [send(): return lax.ppermute(value, AXES, pairs)]
    pallas_call x2, Pallas kernels: 14.2 us -> 4.45 us  [factor_call(): pl.pallas_call(factor_kernel, grid_spec=pltpu.PrefetchScalarGridSpec(num_...]
    ppermute x39 -> x36, starting transfers between devices: 53.8 us -> 44.7 us  [send(): return lax.ppermute(value, AXES, pairs)]
    pallas_call x2, Pallas kernels: 20.5 us -> 14.6 us  [weight_call(): pl.pallas_call(weight_kernel, grid_spec=pltpu.PrefetchScalarGridSpec(num_...]
    pallas_call x2, Pallas kernels: 25.3 us -> 20.1 us  [delta_call(): pl.pallas_call(delta_kernel_b if second else delta_kernel_a, grid=(1,), i...]
    pallas_call x2, Pallas kernels: 10.7 us -> 6.83 us  [sum_call(): pl.pallas_call(body, grid=(own.shape[0] // 2,), in_specs=[block, block] +...]
    pallas_call x1, Pallas kernels: 8.44 us -> 4.72 us  [first_call(): pl.pallas_call(first_kernel, grid_spec=pltpu.PrefetchScalarGridSpec(num_s...]
  transfers between devices with their start and end apart: 39 -> 36, of which waited for: 21 -> 15; matrix products, arithmetic and copies ran while one was open for 6% -> 4% of each run, Pallas kernels for 40% -> 27%
where the time goes in v4:
time: 200 us; the launch traced here: 199 us
  Pallas kernels  62.8 us (31%)
  waiting for transfers between devices  57.3 us (29%)
  starting transfers between devices  44.7 us (22%)
  local copies, waits for them, and re-layouts  24.5 us (12%)
  other arithmetic  8.22 us (4%)
    ppermute x36, waiting for transfers between devices, send(): return lax.ppermute(value, AXES, pairs)  57.3 us
    ppermute x36, starting transfers between devices, send(): return lax.ppermute(value, AXES, pairs)  44.7 us
    unnamed x112, local copies, waits for them, and re-layouts  23.3 us
    pallas_call x2, Pallas kernels, delta_call(): pl.pallas_call(delta_kernel_b if second else delta_kernel_a, grid=(1,), i...  20.1 us
    pallas_call x2, Pallas kernels, weight_call(): pl.pallas_call(weight_kernel, grid_spec=pltpu.PrefetchScalarGridSpec(num_...  14.6 us
    pallas_call x1, Pallas kernels, down_call(): pl.pallas_call(down_kernel, grid_spec=pltpu.PrefetchScalarGridSpec(num_sc...  8.49 us
    pallas_call x2, Pallas kernels, sum_call(): pl.pallas_call(body, grid=(own.shape[0] // 2,), in_specs=[block, block] +...  6.83 us
    pallas_call x1, Pallas kernels, first_call(): pl.pallas_call(first_kernel, grid_spec=pltpu.PrefetchScalarGridSpec(num_s...  4.72 us
  transfers between devices with their start and end apart: 36, of which 15 were waited for; matrix products, arithmetic and copies ran while one was open for 4% of the time, Pallas kernels for 27%

profile of v4, /device:TPU:0, one launch (start us, length us, event | category | flops | bytes accessed | tf_op | source)
XLA Modules:
  0.0 198.8 jit_solution(6613962609824548781)
XLA Ops:
  2.7 3.2 %collective-permute-start.1 = (bf16[128,2048]{1,0:T(8,128)(2,1)}, bf16[128,2048]{1,0:T(8,128)(2,1)}, u32[]{:S(2)}, u32[]{:S(2)}) collective-permute-start(bf16[128,2048]{1,0:T(8,128)(2,1)} %dy.1), channel_id=1, source_target_pairs={{0,4},{1,5},{2,6},{3,7},{4,0},{5,1},{6,2},{7,3},{8,12},{9,13},{10,... | collective-permute-start | bytes 1572872 | tf_op jit(solution)/shard_map/ppermute | solution.py:28
  15.7 4.7 %first.1 = (bf16[2048,128]{1,0:T(8,128)(2,1)S(1)}, bf16[8,1024,512]{2,1,0:T(8,128)(2,1)}) custom-call(s32[17]{0:T(128)S(1)} %stack.89.s_ref, bf16[128,2048]{1,0:T(8,128)(2,1)S(1)} %copy-done.38, f32[1,2048]{1,0:T(1,128)S(1)} %bitcast.85, bf16[8,2,128,512]{3,2,1,0:T(8,128)(2,1)S(1)} %bitcast.79, bf16[8,2,128,512]{3,2,1,0:T(8,128)(2,1)S(1)} %bitcast.81, ...), custom_call_target="tpu_custom_call" | custom-call | flops 1024 | bytes 1024 | tf_op jit(solution)/shard_map/first/pallas_call | solution.py:75
  28.3 5.6 %collective-permute-done.3.gate.up.refs_11_.refs_9_.refs_8_.refs_18_.refs_19_ = bf16[8,1024,512]{2,1,0:T(8,128)(2,1)S(1)} collective-permute-done((bf16[8,1024,512]{2,1,0:T(8,128)(2,1)}, bf16[8,1024,512]{2,1,0:T(8,128)(2,1)S(1)}, u32[]{:S(2)}, u32[]{:S(2)}) %collective-permute-start.3) | collective-permute-done | bytes 8388640 | tf_op jit(solution)/shard_map/ppermute | solution.py:28
  38.1 5.0 %collective-permute-done.2.refs_3_.refs_9_ = bf16[128,2048]{1,0:T(8,128)(2,1)S(1)} collective-permute-done((bf16[128,2048]{1,0:T(8,128)(2,1)}, bf16[128,2048]{1,0:T(8,128)(2,1)S(1)}, u32[]{:S(2)}, u32[]{:S(2)}) %collective-permute-start.2) | collective-permute-done | bytes 524320 | tf_op jit(solution)/shard_map/ppermute | solution.py:28
  44.6 10.2 %deltas_a.1 = (bf16[512,1024]{1,0:T(8,128)(2,1)S(1)}, bf16[512,1024]{1,0:T(8,128)(2,1)S(1)}, bf16[128,2048]{1,0:T(8,128)(2,1)S(1)}, bf16[128,2048]{1,0:T(8,128)(...) custom-call(bf16[128,2048]{1,0:T(8,128)(2,1)S(1)} %copy-done.13, bf16[128,2048]{1,0:T(8,128)(2,1)S(1)} %copy-done.18, ...), custom_call_target="tpu_custom_call" | custom-call | flops 1024 | bytes 1024 | tf_op jit(solution)/shard_map/deltas_a/pallas_call | solution.py:190
  54.9 3.2 %collective-permute-done.7.refs_14_.refs_2_.refs_12_ = bf16[2048,128]{1,0:T(8,128)(2,1)S(1)} collective-permute-done((bf16[2048,128]{1,0:T(8,128)(2,1)S(1)}, bf16[2048,128]{1,0:T(8,128)(2,1)S(1)}, u32[]{:S(2)}, u32[]{:S(2)}) %collective-permute-start.7) | collective-permute-done | bytes 524320 | tf_op jit(solution)/shard_map/ppermute | solution.py:28
  59.3 8.5 %down.1 = (bf16[8,512,256]{2,1,0:T(8,128)(2,1)S(1)}, bf16[8,512,256]{2,1,0:T(8,128)(2,1)}) custom-call(s32[17]{0:T(128)S(1)} %stack.89.s_ref, bf16[512,1024]{1,0:T(8,128)(2,1)S(1)} %get-tuple-element.67.act_own, bf16[512,1024]{1,0:T(8,128)(2,1)S(1)} %get-tuple-element.68.act_oth, bf16[128,2048]{1,0:T(8,128)(2,1)S(1)} %copy-done.14, ...), custom_call_target="tpu_custom_call" | custom-call | flops 1024 | bytes 1024 | tf_op jit(solution)/shard_map/down/pallas_call | solution.py:220
  76.8 9.9 %deltas_b.1 = (bf16[512,1024]{1,0:T(8,128)(2,1)S(1)}, bf16[512,1024]{1,0:T(8,128)(2,1)S(1)}, bf16[2,128,2048]{2,1,0:T(8,128)(2,1)S(1)}, bf16[2,128,2048]{2,1,0:T(8,128)(2,1)S(1)}) custom-call(bf16[2,128,2048]{2,1,0:T(8,128)(2,1)} %collective-permute-done.4.refs_4_.refs_10_.refs_0_, bf16[2,128,2048]{2,1,0:T(8,128)(2,1)} %collective-permute-done.5.refs_5_.refs_11_.refs_1_, ...), custom_call_target="tpu_custom_call" | custom-call | flops 1024 | bytes 1024 | tf_op jit(solution)/shard_map/deltas_b/pallas_call | solution.py:190
  87.9 3.0 %collective-permute-start.9 = (bf16[2,128,2048]{2,1,0:T(8,128)(2,1)S(1)}, bf16[2,128,2048]{2,1,0:T(8,128)(2,1)S(1)}, u32[]{:S(2)}, u32[]{:S(2)}) collective-permute-start(bf16[2,128,2048]{2,1,0:T(8,128)(2,1)S(1)} %get-tuple-element.75), channel_id=1, source_target_pairs={{0,6},{1,7},{2,0},{3,1},{4,2},{5,3},{6,4},{7,5},{8,14},{9,15},{10,... | collective-permute-start | bytes 3145736 | tf_op jit(solution)/shard_map/ppermute | solution.py:28
  90.9 3.2 %pair_sums.1 = (bf16[2,512,256]{2,1,0:T(8,128)(2,1)S(1)}, bf16[2,512,256]{2,1,0:T(8,128)(2,1)S(1)}, bf16[2,512,256]{2,1,0:T(8,128)(2,1)S(1)}, bf16[2,512,256]{2,1,0:T(8,128)(2,1)S(1)}) custom-call(bf16[8,512,256]{2,1,0:T(8,128)(2,1)S(1)} %get-tuple-element.82.own, bf16[8,512,256]{2,1,0:T(8,128)(2,1)} %collective-permute-done.14.back, ...), custom_call_target="tpu_custom_call" | custom-call | flops 1024 | bytes 1024 | tf_op jit(solution)/shard_map/pair_sums/pallas_call | solution.py:325
  95.7 2.7 %collective-permute-start.16 = (bf16[2,512,256]{2,1,0:T(8,128)(2,1)S(1)}, bf16[2,512,256]{2,1,0:T(8,128)(2,1)S(1)}, u32[]{:S(2)}, u32[]{:S(2)}) collective-permute-start(bf16[2,512,256]{2,1,0:T(8,128)(2,1)S(1)} %get-tuple-element.88), channel_id=1, source_target_pairs={{0,32},{1,33},{2,34},{3,35},{4,36},{5,37},{6,38},{7,39},{8,40},{9,... | collective-permute-start | bytes 1572872 | tf_op jit(solution)/shard_map/ppermute | solution.py:28
  99.9 4.2 %weights_0.1 = (bf16[2,256,1024]{2,1,0:T(8,128)(2,1)S(1)}, bf16[2,256,1024]{2,1,0:T(8,128)(2,1)S(1)}, f32[2,256,128]{2,1,0:T(8,128)S(1)}) custom-call(s32[17]{0:T(128)S(1)} %stack.89.s_ref, bf16[512,1024]{1,0:T(8,128)(2,1)S(1)} %get-tuple-element.69.refs_12_.gda, bf16[512,1024]{1,0:T(8,128)(2,1)S(1)} %get-tuple-element.78.refs_0_.gdb, ...), custom_call_target="tpu_custom_call" | custom-call | flops 1024 | bytes 1024 | tf_op jit(solution)/shard_map/weights_0/pallas_call | solution.py:274
  105.0 10.4 %weights_1_2_3.1 = (bf16[6,256,1024]{2,1,0:T(8,128)(2,1)}, bf16[6,256,1024]{2,1,0:T(8,128)(2,1)}, f32[6,256,128]{2,1,0:T(8,128)S(1)}) custom-call(s32[17]{0:T(128)S(1)} %stack.89.s_ref, bf16[512,1024]{1,0:T(8,128)(2,1)S(1)} %get-tuple-element.69.refs_12_.gda, bf16[512,1024]{1,0:T(8,128)(2,1)S(1)} %get-tuple-element.78.refs_0_.gdb, ...), custom_call_target="tpu_custom_call" | custom-call | flops 1024 | bytes 1024 | tf_op jit(solution)/shard_map/weights_1_2_3/pallas_call | solution.py:274
  117.2 3.0 %collective-permute-done.16 = bf16[2,512,256]{2,1,0:T(8,128)(2,1)S(1)} collective-permute-done((bf16[2,512,256]{2,1,0:T(8,128)(2,1)S(1)}, bf16[2,512,256]{2,1,0:T(8,128)(2,1)S(1)}, u32[]{:S(2)}, u32[]{:S(2)}) %collective-permute-start.16) | collective-permute-done | bytes 524320 | tf_op jit(solution)/shard_map/ppermute | solution.py:28
  129.7 3.6 %split_sums.1 = (bf16[2,128,1024]{2,1,0:T(8,128)(2,1)S(1)}, bf16[2,128,1024]{2,1,0:T(8,128)(2,1)S(1)}, bf16[2,128,1024]{2,1,0:T(8,128)(2,1)S(1)}, bf16[3,128,102...) custom-call(bf16[6,256,1024]{2,1,0:T(8,128)(2,1)S(1)} %copy-done.35, bf16[6,256,1024]{2,1,0:T(8,128)(2,1)} %collective-permute-done.18.back), custom_call_target="tpu_custom_call" | custom-call | flops 1024 | bytes 1024 | tf_op jit(solution)/shard_map/split_sums/pallas_call | solution.py:325
  133.4 3.6 %collective-permute-start.21 = (bf16[400,1024]{1,0:T(8,128)(2,1)S(1)}, bf16[400,1024]{1,0:T(8,128)(2,1)S(1)}, u32[]{:S(2)}, u32[]{:S(2)}) collective-permute-start(bf16[400,1024]{1,0:T(8,128)(2,1)S(1)} %pad_maximum_fusion.2), channel_id=1, source_target_pairs={{0,64},{1,65},{2,66},{3,67},{4,68},{5,69},{6,70},{7,71},{8,72},{9,... | collective-permute-start | bytes 2457608 | tf_op jit(solution)/shard_map/ppermute | solution.py:28
  143.8 8.7 %collective-permute-done.19.e = bf16[128,2048]{1,0:T(8,128)(2,1)S(1)} collective-permute-done((bf16[128,2048]{1,0:T(8,128)(2,1)S(1)}, bf16[128,2048]{1,0:T(8,128)(2,1)S(1)}, u32[]{:S(2)}, u32[]{:S(2)}) %collective-permute-start.19) | collective-permute-done | bytes 524320 | tf_op jit(solution)/shard_map/ppermute | solution.py:28
  152.5 3.7 %last.1 = bf16[128,2048]{1,0:T(8,128)(2,1)} custom-call(bf16[128,2048]{1,0:T(8,128)(2,1)S(1)} %copy-done.39, bf16[128,2048]{1,0:T(8,128)(2,1)S(1)} %copy-done.14, f32[1,2048]{1,0:T(1,128)S(1)} %bitcast.86, bf16[128,2048]{1,0:T(8,128)(2,1)S(1)} %copy-done.42, bf16[2,128,2048]{2,1,0:T(8,128)(2,1)S(1)} %collective-permute-done.8.a, ...), custom_call_target="tpu_custom_call" | custom-call | flops 1024 | bytes 1024 | tf_op jit(solution)/shard_map/last/pallas_call | solution.py:303
  156.5 8.4 %collective-permute-done.23 = bf16[2,128,1024]{2,1,0:T(8,128)(2,1)S(1)} collective-permute-done((bf16[2,128,1024]{2,1,0:T(8,128)(2,1)S(1)}, bf16[2,128,1024]{2,1,0:T(8,128)(2,1)S(1)}, u32[]{:S(2)}, u32[]{:S(2)}) %collective-permute-start.23) | collective-permute-done | bytes 524320 | tf_op jit(solution)/shard_map/ppermute | solution.py:28
  166.3 2.7 %collective-permute-start.28 = (bf16[144,1024]{1,0:T(8,128)(2,1)S(1)}, bf16[144,1024]{1,0:T(8,128)(2,1)S(1)}, u32[]{:S(2)}, u32[]{:S(2)}) collective-permute-start(bf16[144,1024]{1,0:T(8,128)(2,1)S(1)} %get-tuple-element.125), channel_id=1, source_target_pairs={{0,48},{1,49},{2,50},{3,51},{4,52},{5,53},{6,54},{7,55},{8,56},{9,... | collective-permute-start | bytes 884744 | tf_op jit(solution)/shard_map/ppermute | solution.py:28
  171.5 10.4 %collective-permute-done.28 = bf16[144,1024]{1,0:T(8,128)(2,1)S(1)} collective-permute-done((bf16[144,1024]{1,0:T(8,128)(2,1)S(1)}, bf16[144,1024]{1,0:T(8,128)(2,1)S(1)}, u32[]{:S(2)}, u32[]{:S(2)}) %collective-permute-start.28) | collective-permute-done | bytes 294944 | tf_op jit(solution)/shard_map/ppermute | solution.py:28
  181.9 3.7 %collective-permute-done.26 = bf16[144,1024]{1,0:T(8,128)(2,1)S(1)} collective-permute-done((bf16[144,1024]{1,0:T(8,128)(2,1)S(1)}, bf16[144,1024]{1,0:T(8,128)(2,1)S(1)}, u32[]{:S(2)}, u32[]{:S(2)}) %collective-permute-start.26) | collective-permute-done | bytes 294944 | tf_op jit(solution)/shard_map/ppermute | solution.py:28
  185.6 2.6 %collective-permute-start.31 = (f32[2,1024]{1,0:T(2,128)S(1)}, f32[2,1024]{1,0:T(2,128)S(1)}, u32[]{:S(2)}, u32[]{:S(2)}) collective-permute-start(f32[2,1024]{1,0:T(2,128)S(1)} %add_add_fusion.1), channel_id=1, source_target_pairs={{0,6},{1,7},{2,0},{3,1},{4,2},{5,3},{6,4},{7,5},{8,14},{9,15},{10,... | collective-permute-start | bytes 24584 | tf_op jit(solution)/shard_map/ppermute | solution.py:28
  190.4 3.0 %collective-permute-done.30 = f32[2,1024]{1,0:T(2,128)S(1)} collective-permute-done((f32[2,1024]{1,0:T(2,128)S(1)}, f32[2,1024]{1,0:T(2,128)S(1)}, u32[]{:S(2)}, u32[]{:S(2)}) %collective-permute-start.30) | collective-permute-done | bytes 8224 | tf_op jit(solution)/shard_map/ppermute | solution.py:28
  (206 shorter events, 70.3 us)
Async XLA Ops:
  0.6 19.8 %collective-permute-start = (bf16[128,2048]{1,0:T(8,128)(2,1)}, bf16[128,2048]{1,0:T(8,128)(2,1)S(1)}, u32[]{:S(2)}, u32[]{:S(2)}) collective-permute-start(bf16[128,2048]{1,0:T(8,128)(2,1)} %dy.1), channel_id=1, source_target_pairs={{0,8},{1,9},{2,10},{3,11},{4,12},{5,13},{6,14},{7,15},{8,0},{9,1},... | collective-permute-start | bytes 1572872 | tf_op jit(solution)/shard_map/ppermute | solution.py:28
  2.7 17.7 %collective-permute-start.1 = (bf16[128,2048]{1,0:T(8,128)(2,1)}, bf16[128,2048]{1,0:T(8,128)(2,1)}, u32[]{:S(2)}, u32[]{:S(2)}) collective-permute-start(bf16[128,2048]{1,0:T(8,128)(2,1)} %dy.1), channel_id=1, source_target_pairs={{0,4},{1,5},{2,6},{3,7},{4,0},{5,1},{6,2},{7,3},{8,12},{9,13},{10,... | collective-permute-start | bytes 1572872 | tf_op jit(solution)/shard_map/ppermute | solution.py:28
  20.6 38.5 %collective-permute-start.4 = (bf16[2,128,2048]{2,1,0:T(8,128)(2,1)S(1)}, bf16[2,128,2048]{2,1,0:T(8,128)(2,1)}, u32[]{:S(2)}, u32[]{:S(2)}) collective-permute-start(bf16[2,128,2048]{2,1,0:T(8,128)(2,1)S(1)} %pad_maximum_fusion), channel_id=1, source_target_pairs={{0,2},{1,3},{2,4},{3,5},{4,6},{5,7},{6,0},{7,1},{8,10},{9,11},{10,... | collective-permute-start | bytes 3145736 | tf_op jit(solution)/shard_map/ppermute | solution.py:28
  21.4 37.8 %collective-permute-start.5 = (bf16[2,128,2048]{2,1,0:T(8,128)(2,1)S(1)}, bf16[2,128,2048]{2,1,0:T(8,128)(2,1)}, u32[]{:S(2)}, u32[]{:S(2)}) collective-permute-start(bf16[2,128,2048]{2,1,0:T(8,128)(2,1)S(1)} %pad_maximum_fusion), channel_id=1, source_target_pairs={{0,6},{1,7},{2,0},{3,1},{4,2},{5,3},{6,4},{7,5},{8,14},{9,15},{10,... | collective-permute-start | bytes 3145736 | tf_op jit(solution)/shard_map/ppermute | solution.py:28
  33.9 20.9 %collective-permute-start.6 = (bf16[2048,128]{1,0:T(8,128)(2,1)S(1)}, bf16[2048,128]{1,0:T(8,128)(2,1)S(1)}, u32[]{:S(2)}, u32[]{:S(2)}) collective-permute-start(bf16[2048,128]{1,0:T(8,128)(2,1)S(1)} %get-tuple-element.71.refs_0_.refs_10_), channel_id=1, source_target_pairs={{0,8},{1,9},{2,10},{3,11},{4,12},{5,13},{6,14},{7,15},{8,0},{9,1},... | collective-permute-start | bytes 1572872 | tf_op jit(solution)/shard_map/ppermute | solution.py:28
  34.1 24.0 %collective-permute-start.7 = (bf16[2048,128]{1,0:T(8,128)(2,1)S(1)}, bf16[2048,128]{1,0:T(8,128)(2,1)S(1)}, u32[]{:S(2)}, u32[]{:S(2)}) collective-permute-start(bf16[2048,128]{1,0:T(8,128)(2,1)S(1)} %get-tuple-element.71.refs_0_.refs_10_), channel_id=1, source_target_pairs={{0,4},{1,5},{2,6},{3,7},{4,0},{5,1},{6,2},{7,3},{8,12},{9,13},{10,... | collective-permute-start | bytes 1572872 | tf_op jit(solution)/shard_map/ppermute | solution.py:28
  67.7 20.2 %collective-permute-start.14 = (bf16[8,512,256]{2,1,0:T(8,128)(2,1)}, bf16[8,512,256]{2,1,0:T(8,128)(2,1)}, u32[]{:S(2)}, u32[]{:S(2)}) collective-permute-start(bf16[8,512,256]{2,1,0:T(8,128)(2,1)} %get-tuple-element.73.refs_10_), channel_id=1, source_target_pairs={{0,1},{1,0},{2,3},{3,2},{4,5},{5,4},{6,7},{7,6},{8,9},{9,8},{10,11... | collective-permute-start | bytes 6291464 | tf_op jit(solution)/shard_map/ppermute | solution.py:28
  67.7 19.9 %collective-permute-start.11 = (bf16[2048,128]{1,0:T(8,128)(2,1)S(1)}, bf16[2048,128]{1,0:T(8,128)(2,1)S(1)}, u32[]{:S(2)}, u32[]{:S(2)}) collective-permute-start(bf16[2048,128]{1,0:T(8,128)(2,1)S(1)} %collective-permute-done.7.refs_14_.refs_2_.refs_12_), channel_id=1, source_target_pairs={{0,8},{1,9},{2,10},{3,11},{4,12},{5,13},{6,14},{7,15},{8,0},{9,1},... | collective-permute-start | bytes 1572872 | tf_op jit(solution)/shard_map/ppermute | solution.py:28
  67.9 27.8 %collective-permute-start.12 = (bf16[2,2048,128]{2,1,0:T(8,128)(2,1)}, bf16[2,2048,128]{2,1,0:T(8,128)(2,1)S(1)}, u32[]{:S(2)}, u32[]{:S(2)}) collective-permute-start(bf16[2,2048,128]{2,1,0:T(8,128)(2,1)} %pad_maximum_fusion.1.refs_13_), channel_id=1, source_target_pairs={{0,2},{1,3},{2,4},{3,5},{4,6},{5,7},{6,0},{7,1},{8,10},{9,11},{10,... | collective-permute-start | bytes 3145736 | tf_op jit(solution)/shard_map/ppermute | solution.py:28
  69.4 29.0 %collective-permute-start.13 = (bf16[2,2048,128]{2,1,0:T(8,128)(2,1)}, bf16[2,2048,128]{2,1,0:T(8,128)(2,1)S(1)}, u32[]{:S(2)}, u32[]{:S(2)}) collective-permute-start(bf16[2,2048,128]{2,1,0:T(8,128)(2,1)} %pad_maximum_fusion.1.refs_13_), channel_id=1, source_target_pairs={{0,6},{1,7},{2,0},{3,1},{4,2},{5,3},{6,4},{7,5},{8,14},{9,15},{10,... | collective-permute-start | bytes 3145736 | tf_op jit(solution)/shard_map/ppermute | solution.py:28
  71.2 23.0 %collective-permute-start.10 = (bf16[128,2048]{1,0:T(8,128)(2,1)}, bf16[128,2048]{1,0:T(8,128)(2,1)S(1)}, u32[]{:S(2)}, u32[]{:S(2)}) collective-permute-start(bf16[128,2048]{1,0:T(8,128)(2,1)} %get-tuple-element.77), channel_id=1, source_target_pairs={{0,8},{1,9},{2,10},{3,11},{4,12},{5,13},{6,14},{7,15},{8,0},{9,1},... | collective-permute-start | bytes 1572872 | tf_op jit(solution)/shard_map/ppermute | solution.py:28
  87.7 29.6 %collective-permute-start.8 = (bf16[2,128,2048]{2,1,0:T(8,128)(2,1)S(1)}, bf16[2,128,2048]{2,1,0:T(8,128)(2,1)S(1)}, u32[]{:S(2)}, u32[]{:S(2)}) collective-permute-start(bf16[2,128,2048]{2,1,0:T(8,128)(2,1)S(1)} %get-tuple-element.74), channel_id=1, source_target_pairs={{0,2},{1,3},{2,4},{3,5},{4,6},{5,7},{6,0},{7,1},{8,10},{9,11},{10,... | collective-permute-start | bytes 3145736 | tf_op jit(solution)/shard_map/ppermute | solution.py:28
  87.9 29.3 %collective-permute-start.9 = (bf16[2,128,2048]{2,1,0:T(8,128)(2,1)S(1)}, bf16[2,128,2048]{2,1,0:T(8,128)(2,1)S(1)}, u32[]{:S(2)}, u32[]{:S(2)}) collective-permute-start(bf16[2,128,2048]{2,1,0:T(8,128)(2,1)S(1)} %get-tuple-element.75), channel_id=1, source_target_pairs={{0,6},{1,7},{2,0},{3,1},{4,2},{5,3},{6,4},{7,5},{8,14},{9,15},{10,... | collective-permute-start | bytes 3145736 | tf_op jit(solution)/shard_map/ppermute | solution.py:28
  94.1 23.1 %collective-permute-start.15 = (bf16[2,512,256]{2,1,0:T(8,128)(2,1)S(1)}, bf16[2,512,256]{2,1,0:T(8,128)(2,1)S(1)}, u32[]{:S(2)}, u32[]{:S(2)}) collective-permute-start(bf16[2,512,256]{2,1,0:T(8,128)(2,1)S(1)} %get-tuple-element.87), channel_id=1, source_target_pairs={{0,16},{1,17},{2,18},{3,19},{4,20},{5,21},{6,22},{7,23},{8,24},{9,... | collective-permute-start | bytes 1572872 | tf_op jit(solution)/shard_map/ppermute | solution.py:28
  95.7 24.6 %collective-permute-start.16 = (bf16[2,512,256]{2,1,0:T(8,128)(2,1)S(1)}, bf16[2,512,256]{2,1,0:T(8,128)(2,1)S(1)}, u32[]{:S(2)}, u32[]{:S(2)}) collective-permute-start(bf16[2,512,256]{2,1,0:T(8,128)(2,1)S(1)} %get-tuple-element.88), channel_id=1, source_target_pairs={{0,32},{1,33},{2,34},{3,35},{4,36},{5,37},{6,38},{7,39},{8,40},{9,... | collective-permute-start | bytes 1572872 | tf_op jit(solution)/shard_map/ppermute | solution.py:28
  98.4 22.5 %collective-permute-start.17 = (bf16[2,512,256]{2,1,0:T(8,128)(2,1)S(1)}, bf16[2,512,256]{2,1,0:T(8,128)(2,1)S(1)}, u32[]{:S(2)}, u32[]{:S(2)}) collective-permute-start(bf16[2,512,256]{2,1,0:T(8,128)(2,1)S(1)} %get-tuple-element.89), channel_id=1, source_target_pairs={{0,48},{1,49},{2,50},{3,51},{4,52},{5,53},{6,54},{7,55},{8,56},{9,... | collective-permute-start | bytes 1572872 | tf_op jit(solution)/shard_map/ppermute | solution.py:28
  123.8 18.4 %collective-permute-start.20 = (bf16[128,2048]{1,0:T(8,128)(2,1)}, bf16[128,2048]{1,0:T(8,128)(2,1)}, u32[]{:S(2)}, u32[]{:S(2)}) collective-permute-start(bf16[128,2048]{1,0:T(8,128)(2,1)} %fusion.3), channel_id=1, source_target_pairs={{0,8},{1,9},{2,10},{3,11},{4,12},{5,13},{6,14},{7,15},{8,0},{9,1},... | collective-permute-start | bytes 1572872 | tf_op jit(solution)/shard_map/ppermute | solution.py:28
  133.4 31.5 %collective-permute-start.21 = (bf16[400,1024]{1,0:T(8,128)(2,1)S(1)}, bf16[400,1024]{1,0:T(8,128)(2,1)S(1)}, u32[]{:S(2)}, u32[]{:S(2)}) collective-permute-start(bf16[400,1024]{1,0:T(8,128)(2,1)S(1)} %pad_maximum_fusion.2), channel_id=1, source_target_pairs={{0,64},{1,65},{2,66},{3,67},{4,68},{5,69},{6,70},{7,71},{8,72},{9,... | collective-permute-start | bytes 2457608 | tf_op jit(solution)/shard_map/ppermute | solution.py:28
  138.4 17.8 %collective-permute-start.22 = (bf16[2,128,1024]{2,1,0:T(8,128)(2,1)S(1)}, bf16[2,128,1024]{2,1,0:T(8,128)(2,1)S(1)}, u32[]{:S(2)}, u32[]{:S(2)}) collective-permute-start(bf16[2,128,1024]{2,1,0:T(8,128)(2,1)S(1)} %get-tuple-element.97), channel_id=1, source_target_pairs={{0,16},{1,17},{2,18},{3,19},{4,20},{5,21},{6,22},{7,23},{8,24},{9,... | collective-permute-start | bytes 1572872 | tf_op jit(solution)/shard_map/ppermute | solution.py:28
  139.9 25.0 %collective-permute-start.23 = (bf16[2,128,1024]{2,1,0:T(8,128)(2,1)S(1)}, bf16[2,128,1024]{2,1,0:T(8,128)(2,1)S(1)}, u32[]{:S(2)}, u32[]{:S(2)}) collective-permute-start(bf16[2,128,1024]{2,1,0:T(8,128)(2,1)S(1)} %get-tuple-element.99), channel_id=1, source_target_pairs={{0,32},{1,33},{2,34},{3,35},{4,36},{5,37},{6,38},{7,39},{8,40},{9,... | collective-permute-start | bytes 1572872 | tf_op jit(solution)/shard_map/ppermute | solution.py:28
  142.2 22.6 %collective-permute-start.24 = (bf16[2,128,1024]{2,1,0:T(8,128)(2,1)S(1)}, bf16[2,128,1024]{2,1,0:T(8,128)(2,1)S(1)}, u32[]{:S(2)}, u32[]{:S(2)}) collective-permute-start(bf16[2,128,1024]{2,1,0:T(8,128)(2,1)S(1)} %get-tuple-element.101), channel_id=1, source_target_pairs={{0,48},{1,49},{2,50},{3,51},{4,52},{5,53},{6,54},{7,55},{8,56},{9,... | collective-permute-start | bytes 1572872 | tf_op jit(solution)/shard_map/ppermute | solution.py:28
  152.5 17.8 %collective-permute-start.32 = (bf16[2,256,1024]{2,1,0:T(8,128)(2,1)S(1)}, bf16[2,256,1024]{2,1,0:T(8,128)(2,1)S(1)}, u32[]{:S(2)}, u32[]{:S(2)}) collective-permute-start(bf16[2,256,1024]{2,1,0:T(8,128)(2,1)S(1)} %copy-done.49), channel_id=1, source_target_pairs={{0,1},{1,0},{2,3},{3,2},{4,5},{5,4},{6,7},{7,6},{8,9},{9,8},{10,11... | collective-permute-start | bytes 3145736 | tf_op jit(solution)/shard_map/ppermute | solution.py:28
  156.2 33.4 %collective-permute-start.35 = (bf16[512,256]{1,0:T(8,128)(2,1)S(1)}, bf16[512,256]{1,0:T(8,128)(2,1)S(1)}, u32[]{:S(2)}, u32[]{:S(2)}) collective-permute-start(bf16[512,256]{1,0:T(8,128)(2,1)S(1)} %fusion.13), channel_id=1, source_target_pairs={{0,64},{1,65},{2,66},{3,67},{4,68},{5,69},{6,70},{7,71},{8,72},{9,... | collective-permute-start | bytes 786440 | tf_op jit(solution)/shard_map/ppermute | solution.py:28
  171.1 23.4 %collective-permute-start.33 = (bf16[256,1024]{1,0:T(8,128)(2,1)S(1)}, bf16[256,1024]{1,0:T(8,128)(2,1)S(1)}, u32[]{:S(2)}, u32[]{:S(2)}) collective-permute-start(bf16[256,1024]{1,0:T(8,128)(2,1)S(1)} %pad_maximum_fusion.3), channel_id=1, source_target_pairs={{0,64},{1,65},{2,66},{3,67},{4,68},{5,69},{6,70},{7,71},{8,72},{9,... | collective-permute-start | bytes 1572872 | tf_op jit(solution)/shard_map/ppermute | solution.py:28
  (68 other events, 508.7 us)

commit v5 on v4

--- a/solution.py
+++ b/solution.py
@@ -16,6 +16,8 @@
 BF = jnp.bfloat16
 F32 = jnp.float32
 MIB = 1024 * 1024
+UPPER = 112
+LOWER = 256 - UPPER
 ANY = pl.BlockSpec(memory_space=pl.ANY)
 
 
@@ -352,7 +354,6 @@
 
 def split_sums(own, back, behind=()):
     count, rows, cols = own.shape
-    half = rows // 2
 
     def body(own, back, *refs):
         refs = refs[len(behind) :]
@@ -361,14 +362,14 @@
 
             @pl.when(pl.program_id(0) == r)
             def _():
-                out[...] = total[:, :half]
+                out[...] = total[:, :UPPER]
 
         for q, out in enumerate(refs[-2:]):
-            out[0] = total[q, half:]
-
-    specs = [pl.BlockSpec((2, half, cols), lambda i: (0, 0, 0))] * (count // 2)
-    specs += [pl.BlockSpec((1, half, cols), lambda i: (i, 0, 0))] * 2
-    shapes = [struct(2, half, cols)] * (count // 2) + [struct(count // 2, half, cols)] * 2
+            out[0] = total[q, UPPER:]
+
+    specs = [pl.BlockSpec((2, UPPER, cols), lambda i: (0, 0, 0))] * (count // 2)
+    specs += [pl.BlockSpec((1, LOWER, cols), lambda i: (i, 0, 0))] * 2
+    shapes = [struct(2, UPPER, cols)] * (count // 2) + [struct(count // 2, LOWER, cols)] * 2
     return sum_call(body, own, back, behind, specs, shapes, "split_sums")
 
 
@@ -438,15 +439,18 @@
     own_r, oth_r, gain_r = weight_call((1, 2, 3), *w_args, [own_0])
     back_r = send(after(oth_r, a, b, *down_got), c=1)
     f = send(total_of(after(n_z, oth_r), a[1], b[1]).astype(BF), zl=1)
-    *up_r, low_same, low_other = split_sums(own_r, back_r)
-    up_got = [send(up_r[r - 1], x=r) for r in (1, 2, 3)]
     gain_rows = jnp.concatenate([jnp.sum(g, axis=-1) for g in (gain_0, gain_r)])
     gain_rows = jnp.roll(gain_rows.reshape(4, 2, 256), (x_at, zh), (0, 1))
     gain_rows = gain_rows.transpose(1, 0, 2).reshape(D)
     gain_rows = gain_rows.reshape(2, 1024)
-    low_got = send(jnp.concatenate([low_other.reshape(384, 1024), two_parts(gain_rows)]), zh=1)
-    gain_rows = gain_rows + from_parts(low_got[384:])
-    low_got = low_got[:384].reshape(3, 128, 1024)
+    gain_rows = total_of(
+        gain_rows, send(gain_rows, c=1), send(gain_rows, zl=1), send(gain_rows, zl=1, c=1)
+    )
+    *up_r, low_same, low_other = split_sums(own_r, back_r, (gain_rows,))
+    up_got = [send(up_r[r - 1], x=r) for r in (1, 2, 3)]
+    low_got = send(jnp.concatenate([low_other.reshape(3 * LOWER, 1024), two_parts(gain_rows)]), zh=1)
+    gain_rows = gain_rows + from_parts(low_got[3 * LOWER :])
+    low_got = low_got[: 3 * LOWER].reshape(3, LOWER, 1024)
     back_0 = send(after(oth_0, low_other), c=1)
     part_0 = total_of(own_0, back_0)
     down_both = total_of(parts[0], *(after(g, low_other) for g in down_got))
@@ -455,22 +459,19 @@
     token_grad = last_call(tokens, out_grad, gain.reshape(1, D), n_own, a, b, e, f, ())
 
     up_got = [after(g, token_grad) for g in up_got]
-    gain_rows = after(gain_rows, *up_got)
-    gain_rows = gain_rows + send(gain_rows, c=1)
-    low_sum = total_of(low_same, low_got)
+    low_sum = total_of(low_same, after(low_got, *up_got))
     low_x = [
         send(jnp.concatenate([low_sum[r - 1].astype(BF), two_parts(gain_rows)]), x=r)
         for r in (1, 2, 3)
     ]
-    gain_rows = gain_rows + total_of(*(from_parts(g[128:]) for g in low_x))
-    up_sum = total_of(part_0[:, :128], *up_got)
-    rest = send(jnp.concatenate([up_sum[1], part_0[1, 128:]]).astype(BF), zh=1)
+    gain_rows = gain_rows + total_of(*(from_parts(g[LOWER:]) for g in low_x))
+    up_sum = total_of(part_0[:, :UPPER], *up_got)
+    rest = send(jnp.concatenate([up_sum[1], part_0[1, UPPER:]]).astype(BF), zh=1)
     gain_rows = total_of(gain_rows, *(send(gain_rows, y=k) for k in (1, 2, 3)))
     gain_rows = after(gain_rows, rest)
-    gain_rows = gain_rows + send(gain_rows, zl=1)
     gain_rows = gain_rows.reshape(D) / gain
-    low_all = total_of(part_0[0, 128:], rest[128:], *(g[:128] for g in low_x))
-    both_sum = jnp.concatenate([total_of(up_sum[0], rest[:128]), low_all])
+    low_all = total_of(part_0[0, UPPER:], rest[UPPER:], *(g[:LOWER] for g in low_x))
+    both_sum = jnp.concatenate([total_of(up_sum[0], rest[:UPPER]), low_all])
     return (
         token_grad,
         gain_rows,

time: 200 us -> 195 us (0.975)
  waiting for transfers between devices: 57.3 us -> 54.2 us
    ppermute x36 -> x37, waiting for transfers between devices: 57.3 us -> 54.2 us  [send(): return lax.ppermute(value, AXES, pairs)]
    ppermute x36 -> x37, starting transfers between devices: 44.7 us -> 45.8 us  [send(): return lax.ppermute(value, AXES, pairs)]
  transfers between devices with their start and end apart: 36 -> 37, of which waited for: 15 -> 14; matrix products, arithmetic and copies ran while one was open for 4% -> 3% of each run, Pallas kernels for 27% -> 27%
where the time goes in v5:
time: 195 us; the launch traced here: 194 us
  Pallas kernels  61.2 us (31%)
  waiting for transfers between devices  54.2 us (28%)
  starting transfers between devices  45.8 us (23%)
  local copies, waits for them, and re-layouts  24.5 us (13%)
  other arithmetic  7.4 us (4%)
    ppermute x37, waiting for transfers between devices, send(): return lax.ppermute(value, AXES, pairs)  54.2 us
    ppermute x37, starting transfers between devices, send(): return lax.ppermute(value, AXES, pairs)  45.8 us
    unnamed x112, local copies, waits for them, and re-layouts  23.3 us
    pallas_call x2, Pallas kernels, delta_call(): pl.pallas_call(delta_kernel_b if second else delta_kernel_a, grid=(1,), i...  20.1 us
    pallas_call x2, Pallas kernels, weight_call(): pl.pallas_call(weight_kernel, grid_spec=pltpu.PrefetchScalarGridSpec(num_...  14.6 us
    pallas_call x1, Pallas kernels, down_call(): pl.pallas_call(down_kernel, grid_spec=pltpu.PrefetchScalarGridSpec(num_sc...  8.49 us
    pallas_call x2, Pallas kernels, sum_call(): pl.pallas_call(body, grid=(own.shape[0] // 2,), in_specs=[block, block] +...  6.77 us
    pallas_call x1, Pallas kernels, first_call(): pl.pallas_call(first_kernel, grid_spec=pltpu.PrefetchScalarGridSpec(num_s...  4.72 us
  transfers between devices with their start and end apart: 37, of which 14 were waited for; matrix products, arithmetic and copies ran while one was open for 3% of the time, Pallas kernels for 27%

profile of v5, /device:TPU:0, one launch (start us, length us, event | category | flops | bytes accessed | tf_op | source)
XLA Modules:
  0.0 194.4 jit_solution(9456170724704993744)
XLA Ops:
  2.7 3.2 %collective-permute-start.1 = (bf16[128,2048]{1,0:T(8,128)(2,1)}, bf16[128,2048]{1,0:T(8,128)(2,1)}, u32[]{:S(2)}, u32[]{:S(2)}) collective-permute-start(bf16[128,2048]{1,0:T(8,128)(2,1)} %dy.1), channel_id=1, source_target_pairs={{0,4},{1,5},{2,6},{3,7},{4,0},{5,1},{6,2},{7,3},{8,12},{9,13},{10,... | collective-permute-start | bytes 1572872 | tf_op jit(solution)/shard_map/ppermute | solution.py:30
  15.7 4.7 %first.1 = (bf16[2048,128]{1,0:T(8,128)(2,1)S(1)}, bf16[8,1024,512]{2,1,0:T(8,128)(2,1)}) custom-call(s32[17]{0:T(128)S(1)} %stack.89.s_ref, bf16[128,2048]{1,0:T(8,128)(2,1)S(1)} %copy-done.38, f32[1,2048]{1,0:T(1,128)S(1)} %bitcast.83, bf16[8,2,128,512]{3,2,1,0:T(8,128)(2,1)S(1)} %bitcast.77, bf16[8,2,128,512]{3,2,1,0:T(8,128)(2,1)S(1)} %bitcast.79, ...), custom_call_target="tpu_custom_call" | custom-call | flops 1024 | bytes 1024 | tf_op jit(solution)/shard_map/first/pallas_call | solution.py:77
  21.4 2.6 %collective-permute-start.5 = (bf16[2,128,2048]{2,1,0:T(8,128)(2,1)S(1)}, bf16[2,128,2048]{2,1,0:T(8,128)(2,1)}, u32[]{:S(2)}, u32[]{:S(2)}) collective-permute-start(bf16[2,128,2048]{2,1,0:T(8,128)(2,1)S(1)} %pad_maximum_fusion), channel_id=1, source_target_pairs={{0,6},{1,7},{2,0},{3,1},{4,2},{5,3},{6,4},{7,5},{8,14},{9,15},{10,... | collective-permute-start | bytes 3145736 | tf_op jit(solution)/shard_map/ppermute | solution.py:30
  28.3 5.6 %collective-permute-done.3.gate.up.refs_11_.refs_9_.refs_8_.refs_18_.refs_19_ = bf16[8,1024,512]{2,1,0:T(8,128)(2,1)S(1)} collective-permute-done((bf16[8,1024,512]{2,1,0:T(8,128)(2,1)}, bf16[8,1024,512]{2,1,0:T(8,128)(2,1)S(1)}, u32[]{:S(2)}, u32[]{:S(2)}) %collective-permute-start.3) | collective-permute-done | bytes 8388640 | tf_op jit(solution)/shard_map/ppermute | solution.py:30
  38.1 5.0 %collective-permute-done.2.refs_3_.refs_9_ = bf16[128,2048]{1,0:T(8,128)(2,1)S(1)} collective-permute-done((bf16[128,2048]{1,0:T(8,128)(2,1)}, bf16[128,2048]{1,0:T(8,128)(2,1)S(1)}, u32[]{:S(2)}, u32[]{:S(2)}) %collective-permute-start.2) | collective-permute-done | bytes 524320 | tf_op jit(solution)/shard_map/ppermute | solution.py:30
  44.6 10.2 %deltas_a.1 = (bf16[512,1024]{1,0:T(8,128)(2,1)S(1)}, bf16[512,1024]{1,0:T(8,128)(2,1)S(1)}, bf16[128,2048]{1,0:T(8,128)(2,1)S(1)}, bf16[128,2048]{1,0:T(8,128)(...) custom-call(bf16[128,2048]{1,0:T(8,128)(2,1)S(1)} %copy-done.13, bf16[128,2048]{1,0:T(8,128)(2,1)S(1)} %copy-done.18, ...), custom_call_target="tpu_custom_call" | custom-call | flops 1024 | bytes 1024 | tf_op jit(solution)/shard_map/deltas_a/pallas_call | solution.py:192
  54.9 3.2 %collective-permute-done.7.refs_14_.refs_2_.refs_12_ = bf16[2048,128]{1,0:T(8,128)(2,1)S(1)} collective-permute-done((bf16[2048,128]{1,0:T(8,128)(2,1)S(1)}, bf16[2048,128]{1,0:T(8,128)(2,1)S(1)}, u32[]{:S(2)}, u32[]{:S(2)}) %collective-permute-start.7) | collective-permute-done | bytes 524320 | tf_op jit(solution)/shard_map/ppermute | solution.py:30
  59.3 8.5 %down.1 = (bf16[8,512,256]{2,1,0:T(8,128)(2,1)S(1)}, bf16[8,512,256]{2,1,0:T(8,128)(2,1)}) custom-call(s32[17]{0:T(128)S(1)} %stack.89.s_ref, bf16[512,1024]{1,0:T(8,128)(2,1)S(1)} %get-tuple-element.67.act_own, bf16[512,1024]{1,0:T(8,128)(2,1)S(1)} %get-tuple-element.68.act_oth, bf16[128,2048]{1,0:T(8,128)(2,1)S(1)} %copy-done.14, ...), custom_call_target="tpu_custom_call" | custom-call | flops 1024 | bytes 1024 | tf_op jit(solution)/shard_map/down/pallas_call | solution.py:222
  76.8 9.9 %deltas_b.1 = (bf16[512,1024]{1,0:T(8,128)(2,1)S(1)}, bf16[512,1024]{1,0:T(8,128)(2,1)S(1)}, bf16[2,128,2048]{2,1,0:T(8,128)(2,1)S(1)}, bf16[2,128,2048]{2,1,0:T(8,128)(2,1)S(1)}) custom-call(bf16[2,128,2048]{2,1,0:T(8,128)(2,1)} %collective-permute-done.4.refs_4_.refs_10_.refs_0_, bf16[2,128,2048]{2,1,0:T(8,128)(2,1)} %collective-permute-done.5.refs_5_.refs_11_.refs_1_, ...), custom_call_target="tpu_custom_call" | custom-call | flops 1024 | bytes 1024 | tf_op jit(solution)/shard_map/deltas_b/pallas_call | solution.py:192
  87.9 3.0 %collective-permute-start.9 = (bf16[2,128,2048]{2,1,0:T(8,128)(2,1)S(1)}, bf16[2,128,2048]{2,1,0:T(8,128)(2,1)S(1)}, u32[]{:S(2)}, u32[]{:S(2)}) collective-permute-start(bf16[2,128,2048]{2,1,0:T(8,128)(2,1)S(1)} %get-tuple-element.75), channel_id=1, source_target_pairs={{0,6},{1,7},{2,0},{3,1},{4,2},{5,3},{6,4},{7,5},{8,14},{9,15},{10,... | collective-permute-start | bytes 3145736 | tf_op jit(solution)/shard_map/ppermute | solution.py:30
  90.9 3.2 %pair_sums.1 = (bf16[2,512,256]{2,1,0:T(8,128)(2,1)S(1)}, bf16[2,512,256]{2,1,0:T(8,128)(2,1)S(1)}, bf16[2,512,256]{2,1,0:T(8,128)(2,1)S(1)}, bf16[2,512,256]{2,1,0:T(8,128)(2,1)S(1)}) custom-call(bf16[8,512,256]{2,1,0:T(8,128)(2,1)S(1)} %get-tuple-element.82.own, bf16[8,512,256]{2,1,0:T(8,128)(2,1)} %collective-permute-done.14.back, ...), custom_call_target="tpu_custom_call" | custom-call | flops 1024 | bytes 1024 | tf_op jit(solution)/shard_map/pair_sums/pallas_call | solution.py:327
  95.7 2.7 %collective-permute-start.16 = (bf16[2,512,256]{2,1,0:T(8,128)(2,1)S(1)}, bf16[2,512,256]{2,1,0:T(8,128)(2,1)S(1)}, u32[]{:S(2)}, u32[]{:S(2)}) collective-permute-start(bf16[2,512,256]{2,1,0:T(8,128)(2,1)S(1)} %get-tuple-element.88), channel_id=1, source_target_pairs={{0,32},{1,33},{2,34},{3,35},{4,36},{5,37},{6,38},{7,39},{8,40},{9,... | collective-permute-start | bytes 1572872 | tf_op jit(solution)/shard_map/ppermute | solution.py:30
  99.9 4.2 %weights_0.1 = (bf16[2,256,1024]{2,1,0:T(8,128)(2,1)S(1)}, bf16[2,256,1024]{2,1,0:T(8,128)(2,1)S(1)}, f32[2,256,128]{2,1,0:T(8,128)S(1)}) custom-call(s32[17]{0:T(128)S(1)} %stack.89.s_ref, bf16[512,1024]{1,0:T(8,128)(2,1)S(1)} %get-tuple-element.69.refs_12_.gda, bf16[512,1024]{1,0:T(8,128)(2,1)S(1)} %get-tuple-element.78.refs_0_.gdb, ...), custom_call_target="tpu_custom_call" | custom-call | flops 1024 | bytes 1024 | tf_op jit(solution)/shard_map/weights_0/pallas_call | solution.py:276
  105.0 10.4 %weights_1_2_3.1 = (bf16[6,256,1024]{2,1,0:T(8,128)(2,1)}, bf16[6,256,1024]{2,1,0:T(8,128)(2,1)}, f32[6,256,128]{2,1,0:T(8,128)S(1)}) custom-call(s32[17]{0:T(128)S(1)} %stack.89.s_ref, bf16[512,1024]{1,0:T(8,128)(2,1)S(1)} %get-tuple-element.69.refs_12_.gda, bf16[512,1024]{1,0:T(8,128)(2,1)S(1)} %get-tuple-element.78.refs_0_.gdb, ...), custom_call_target="tpu_custom_call" | custom-call | flops 1024 | bytes 1024 | tf_op jit(solution)/shard_map/weights_1_2_3/pallas_call | solution.py:276
  117.2 3.0 %collective-permute-done.16 = bf16[2,512,256]{2,1,0:T(8,128)(2,1)S(1)} collective-permute-done((bf16[2,512,256]{2,1,0:T(8,128)(2,1)S(1)}, bf16[2,512,256]{2,1,0:T(8,128)(2,1)S(1)}, u32[]{:S(2)}, u32[]{:S(2)}) %collective-permute-start.16) | collective-permute-done | bytes 524320 | tf_op jit(solution)/shard_map/ppermute | solution.py:30
  131.0 3.6 %split_sums.1 = (bf16[2,112,1024]{2,1,0:T(8,128)(2,1)S(1)}, bf16[2,112,1024]{2,1,0:T(8,128)(2,1)S(1)}, bf16[2,112,1024]{2,1,0:T(8,128)(2,1)S(1)}, bf16[3,144,102...) custom-call(bf16[6,256,1024]{2,1,0:T(8,128)(2,1)S(1)} %copy-done.35, bf16[6,256,1024]{2,1,0:T(8,128)(2,1)} %collective-permute-done.18.back, ...), custom_call_target="tpu_custom_call" | custom-call | flops 1024 | bytes 1024 | tf_op jit(solution)/shard_map/split_sums/pallas_call | solution.py:327
  134.7 3.7 %collective-permute-start.24 = (bf16[448,1024]{1,0:T(8,128)(2,1)S(1)}, bf16[448,1024]{1,0:T(8,128)(2,1)S(1)}, u32[]{:S(2)}, u32[]{:S(2)}) collective-permute-start(bf16[448,1024]{1,0:T(8,128)(2,1)S(1)} %pad_maximum_fusion.2), channel_id=1, source_target_pairs={{0,64},{1,65},{2,66},{3,67},{4,68},{5,69},{6,70},{7,71},{8,72},{9,... | collective-permute-start | bytes 2752520 | tf_op jit(solution)/shard_map/ppermute | solution.py:30
  140.8 2.7 %collective-permute-start.26 = (bf16[2,112,1024]{2,1,0:T(8,128)(2,1)S(1)}, bf16[2,112,1024]{2,1,0:T(8,128)(2,1)S(1)}, u32[]{:S(2)}, u32[]{:S(2)}) collective-permute-start(bf16[2,112,1024]{2,1,0:T(8,128)(2,1)S(1)} %get-tuple-element.100), channel_id=1, source_target_pairs={{0,32},{1,33},{2,34},{3,35},{4,36},{5,37},{6,38},{7,39},{8,40},{9,... | collective-permute-start | bytes 1376264 | tf_op jit(solution)/shard_map/ppermute | solution.py:30
  144.8 8.8 %collective-permute-done.22.e = bf16[128,2048]{1,0:T(8,128)(2,1)S(1)} collective-permute-done((bf16[128,2048]{1,0:T(8,128)(2,1)S(1)}, bf16[128,2048]{1,0:T(8,128)(2,1)S(1)}, u32[]{:S(2)}, u32[]{:S(2)}) %collective-permute-start.22) | collective-permute-done | bytes 524320 | tf_op jit(solution)/shard_map/ppermute | solution.py:30
  157.0 6.3 %collective-permute-done.26 = bf16[2,112,1024]{2,1,0:T(8,128)(2,1)S(1)} collective-permute-done((bf16[2,112,1024]{2,1,0:T(8,128)(2,1)S(1)}, bf16[2,112,1024]{2,1,0:T(8,128)(2,1)S(1)}, u32[]{:S(2)}, u32[]{:S(2)}) %collective-permute-start.26) | collective-permute-done | bytes 458784 | tf_op jit(solution)/shard_map/ppermute | solution.py:30
  165.3 2.7 %collective-permute-start.30 = (bf16[160,1024]{1,0:T(8,128)(2,1)S(1)}, bf16[160,1024]{1,0:T(8,128)(2,1)S(1)}, u32[]{:S(2)}, u32[]{:S(2)}) collective-permute-start(bf16[160,1024]{1,0:T(8,128)(2,1)S(1)} %get-tuple-element.124), channel_id=1, source_target_pairs={{0,48},{1,49},{2,50},{3,51},{4,52},{5,53},{6,54},{7,55},{8,56},{9,... | collective-permute-start | bytes 983048 | tf_op jit(solution)/shard_map/ppermute | solution.py:30
  169.9 11.7 %collective-permute-done.30 = bf16[160,1024]{1,0:T(8,128)(2,1)S(1)} collective-permute-done((bf16[160,1024]{1,0:T(8,128)(2,1)S(1)}, bf16[160,1024]{1,0:T(8,128)(2,1)S(1)}, u32[]{:S(2)}, u32[]{:S(2)}) %collective-permute-start.30) | collective-permute-done | bytes 327712 | tf_op jit(solution)/shard_map/ppermute | solution.py:30
  181.6 3.7 %collective-permute-done.28 = bf16[160,1024]{1,0:T(8,128)(2,1)S(1)} collective-permute-done((bf16[160,1024]{1,0:T(8,128)(2,1)S(1)}, bf16[160,1024]{1,0:T(8,128)(2,1)S(1)}, u32[]{:S(2)}, u32[]{:S(2)}) %collective-permute-start.28) | collective-permute-done | bytes 327712 | tf_op jit(solution)/shard_map/ppermute | solution.py:30
  189.2 2.7 %collective-permute-done.32 = f32[2,1024]{1,0:T(2,128)S(1)} collective-permute-done((f32[2,1024]{1,0:T(2,128)S(1)}, f32[2,1024]{1,0:T(2,128)S(1)}, u32[]{:S(2)}, u32[]{:S(2)}) %collective-permute-start.32) | collective-permute-done | bytes 8224 | tf_op jit(solution)/shard_map/ppermute | solution.py:30
  (207 shorter events, 67.8 us)
Async XLA Ops:
  0.6 19.8 %collective-permute-start = (bf16[128,2048]{1,0:T(8,128)(2,1)}, bf16[128,2048]{1,0:T(8,128)(2,1)S(1)}, u32[]{:S(2)}, u32[]{:S(2)}) collective-permute-start(bf16[128,2048]{1,0:T(8,128)(2,1)} %dy.1), channel_id=1, source_target_pairs={{0,8},{1,9},{2,10},{3,11},{4,12},{5,13},{6,14},{7,15},{8,0},{9,1},... | collective-permute-start | bytes 1572872 | tf_op jit(solution)/shard_map/ppermute | solution.py:30
  2.7 17.7 %collective-permute-start.1 = (bf16[128,2048]{1,0:T(8,128)(2,1)}, bf16[128,2048]{1,0:T(8,128)(2,1)}, u32[]{:S(2)}, u32[]{:S(2)}) collective-permute-start(bf16[128,2048]{1,0:T(8,128)(2,1)} %dy.1), channel_id=1, source_target_pairs={{0,4},{1,5},{2,6},{3,7},{4,0},{5,1},{6,2},{7,3},{8,12},{9,13},{10,... | collective-permute-start | bytes 1572872 | tf_op jit(solution)/shard_map/ppermute | solution.py:30
  20.6 38.5 %collective-permute-start.4 = (bf16[2,128,2048]{2,1,0:T(8,128)(2,1)S(1)}, bf16[2,128,2048]{2,1,0:T(8,128)(2,1)}, u32[]{:S(2)}, u32[]{:S(2)}) collective-permute-start(bf16[2,128,2048]{2,1,0:T(8,128)(2,1)S(1)} %pad_maximum_fusion), channel_id=1, source_target_pairs={{0,2},{1,3},{2,4},{3,5},{4,6},{5,7},{6,0},{7,1},{8,10},{9,11},{10,... | collective-permute-start | bytes 3145736 | tf_op jit(solution)/shard_map/ppermute | solution.py:30
  21.4 37.8 %collective-permute-start.5 = (bf16[2,128,2048]{2,1,0:T(8,128)(2,1)S(1)}, bf16[2,128,2048]{2,1,0:T(8,128)(2,1)}, u32[]{:S(2)}, u32[]{:S(2)}) collective-permute-start(bf16[2,128,2048]{2,1,0:T(8,128)(2,1)S(1)} %pad_maximum_fusion), channel_id=1, source_target_pairs={{0,6},{1,7},{2,0},{3,1},{4,2},{5,3},{6,4},{7,5},{8,14},{9,15},{10,... | collective-permute-start | bytes 3145736 | tf_op jit(solution)/shard_map/ppermute | solution.py:30
  33.9 20.9 %collective-permute-start.6 = (bf16[2048,128]{1,0:T(8,128)(2,1)S(1)}, bf16[2048,128]{1,0:T(8,128)(2,1)S(1)}, u32[]{:S(2)}, u32[]{:S(2)}) collective-permute-start(bf16[2048,128]{1,0:T(8,128)(2,1)S(1)} %get-tuple-element.71.refs_0_.refs_10_), channel_id=1, source_target_pairs={{0,8},{1,9},{2,10},{3,11},{4,12},{5,13},{6,14},{7,15},{8,0},{9,1},... | collective-permute-start | bytes 1572872 | tf_op jit(solution)/shard_map/ppermute | solution.py:30
  34.1 24.0 %collective-permute-start.7 = (bf16[2048,128]{1,0:T(8,128)(2,1)S(1)}, bf16[2048,128]{1,0:T(8,128)(2,1)S(1)}, u32[]{:S(2)}, u32[]{:S(2)}) collective-permute-start(bf16[2048,128]{1,0:T(8,128)(2,1)S(1)} %get-tuple-element.71.refs_0_.refs_10_), channel_id=1, source_target_pairs={{0,4},{1,5},{2,6},{3,7},{4,0},{5,1},{6,2},{7,3},{8,12},{9,13},{10,... | collective-permute-start | bytes 1572872 | tf_op jit(solution)/shard_map/ppermute | solution.py:30
  67.7 20.2 %collective-permute-start.14 = (bf16[8,512,256]{2,1,0:T(8,128)(2,1)}, bf16[8,512,256]{2,1,0:T(8,128)(2,1)}, u32[]{:S(2)}, u32[]{:S(2)}) collective-permute-start(bf16[8,512,256]{2,1,0:T(8,128)(2,1)} %get-tuple-element.73.refs_10_), channel_id=1, source_target_pairs={{0,1},{1,0},{2,3},{3,2},{4,5},{5,4},{6,7},{7,6},{8,9},{9,8},{10,11... | collective-permute-start | bytes 6291464 | tf_op jit(solution)/shard_map/ppermute | solution.py:30
  67.7 19.9 %collective-permute-start.11 = (bf16[2048,128]{1,0:T(8,128)(2,1)S(1)}, bf16[2048,128]{1,0:T(8,128)(2,1)S(1)}, u32[]{:S(2)}, u32[]{:S(2)}) collective-permute-start(bf16[2048,128]{1,0:T(8,128)(2,1)S(1)} %collective-permute-done.7.refs_14_.refs_2_.refs_12_), channel_id=1, source_target_pairs={{0,8},{1,9},{2,10},{3,11},{4,12},{5,13},{6,14},{7,15},{8,0},{9,1},... | collective-permute-start | bytes 1572872 | tf_op jit(solution)/shard_map/ppermute | solution.py:30
  67.9 27.8 %collective-permute-start.12 = (bf16[2,2048,128]{2,1,0:T(8,128)(2,1)}, bf16[2,2048,128]{2,1,0:T(8,128)(2,1)S(1)}, u32[]{:S(2)}, u32[]{:S(2)}) collective-permute-start(bf16[2,2048,128]{2,1,0:T(8,128)(2,1)} %pad_maximum_fusion.1.refs_13_), channel_id=1, source_target_pairs={{0,2},{1,3},{2,4},{3,5},{4,6},{5,7},{6,0},{7,1},{8,10},{9,11},{10,... | collective-permute-start | bytes 3145736 | tf_op jit(solution)/shard_map/ppermute | solution.py:30
  69.4 29.0 %collective-permute-start.13 = (bf16[2,2048,128]{2,1,0:T(8,128)(2,1)}, bf16[2,2048,128]{2,1,0:T(8,128)(2,1)S(1)}, u32[]{:S(2)}, u32[]{:S(2)}) collective-permute-start(bf16[2,2048,128]{2,1,0:T(8,128)(2,1)} %pad_maximum_fusion.1.refs_13_), channel_id=1, source_target_pairs={{0,6},{1,7},{2,0},{3,1},{4,2},{5,3},{6,4},{7,5},{8,14},{9,15},{10,... | collective-permute-start | bytes 3145736 | tf_op jit(solution)/shard_map/ppermute | solution.py:30
  71.2 23.0 %collective-permute-start.10 = (bf16[128,2048]{1,0:T(8,128)(2,1)}, bf16[128,2048]{1,0:T(8,128)(2,1)S(1)}, u32[]{:S(2)}, u32[]{:S(2)}) collective-permute-start(bf16[128,2048]{1,0:T(8,128)(2,1)} %get-tuple-element.77), channel_id=1, source_target_pairs={{0,8},{1,9},{2,10},{3,11},{4,12},{5,13},{6,14},{7,15},{8,0},{9,1},... | collective-permute-start | bytes 1572872 | tf_op jit(solution)/shard_map/ppermute | solution.py:30
  87.7 29.6 %collective-permute-start.8 = (bf16[2,128,2048]{2,1,0:T(8,128)(2,1)S(1)}, bf16[2,128,2048]{2,1,0:T(8,128)(2,1)S(1)}, u32[]{:S(2)}, u32[]{:S(2)}) collective-permute-start(bf16[2,128,2048]{2,1,0:T(8,128)(2,1)S(1)} %get-tuple-element.74), channel_id=1, source_target_pairs={{0,2},{1,3},{2,4},{3,5},{4,6},{5,7},{6,0},{7,1},{8,10},{9,11},{10,... | collective-permute-start | bytes 3145736 | tf_op jit(solution)/shard_map/ppermute | solution.py:30
  87.9 29.3 %collective-permute-start.9 = (bf16[2,128,2048]{2,1,0:T(8,128)(2,1)S(1)}, bf16[2,128,2048]{2,1,0:T(8,128)(2,1)S(1)}, u32[]{:S(2)}, u32[]{:S(2)}) collective-permute-start(bf16[2,128,2048]{2,1,0:T(8,128)(2,1)S(1)} %get-tuple-element.75), channel_id=1, source_target_pairs={{0,6},{1,7},{2,0},{3,1},{4,2},{5,3},{6,4},{7,5},{8,14},{9,15},{10,... | collective-permute-start | bytes 3145736 | tf_op jit(solution)/shard_map/ppermute | solution.py:30
  94.1 23.1 %collective-permute-start.15 = (bf16[2,512,256]{2,1,0:T(8,128)(2,1)S(1)}, bf16[2,512,256]{2,1,0:T(8,128)(2,1)S(1)}, u32[]{:S(2)}, u32[]{:S(2)}) collective-permute-start(bf16[2,512,256]{2,1,0:T(8,128)(2,1)S(1)} %get-tuple-element.87), channel_id=1, source_target_pairs={{0,16},{1,17},{2,18},{3,19},{4,20},{5,21},{6,22},{7,23},{8,24},{9,... | collective-permute-start | bytes 1572872 | tf_op jit(solution)/shard_map/ppermute | solution.py:30
  95.7 24.6 %collective-permute-start.16 = (bf16[2,512,256]{2,1,0:T(8,128)(2,1)S(1)}, bf16[2,512,256]{2,1,0:T(8,128)(2,1)S(1)}, u32[]{:S(2)}, u32[]{:S(2)}) collective-permute-start(bf16[2,512,256]{2,1,0:T(8,128)(2,1)S(1)} %get-tuple-element.88), channel_id=1, source_target_pairs={{0,32},{1,33},{2,34},{3,35},{4,36},{5,37},{6,38},{7,39},{8,40},{9,... | collective-permute-start | bytes 1572872 | tf_op jit(solution)/shard_map/ppermute | solution.py:30
  98.4 22.5 %collective-permute-start.17 = (bf16[2,512,256]{2,1,0:T(8,128)(2,1)S(1)}, bf16[2,512,256]{2,1,0:T(8,128)(2,1)S(1)}, u32[]{:S(2)}, u32[]{:S(2)}) collective-permute-start(bf16[2,512,256]{2,1,0:T(8,128)(2,1)S(1)} %get-tuple-element.89), channel_id=1, source_target_pairs={{0,48},{1,49},{2,50},{3,51},{4,52},{5,53},{6,54},{7,55},{8,56},{9,... | collective-permute-start | bytes 1572872 | tf_op jit(solution)/shard_map/ppermute | solution.py:30
  127.1 16.4 %collective-permute-start.23 = (bf16[128,2048]{1,0:T(8,128)(2,1)S(1)}, bf16[128,2048]{1,0:T(8,128)(2,1)S(1)}, u32[]{:S(2)}, u32[]{:S(2)}) collective-permute-start(bf16[128,2048]{1,0:T(8,128)(2,1)S(1)} %fusion), channel_id=1, source_target_pairs={{0,8},{1,9},{2,10},{3,11},{4,12},{5,13},{6,14},{7,15},{8,0},{9,1},... | collective-permute-start | bytes 1572872 | tf_op jit(solution)/shard_map/ppermute | solution.py:30
  134.7 30.0 %collective-permute-start.24 = (bf16[448,1024]{1,0:T(8,128)(2,1)S(1)}, bf16[448,1024]{1,0:T(8,128)(2,1)S(1)}, u32[]{:S(2)}, u32[]{:S(2)}) collective-permute-start(bf16[448,1024]{1,0:T(8,128)(2,1)S(1)} %pad_maximum_fusion.2), channel_id=1, source_target_pairs={{0,64},{1,65},{2,66},{3,67},{4,68},{5,69},{6,70},{7,71},{8,72},{9,... | collective-permute-start | bytes 2752520 | tf_op jit(solution)/shard_map/ppermute | solution.py:30
  139.5 16.4 %collective-permute-start.25 = (bf16[2,112,1024]{2,1,0:T(8,128)(2,1)S(1)}, bf16[2,112,1024]{2,1,0:T(8,128)(2,1)S(1)}, u32[]{:S(2)}, u32[]{:S(2)}) collective-permute-start(bf16[2,112,1024]{2,1,0:T(8,128)(2,1)S(1)} %get-tuple-element.98), channel_id=1, source_target_pairs={{0,16},{1,17},{2,18},{3,19},{4,20},{5,21},{6,22},{7,23},{8,24},{9,... | collective-permute-start | bytes 1376264 | tf_op jit(solution)/shard_map/ppermute | solution.py:30
  140.8 22.4 %collective-permute-start.26 = (bf16[2,112,1024]{2,1,0:T(8,128)(2,1)S(1)}, bf16[2,112,1024]{2,1,0:T(8,128)(2,1)S(1)}, u32[]{:S(2)}, u32[]{:S(2)}) collective-permute-start(bf16[2,112,1024]{2,1,0:T(8,128)(2,1)S(1)} %get-tuple-element.100), channel_id=1, source_target_pairs={{0,32},{1,33},{2,34},{3,35},{4,36},{5,37},{6,38},{7,39},{8,40},{9,... | collective-permute-start | bytes 1376264 | tf_op jit(solution)/shard_map/ppermute | solution.py:30
  143.6 19.7 %collective-permute-start.27 = (bf16[2,112,1024]{2,1,0:T(8,128)(2,1)S(1)}, bf16[2,112,1024]{2,1,0:T(8,128)(2,1)S(1)}, u32[]{:S(2)}, u32[]{:S(2)}) collective-permute-start(bf16[2,112,1024]{2,1,0:T(8,128)(2,1)S(1)} %get-tuple-element.102), channel_id=1, source_target_pairs={{0,48},{1,49},{2,50},{3,51},{4,52},{5,53},{6,54},{7,55},{8,56},{9,... | collective-permute-start | bytes 1376264 | tf_op jit(solution)/shard_map/ppermute | solution.py:30
  155.9 32.5 %collective-permute-start.36 = (bf16[512,256]{1,0:T(8,128)(2,1)S(1)}, bf16[512,256]{1,0:T(8,128)(2,1)S(1)}, u32[]{:S(2)}, u32[]{:S(2)}) collective-permute-start(bf16[512,256]{1,0:T(8,128)(2,1)S(1)} %fusion.11), channel_id=1, source_target_pairs={{0,64},{1,65},{2,66},{3,67},{4,68},{5,69},{6,70},{7,71},{8,72},{9,... | collective-permute-start | bytes 786440 | tf_op jit(solution)/shard_map/ppermute | solution.py:30
  168.8 16.4 %collective-permute-start.28 = (bf16[160,1024]{1,0:T(8,128)(2,1)S(1)}, bf16[160,1024]{1,0:T(8,128)(2,1)S(1)}, u32[]{:S(2)}, u32[]{:S(2)}) collective-permute-start(bf16[160,1024]{1,0:T(8,128)(2,1)S(1)} %get-tuple-element.122), channel_id=1, source_target_pairs={{0,16},{1,17},{2,18},{3,19},{4,20},{5,21},{6,22},{7,23},{8,24},{9,... | collective-permute-start | bytes 983048 | tf_op jit(solution)/shard_map/ppermute | solution.py:30
  169.8 22.8 %collective-permute-start.35 = (bf16[256,1024]{1,0:T(8,128)(2,1)S(1)}, bf16[256,1024]{1,0:T(8,128)(2,1)S(1)}, u32[]{:S(2)}, u32[]{:S(2)}) collective-permute-start(bf16[256,1024]{1,0:T(8,128)(2,1)S(1)} %pad_maximum_fusion.12), channel_id=1, source_target_pairs={{0,64},{1,65},{2,66},{3,67},{4,68},{5,69},{6,70},{7,71},{8,72},{9,... | collective-permute-start | bytes 1572872 | tf_op jit(solution)/shard_map/ppermute | solution.py:30
  (69 other events, 511.3 us)
